TPU v7x, 32 devices: a whole 2x2x4 slice. The times are simulated.
32 devices in a mesh: level: 2 (over core), dp: 16 (over z, y, x).
Axes of the slice: x: 2, y: 2, z: 4, core: 2. Of those that a mesh axis runs over, the one named last changes fastest.
Arguments:
- image: bfloat16 [3, 3, 512, 128], P(None, None, 'dp'), may hold values from -6 to 6
- mask: int32 [3, 512, 128], P(None, 'dp'), may hold values from 0 to 1
- codes: int32 [2, 3, 512, 128], P('level', None, 'dp'), may hold values from 0 to 511
- ema_count: float32 [2, 512], P('level'), may hold values from 0.5 to 3
- ema_sum: float32 [2, 512, 64], P('level'), may hold values from -6 to 6
- encoder_weight: float32 [2, 27, 128], P('level'), may hold values from -1.25 to 1.25
- encoder_first: float32 [2, 27, 128], P('level'), may hold values from -0.013671875 to 0.013671875
- encoder_second: float32 [2, 27, 128], P('level'), may hold values from 8.138021e-07 to 3.2552084e-06
- latent_weight: float32 [2, 128, 64], P('level'), may hold values from -0.5 to 0.5
- latent_first: float32 [2, 128, 64], P('level'), may hold values from -0.01953125 to 0.01953125
- latent_second: float32 [2, 128, 64], P('level'), may hold values from 1.8310546e-06 to 7.3242186e-06
- decoder_weight: float32 [2, 1152, 128], P('level'), may hold values from -0.1875 to 0.1875
- decoder_first: float32 [2, 1152, 128], P('level'), may hold values from -0.009765625 to 0.009765625
- decoder_second: float32 [2, 1152, 128], P('level'), may hold values from 4.5776366e-07 to 1.8310546e-06
- readout_weight: float32 [2, 128, 3], P('level'), may hold values from -0.5 to 0.5
- readout_first: float32 [2, 128, 3], P('level'), may hold values from -0.0625 to 0.0625
- readout_second: float32 [2, 128, 3], P('level'), may hold values from 1.6276043e-05 to 6.612142e-05
Outputs:
- loss_sum: float32 [], replicated
- valid_count: float32 [], replicated
- count_new: float32 [2, 512], P('level')
- sum_new: float32 [2, 512, 64], P('level')
- encoder_moment: float32 [2, 27, 128], P('level')
- encoder_square: float32 [2, 27, 128], P('level')
- encoder_master: float32 [2, 27, 128], P('level')
- encoder_copy: bfloat16 [2, 27, 128], P('level')
- latent_moment: float32 [2, 128, 64], P('level')
- latent_square: float32 [2, 128, 64], P('level')
- latent_master: float32 [2, 128, 64], P('level')
- latent_copy: bfloat16 [2, 128, 64], P('level')
- decoder_moment: float32 [2, 1152, 128], P('level')
- decoder_square: float32 [2, 1152, 128], P('level')
- decoder_master: float32 [2, 1152, 128], P('level')
- decoder_copy: bfloat16 [2, 1152, 128], P('level')
- readout_moment: float32 [2, 128, 3], P('level')
- readout_square: float32 [2, 128, 3], P('level')
- readout_master: float32 [2, 128, 3], P('level')
- readout_copy: bfloat16 [2, 128, 3], P('level')
All inputs are finite; a program needn't handle non-finite values.
Results may differ from a plain program's by a relative error of at most 0.0059.
The roundings to bfloat16 on the way count: a program that leaves them out, or rounds other values in their place, can miss the bound.
Values may be sent and summed in bfloat16 or wider, within the bound.
No kernel may reach another device: no remote copies, remote signals or barrier semaphores. Data moves between devices by JAX's collectives and lax.ppermute only.
A program may use at most 128 MiB of HBM per device.

v0:
```python
import functools
import math

import jax
import jax.numpy as jnp
from jax import lax
from jax.experimental import pallas as pl
from jax.experimental.pallas import tpu as pltpu
from jax.sharding import PartitionSpec as P

CROP = 128
STEP = 5
RATES = (0.05, 0.03, 0.01, 0.03)

F32 = jnp.float32
BF = jnp.bfloat16
W = 128
NOBODY = 300.0

TAPS = 9 * 128
R_ET = TAPS
R_ZN = R_ET + 128
R_ZT = R_ZN + 128
R_OT = R_ZT + 64
R_BT = R_OT + 16
R_CODE = R_BT + 256
BIG = TAPS + 256
S_Z, S_E, S_O, S_X = 0, 64, 96, 112
SMALL = 128
EXACT = 5

NN = (((1,), (0,)), ((), ()))
NT = (((1,), (1,)), ((), ()))
VMEM = pl.BlockSpec(memory_space=pltpu.VMEM)
SMEM = pl.BlockSpec(memory_space=pltpu.SMEM)


def dot(a, b, dims=NN):
    return lax.dot_general(a, b, dims, preferred_element_type=F32)


def part(value, count):
    out = []
    for _ in range(count):
        piece = value.astype(BF)
        out.append(piece)
        value = value - piece.astype(F32)
    return out


def pack_kernel(
    place, image, mask, codes, count, total, enc, lat, dec, read,
    tile, near, across, pack, code_rows, flat,
):
    level = place[0]
    batches, _, band, _ = image.shape
    for b in range(batches):
        base = b * band * 8
        shown = image[b].astype(F32)
        for c in range(3):
            tile[pl.ds(base + c, band, stride=8), :] = shown[c]
        tile[pl.ds(base + 3, band, stride=8), :] = mask[b].astype(F32)
        code = codes[0, b]
        code = jnp.where(code < 256, code, code - 512).astype(F32)
        code_rows[b * band : (b + 1) * band] = code
        tile[pl.ds(base + 4, band, stride=8), :] = code
        for c in range(5, 8):
            tile[pl.ds(base + c, band, stride=8), :] = jnp.zeros((band, W), F32)
    ends = []
    for b in range(batches):
        row = jnp.where(level == 0, band - 2, 0)
        start = pl.multiple_of((b * band + row) * 8, 8)
        near[b * 16 : (b + 1) * 16] = tile[pl.ds(start, 16), :].astype(BF)
        for r in range(2):
            ends.append(
                jnp.where(
                    level == 0,
                    code_rows[b * band + r : b * band + r + 1],
                    code_rows[(b + 1) * band - 2 + r : (b + 1) * band - 1 + r],
                )
            )
    fill = across.shape[0] - len(ends)
    across[...] = jnp.concatenate(ends + [jnp.zeros((fill, W), F32)], 0).astype(BF)

    pack[0:TAPS] = dec[0].astype(BF)
    flat[...] = jnp.zeros_like(flat)
    for t in range(9):
        flat[8 * t : 8 * t + 3] = enc[0, 3 * t : 3 * t + 3]
    pack[R_ET : R_ET + 128] = flat[...].T.astype(BF)
    flat[...] = jnp.zeros_like(flat)
    flat[:, 0:64] = lat[0]
    pack[R_ZN : R_ZN + 128] = flat[...].astype(BF)
    pack[R_ZT : R_ZT + 64] = flat[...].T[0:64].astype(BF)
    flat[...] = jnp.zeros_like(flat)
    flat[:, 0:3] = read[0]
    pack[R_OT : R_OT + 16] = flat[...].T[0:16].astype(BF)
    for quarter in range(4):
        flat[:, 0:64] = total[0, quarter * 128 : (quarter + 1) * 128]
        book = flat[...].T[0:64] / count[0:1, quarter * 128 : (quarter + 1) * 128]
        row = R_BT + (quarter % 2) * 128 + (quarter // 2) * 64
        pack[row : row + 64] = book.astype(BF)
    pack[R_CODE : R_CODE + batches * band] = code_rows[...].astype(BF)


def sides(v):
    lane = lax.broadcasted_iota(jnp.int32, (v.shape[0], W), 1)
    before, after = [], []
    for i in range(v.shape[1] // W):
        row = v[:, i * W : (i + 1) * W]
        before.append(jnp.where(lane == 0, 0.0, pltpu.roll(row, 1, 1)))
        after.append(jnp.where(lane == W - 1, 0.0, pltpu.roll(row, W - 1, 1)))
    if len(before) == 1:
        return before[0], v, after[0]
    return jnp.concatenate(before, 1), v, jnp.concatenate(after, 1)


def at(row, rows):
    return pl.ds(pl.multiple_of(row * W, W), rows * W)


def fold(v, width):
    return sum(v[:, i : i + width] for i in range(0, v.shape[1], width))


def silu_parts(v):
    s = 0.5 * jnp.tanh(0.5 * v) + 0.5
    out = v * s
    return out, s + out * (1.0 - s)


def step_kernel(
    place, tile, near, across, mine, theirs,
    keep_big, keep_small, send,
    t_s, far_s, dn, dt, et, zn, zt, ot, on, bt,
    u_s, p_s, h_s, slope_s, gap_s, da_s, g_d, g_o, g_e, g_z, g_s, l_s,
    *, batches, rows, step_e, step_d, step_b,
):
    level, valid = place[0], place[1]
    band, ext = 2 * rows, rows + 4
    bottom = level == 1

    def pair(start, size):
        a, b = mine[start : start + size], theirs[start : start + size]
        return jnp.where(bottom, a, b), jnp.where(bottom, b, a)

    for t in range(9):
        one, zero = pair(t * 128, 128)
        zero = jnp.concatenate([jnp.zeros((64, 128), BF), zero[0:64]], 0)
        dn[t * 128 : (t + 1) * 128, 0:128] = one
        dn[t * 128 : (t + 1) * 128, 128:256] = zero
        dt[0:128, t * 128 : (t + 1) * 128] = one.astype(F32).T.astype(BF)
        dt[128:256, t * 128 : (t + 1) * 128] = zero.astype(F32).T.astype(BF)
    one, zero = pair(R_ET, 128)
    et[0:128], et[128:256] = one, zero
    one, zero = pair(R_ZN, 128)
    zn[0:128] = one
    zn[128:256] = pltpu.roll(zero.astype(F32), 64, 1).astype(BF)
    one, zero = pair(R_ZT, 64)
    blank = jnp.zeros((64, 128), BF)
    zt[0:64] = jnp.concatenate([one, blank], 1)
    zt[64:128] = jnp.concatenate([blank, zero], 1)
    one, zero = pair(R_OT, 16)
    blank = jnp.zeros((8, 128), F32)
    out_t = jnp.concatenate(
        [
            jnp.concatenate([one[0:8].astype(F32), blank], 1),
            jnp.concatenate([blank, zero[0:8].astype(F32)], 1),
        ],
        0,
    )
    ot[...] = out_t.astype(BF)
    on[...] = out_t.T.astype(BF)
    for half in range(2):
        one, zero = pair(R_BT + half * 128, 128)
        bt[0, :, half * 128 : (half + 1) * 128] = one
        bt[1, :, half * 128 : (half + 1) * 128] = zero

    far_s[0 : batches * band] = theirs[R_CODE : R_CODE + batches * band].astype(F32)
    far_s[batches * band : batches * band + across.shape[0]] = across[...].astype(F32)
    sub = lax.broadcasted_iota(jnp.int32, (8, W), 0)
    own_sub = jnp.where(bottom, 4, 5)

    def lay(b, e, shown, other):
        code = shown[4:5]
        t_s[b, e] = jnp.where(sub < 4, shown, jnp.where(sub == own_sub, code, other))

    def inner(i, _):
        b, e = i // (rows + 2), i % (rows + 2)
        row = b * band + level * (rows - 2) + e
        lay(
            b,
            e + jnp.where(bottom, 0, 2),
            tile[pl.ds(pl.multiple_of(row * 8, 8), 8), :],
            far_s[pl.ds(row, 1), :],
        )
        return 0

    lax.fori_loop(0, batches * (rows + 2), inner, 0, unroll=2)
    for b in range(batches):
        both = near[b * 16 : (b + 1) * 16].astype(F32)
        for r in range(2):
            row = batches * band + b * 2 + r
            shown = jnp.where(valid > 0, both[r * 8 : (r + 1) * 8], jnp.where(sub == 4, NOBODY, 0.0))
            other = jnp.where(valid > 0, far_s[row : row + 1], NOBODY)
            lay(b, jnp.where(bottom, rows + 2 + r, r), shown, other)

    for ref in (g_d, g_o, g_e, g_z, g_s, l_s):
        ref[...] = jnp.zeros_like(ref)

    def patch(i, _):
        b, e = i // rows, i % rows + 2
        views = [view for dr in range(3) for view in sides(t_s[b, e + dr - 1])]
        value = jnp.concatenate(views + [jnp.zeros((56, W), F32)], 0)
        p_s[:, at(i, 1)] = value.astype(BF)
        return 0

    lax.fori_loop(0, batches * rows, patch, 0, unroll=2)

    def lookup(b, e, n):
        here = jnp.concatenate([t_s[b, e + i] for i in range(n)], 1)
        ids = lax.broadcasted_iota(jnp.int32, (256, n * W), 0).astype(F32)
        quants, onehots, highs = [], [], []
        for v in range(2):
            code = here[4 + v : 5 + v]
            high = code < 0.0
            low = jnp.where(high, code + 256.0, code)
            onehot = jnp.where(ids == low, 1.0, 0.0).astype(BF)
            both = dot(bt[v], onehot)
            quants.append(jnp.where(high, both[64:128], both[0:64]))
            onehots.append(onehot)
            highs.append(high)
        u = jnp.concatenate(quants, 0)
        for k, view in enumerate(sides(u)):
            u_s[k, :, at(b * ext + e, n)] = view.astype(BF)
        return here, u, onehots, highs

    def outer(i, _):
        lookup(i // 2, (i % 2) * (rows + 2), 2)
        return 0

    lax.fori_loop(0, batches * 2, outer, 0)

    def encode(i, _):
        n = step_e
        b, e = i // (rows // n), (i % (rows // n)) * n + 2
        here, u, onehots, highs = lookup(b, e, n)
        own = at(i * n, n)
        h, slope = silu_parts(dot(et[...], p_s[:, own]))
        slope_s[:, own] = slope
        h = h.astype(BF)
        h_s[:, own] = h
        z = dot(zt[...], h)
        k = here[3:4]
        gap = z - u
        kept = k * gap
        l_s[0:128] += fold(kept * gap, 256)
        gap_s[:, own] = 0.5 * kept
        z = k * z.astype(BF).astype(F32)
        row = lax.broadcasted_iota(jnp.int32, (16, n * W), 0)
        for v in range(2):
            part_z = z[v * 64 : v * 64 + 64]
            low_k = jnp.where(highs[v], 0.0, k)
            high_k = jnp.where(highs[v], k, 0.0)
            left = jnp.concatenate(
                [
                    jnp.where(highs[v], 0.0, part_z),
                    jnp.where(highs[v], part_z, 0.0),
                    jnp.where(row == 0, low_k, jnp.where(row == 1, high_k, 0.0)),
                ],
                0,
            ).astype(BF)
            g_s[v] += dot(left, onehots[v], NT)
        return 0

    lax.fori_loop(0, batches * (rows // step_e), encode, 0)

    def decode(b, spans, own):
        views = []
        for dr in range(3):
            for dc in range(3):
                runs = [u_s[dc, :, at(b * ext + e + dr - 1, n)] for e, n in spans]
                views.append(runs[0] if len(runs) == 1 else jnp.concatenate(runs, 1))
        u = jnp.concatenate(views, 0)
        g, slope = silu_parts(dot(dt[...], u))
        g = g.astype(BF)
        y = dot(ot[...], g)
        here = jnp.concatenate([t_s[b, e + i] for e, n in spans for i in range(n)], 1)
        k = here[3:4]
        x = jnp.where(lax.broadcasted_iota(jnp.int32, here.shape, 0) < 3, here, 0.0)
        diff = y - jnp.concatenate([x, x], 0)
        kept = k * diff
        dy = (2.0 * kept).astype(BF)
        da = dot(on[...], dy) * slope
        for dc, view in enumerate(sides(da)):
            first = 0
            for e, n in spans:
                da_s[dc, :, at(b * (rows + 2) + e - 1, n)] = view[:, first : first + n * W].astype(BF)
                first += n * W
        if own:
            l_s[128:144] += fold(kept * diff, 256)
            g_o[...] += dot(dy, g, NT)
            g_d[...] += dot(u, da.astype(BF), NT)

    def edge(b, _):
        decode(b, [(1, 1), (rows + 2, 1)], False)
        return 0

    lax.fori_loop(0, batches, edge, 0)

    def middle(i, _):
        n = step_d
        decode(i // (rows // n), [((i % (rows // n)) * n + 2, n)], True)
        return 0

    lax.fori_loop(0, batches * (rows // step_d), middle, 0)

    def back(i, _):
        n = step_b
        b, r = i // (rows // n), (i % (rows // n)) * n
        own = at(i * n, n)
        du = jnp.zeros((128, n * W), F32)
        for dr in range(3):
            for dc in range(3):
                t = 3 * dr + dc
                view = da_s[2 - dc, :, at(b * (rows + 2) + r + 2 - dr, n)]
                du = du + dot(dn[t * 128 : (t + 1) * 128], view)
        dz = (du + gap_s[:, own]).astype(BF)
        g_z[...] += dot(dz, h_s[:, own], NT)
        dpre = (dot(zn[...], dz) * slope_s[:, own]).astype(BF)
        g_e[...] += dot(p_s[:, own], dpre, NT)
        return 0

    lax.fori_loop(0, batches * (rows // step_b), back, 0)

    def give(start, one, zero, keep, offset):
        n = one.shape[0]
        keep[start : start + n] = jnp.where(bottom, one, zero).astype(keep.dtype)
        send[offset + start : offset + start + n] = jnp.where(bottom, zero, one).astype(BF)

    for t in range(9):
        top = jnp.concatenate([g_d[t * 128 + 64 : (t + 1) * 128, 128:256], jnp.zeros((64, 128), F32)], 0)
        give(t * 128, g_d[t * 128 : (t + 1) * 128, 0:128], top, keep_big, 0)
    for half in range(2):
        cols = slice(half * 128, (half + 1) * 128)
        give(TAPS + half * 128, g_s[0, 0:128, cols], g_s[1, 0:128, cols], keep_big, 0)
    give(S_Z, g_z[0:64, 0:128], g_z[64:128, 128:256], keep_small, BIG)
    enc = []
    for cols in (slice(0, 128), slice(128, 256)):
        runs = [g_e[8 * t : 8 * t + 3, cols] for t in range(9)]
        enc.append(jnp.concatenate(runs + [jnp.zeros((5, 128), F32)], 0))
    give(S_E, enc[0], enc[1], keep_small, BIG)
    blank = jnp.zeros((8, 128), F32)
    give(
        S_O,
        jnp.concatenate([g_o[0:8, 0:128], blank], 0),
        jnp.concatenate([g_o[8:16, 128:256], blank], 0),
        keep_small,
        BIG,
    )
    valid_sum = jnp.sum(g_s[0, 128:130])
    loss = 0.25 * jnp.sum(l_s[0:128]) + jnp.sum(l_s[128:144])
    lane = lax.broadcasted_iota(jnp.int32, (1, W), 1)
    other = jnp.where(lane == 0, loss, jnp.where(lane == 1, valid_sum, 0.0))
    exact = []
    for v in range(2):
        runs = [g_s[v, 128 + hi : 129 + hi, half * 128 : (half + 1) * 128] for hi in range(2) for half in range(2)]
        pieces = part(jnp.concatenate(runs + [other], 0), 3)
        exact.append(jnp.concatenate([p.astype(F32) for p in pieces] + [jnp.zeros((1, 128), F32)], 0))
    give(S_X, exact[0], exact[1], keep_small, BIG)


def update_kernel(
    order, *refs, stages
):
    (parts, refs) = refs[:stages], refs[stages:]
    (count, total, ew, e1, e2, zw, z1, z2, dw, d1, d2, ow, o1, o2,
     loss_out, valid_out, count_out, total_out,
     em, es, ep, ec, zm, zs, zp, zc, dm, ds, dp, dc, om, os, op, oc, big, flat) = refs
    share = BIG // stages
    small = jnp.zeros((SMALL, W), F32)
    for n, ref in enumerate(parts):
        big[pl.ds(pl.multiple_of(order[n] * share, 16), share), :] = ref[0:share].astype(F32)
        small = small + ref[share : share + SMALL].astype(F32)
    exact = sum(small[S_X + EXACT * i : S_X + EXACT * (i + 1)] for i in range(3))
    loss = jnp.sum(exact[4:5, 0:1])
    valid = jnp.sum(exact[4:5, 1:2])
    loss_out[0, 0] = loss
    valid_out[0, 0] = valid
    counts = jnp.concatenate([exact[i : i + 1] for i in range(4)], 1)
    count_out[...] = 0.99 * count[...] + 0.01 * counts
    for quarter in range(4):
        row = TAPS + (quarter % 2) * 128 + (quarter // 2) * 64
        flat[0:64] = big[row : row + 64]
        rows = slice(quarter * 128, (quarter + 1) * 128)
        total_out[0, rows] = 0.99 * total[0, rows] + 0.01 * flat[...].T[:, 0:64]

    scale = 1.0 - 0.5**STEP

    def adamw(grad, w, first, second, rate, outs):
        grad = grad / valid
        moment = 0.5 * first[0] + 0.5 * grad
        square = 0.5 * second[0] + 0.5 * grad * grad
        weight = w[0]
        master = weight - rate * (moment / scale / (jnp.sqrt(square / scale) + 1e-08) + 0.01 * weight)
        outs[0][0] = moment
        outs[1][0] = square
        outs[2][0] = master
        outs[3][0] = master.astype(BF)

    adamw(small[S_E : S_E + 27], ew, e1, e2, RATES[0], (em, es, ep, ec))
    flat[0:64] = small[S_Z : S_Z + 64]
    adamw(flat[...].T[:, 0:64], zw, z1, z2, RATES[1], (zm, zs, zp, zc))
    adamw(big[0:TAPS], dw, d1, d2, RATES[2], (dm, ds, dp, dc))
    flat[0:16] = small[S_O : S_O + 16]
    adamw(flat[...].T[:, 0:3], ow, o1, o2, RATES[3], (om, os, op, oc))


def radices(devices):
    bits = devices.bit_length() - 1
    return [(start, min(2, bits - start)) for start in range(0, bits, 2)]


def partners(start, width):
    return [k << start for k in range(1, 1 << width)]


def xor_pairs(devices, by):
    return [(i, i ^ by) for i in range(devices)]


def lowered(value):
    return lax.reduce_precision(value, 8, 7)


def sum_small(parts):
    total = sum(item.astype(F32) for item in parts)
    value = sum(total[S_X + EXACT * i : S_X + EXACT * (i + 1)] for i in range(3))
    high = lowered(value)
    middle = lowered(value - high)
    low = value - high - middle
    rest = total[S_X + 3 * EXACT :]
    return jnp.concatenate([total[:S_X], high, middle, low, rest], 0).astype(BF)


def local(
    image, mask, codes, ema_count, ema_sum,
    encoder_weight, encoder_first, encoder_second,
    latent_weight, latent_first, latent_second,
    decoder_weight, decoder_first, decoder_second,
    readout_weight, readout_first, readout_second,
):
    batches, _, band, width = image.shape
    rows = band // 2
    level, me = lax.axis_index("level"), lax.axis_index("dp")
    devices = lax.axis_size("dp")
    row_first = me * band + band
    top_ok = (row_first % CROP != 0) & (me > 0)
    bottom_ok = ((row_first + band) % CROP != 0) & (me < devices - 1)
    valid = jnp.where(level == 0, top_ok, bottom_ok)
    place = jnp.stack([level, valid.astype(jnp.int32)]).astype(jnp.int32)

    limit = pltpu.CompilerParams(vmem_limit_bytes=56 * 1024 * 1024)
    packed = R_CODE + batches * band
    tile, near, across, pack = pl.pallas_call(
        pack_kernel,
        out_shape=[
            jax.ShapeDtypeStruct((batches * band * 8, W), F32),
            jax.ShapeDtypeStruct((batches * 16, W), BF),
            jax.ShapeDtypeStruct((16, W), BF),
            jax.ShapeDtypeStruct((packed, W), BF),
        ],
        in_specs=[SMEM] + [VMEM] * 9,
        out_specs=[VMEM] * 4,
        scratch_shapes=[pltpu.VMEM((batches * band, W), F32), pltpu.VMEM((128, 128), F32)],
        compiler_params=limit,
    )(place, image, mask, codes, ema_count, ema_sum, encoder_weight, latent_weight, decoder_weight, readout_weight)

    both = ("level", "dp")
    same = [(d - 1, d) for d in range(1, devices)] + [(devices + d + 1, devices + d) for d in range(devices - 1)]
    cross = [(devices + d - 1, d) for d in range(1, devices)] + [(d + 1, devices + d) for d in range(devices - 1)]
    near = lax.ppermute(near, both, same)
    across = lax.ppermute(across, both, cross)
    theirs = lax.ppermute(pack, "level", [(0, 1), (1, 0)])

    ext = rows + 4
    pixels = batches * rows * W
    keep_big, keep_small, send = pl.pallas_call(
        functools.partial(step_kernel, batches=batches, rows=rows, step_e=rows, step_d=rows, step_b=rows // 2),
        out_shape=[
            jax.ShapeDtypeStruct((BIG, W), F32),
            jax.ShapeDtypeStruct((SMALL, W), BF),
            jax.ShapeDtypeStruct((BIG + SMALL, W), BF),
        ],
        in_specs=[SMEM] + [VMEM] * 5,
        out_specs=[VMEM] * 3,
        scratch_shapes=[
            pltpu.VMEM((batches, ext, 8, W), F32),
            pltpu.VMEM((batches * band + 16, W), F32),
            pltpu.VMEM((TAPS, 256), BF),
            pltpu.VMEM((256, TAPS), BF),
            pltpu.VMEM((256, 128), BF),
            pltpu.VMEM((256, 128), BF),
            pltpu.VMEM((128, 256), BF),
            pltpu.VMEM((16, 256), BF),
            pltpu.VMEM((256, 16), BF),
            pltpu.VMEM((2, 128, 256), BF),
            pltpu.VMEM((3, 128, batches * ext * W), BF),
            pltpu.VMEM((128, pixels), BF),
            pltpu.VMEM((256, pixels), BF),
            pltpu.VMEM((256, pixels), F32),
            pltpu.VMEM((128, pixels), F32),
            pltpu.VMEM((3, 256, batches * (rows + 2) * W), BF),
            pltpu.VMEM((TAPS, 256), F32),
            pltpu.VMEM((16, 256), F32),
            pltpu.VMEM((128, 256), F32),
            pltpu.VMEM((128, 256), F32),
            pltpu.VMEM((2, 144, 256), F32),
            pltpu.VMEM((144, 256), F32),
        ],
        compiler_params=limit,
    )(place, tile, near, across, pack, theirs)

    got = lax.ppermute(send, "level", [(0, 1), (1, 0)])
    small = sum_small([keep_small, got[BIG:]])
    big = keep_big + got[:BIG].astype(F32)

    stages = radices(devices)
    for start, width_bits in stages:
        count = 1 << width_bits
        index = (me >> start) & (count - 1)
        pieces = big.reshape(count, -1, W)
        total = lax.dynamic_index_in_dim(pieces, index, 0, False)
        for k in range(count - 1, 0, -1):
            out = lax.dynamic_index_in_dim(pieces, index ^ k, 0, False).astype(BF)
            total = total + lax.ppermute(out, "dp", xor_pairs(devices, k << start)).astype(F32)
        big = total
    big = big.astype(BF)
    for number, (start, width_bits) in enumerate(reversed(stages)):
        count = 1 << width_bits
        index = (me >> start) & (count - 1)
        payload = jnp.concatenate([big, small], 0)
        parts = [payload] + [lax.ppermute(payload, "dp", xor_pairs(devices, k << start)) for k in range(1, count)]
        order = jnp.stack([index ^ k for k in range(count)]).astype(jnp.int32)
        if number == len(stages) - 1:
            break
        size = big.shape[0]
        stacked = jnp.zeros((count, size, W), BF)
        for k in range(count):
            stacked = lax.dynamic_update_index_in_dim(stacked, parts[k][:size], index ^ k, 0)
        big = stacked.reshape(count * size, W)
        small = sum_small([item[size:] for item in parts])

    state = (
        ema_count, ema_sum,
        encoder_weight, encoder_first, encoder_second, latent_weight, latent_first, latent_second,
        decoder_weight, decoder_first, decoder_second, readout_weight, readout_first, readout_second,
    )
    outs = [jax.ShapeDtypeStruct((1, 1), F32)] * 2
    outs += [jax.ShapeDtypeStruct(ema_count.shape, F32), jax.ShapeDtypeStruct(ema_sum.shape, F32)]
    for item in (encoder_weight, latent_weight, decoder_weight, readout_weight):
        outs += [jax.ShapeDtypeStruct(item.shape, F32)] * 3 + [jax.ShapeDtypeStruct(item.shape, BF)]
    result = pl.pallas_call(
        functools.partial(update_kernel, stages=len(parts)),
        out_shape=outs,
        in_specs=[SMEM] + [VMEM] * (len(parts) + len(state)),
        out_specs=[SMEM] * 2 + [VMEM] * (len(outs) - 2),
        scratch_shapes=[pltpu.VMEM((BIG, W), F32), pltpu.VMEM((128, 128), F32)],
        compiler_params=limit,
    )(order, *parts, *state)
    return (result[0].reshape(()), result[1].reshape(()), *result[2:])


def solution(mesh):
    rank = (0, 0, 2, 3) + (3,) * 16
    in_specs = (P(None, None, "dp", None), P(None, "dp", None), P("level", None, "dp", None), P("level", None))
    in_specs += (P("level", None, None),) * 13
    out_specs = tuple(P(*(("level",) + (None,) * (n - 1) if n else ())) for n in rank)
    return jax.shard_map(local, mesh=mesh, in_specs=in_specs, out_specs=out_specs, check_vma=False)
```

profile of v0, /device:TPU:0, one launch (start us, length us, event | category | flops | bytes accessed | tf_op | source)
XLA Modules:
  0.0 109.8 jit_solution(11196550751239883520)
XLA Ops:
  0.7 0.7 copy-done.16
  2.0 0.7 copy.39.lat.refs_9_
  2.7 0.7 copy.40.read.refs_15_
  3.5 0.8 copy.37.total.refs_5_
  4.9 2.3 %shard_map.320 = (f32[768,128]{1,0:T(8,128)}, bf16[48,128]{1,0:T(8,128)(2,1)}, bf16[16,128]{1,0:T(8,128)(2,1)}, bf16[1840,128]{1,0:T(8,128)(2,1)}) custom-call(s32[2]{0:T(128)} %pad_add_fusion.1.place, bf16[3,3,32,128]{3,2,1,0:T(8,128)(2,1)} %image.1, s32[3,32,128]{2,1,0:T(8,128)} %mask.1, s32[1,3,32,128]{3,2,1,0:T(8,128)} %codes.1, f32[1,512]{1,0:T(1,128)} %refs_4_.1, ...), custom_call_target="tpu_custom_call" | custom-call | tf_op jit(solution)/shard_map/pallas_call | solution.py:464
  7.7 4.4 %collective-permute-start = (bf16[48,128]{1,0:T(8,128)(2,1)}, bf16[48,128]{1,0:T(8,128)(2,1)S(1)}, u32[]{:S(2)}, u32[]{:S(2)}) collective-permute-start(bf16[48,128]{1,0:T(8,128)(2,1)} %get-tuple-element.48), channel_id=1, source_target_pairs={{0,1},{1,2},{2,3},{3,4},{4,5},{5,6},{6,7},{7,8},{8,9},{9,10},{10,1... | collective-permute-start | bytes 36872 | tf_op jit(solution)/shard_map/ppermute | solution.py:481
  12.1 0.7 collective-permute-start.1
  12.8 0.9 collective-permute-done.near
  14.5 36.1 %shard_map.321 = (f32[1408,128]{1,0:T(8,128)}, bf16[128,128]{1,0:T(8,128)(2,1)}, bf16[1536,128]{1,0:T(8,128)(2,1)}) custom-call(s32[2]{0:T(128)} %pad_add_fusion.1.place, f32[768,128]{1,0:T(8,128)} %get-tuple-element.47.tile, bf16[48,128]{1,0:T(8,128)(2,1)} %copy-done.19, bf16[16,128]{1,0:T(8,128)(2,1)} %copy-done.20, ...), custom_call_target="tpu_custom_call" | custom-call | tf_op jit(solution)/shard_map/pallas_call | solution.py:487
  50.6 3.2 %collective-permute-start.3 = (bf16[1536,128]{1,0:T(8,128)(2,1)}, bf16[1536,128]{1,0:T(8,128)(2,1)S(1)}, u32[]{:S(2)}, u32[]{:S(2)}) collective-permute-start(bf16[1536,128]{1,0:T(8,128)(2,1)} %get-tuple-element.52), channel_id=1, source_target_pairs={{0,16},{16,0},{1,17},{17,1},{2,18},{18,2},{3,19},{19,3},{4,20},{20... | collective-permute-start | bytes 1179656 | tf_op jit(solution)/shard_map/ppermute | solution.py:523
  53.8 1.6 %collective-permute-done.3 = bf16[1536,128]{1,0:T(8,128)(2,1)S(1)} collective-permute-done((bf16[1536,128]{1,0:T(8,128)(2,1)}, bf16[1536,128]{1,0:T(8,128)(2,1)S(1)}, u32[]{:S(2)}, u32[]{:S(2)}) %collective-permute-start.3) | collective-permute-done | bytes 393248 | tf_op jit(solution)/shard_map/ppermute | solution.py:523
  55.4 1.2 %convert_add_fusion = f32[1408,128]{1,0:T(8,128)S(1)} fusion(f32[1408,128]{1,0:T(8,128)} %get-tuple-element.51, bf16[1536,128]{1,0:T(8,128)(2,1)S(1)} %collective-permute-done.3), kind=kLoop, calls=%fused_computation | loop fusion | flops 360448 | bytes 1802240 | tf_op jit(solution)/shard_map/add | solution.py:525
  56.6 3.7 %collective-permute-start.4 = (bf16[352,128]{1,0:T(8,128)(2,1)S(1)}, bf16[352,128]{1,0:T(8,128)(2,1)S(1)}, u32[]{:S(2)}, u32[]{:S(2)}) collective-permute-start(bf16[352,128]{1,0:T(8,128)(2,1)S(1)} %get-tuple-element.102), channel_id=1, source_target_pairs={{0,3},{1,2},{2,1},{3,0},{4,7},{5,6},{6,5},{7,4},{8,11},{9,10},{10,... | collective-permute-start | bytes 270344 | tf_op jit(solution)/shard_map/ppermute | solution.py:535
  60.3 0.7 collective-permute-start.6
  61.1 2.7 %collective-permute-done.4 = bf16[352,128]{1,0:T(8,128)(2,1)S(1)} collective-permute-done((bf16[352,128]{1,0:T(8,128)(2,1)S(1)}, bf16[352,128]{1,0:T(8,128)(2,1)S(1)}, u32[]{:S(2)}, u32[]{:S(2)}) %collective-permute-start.4) | collective-permute-done | bytes 90144 | tf_op jit(solution)/shard_map/ppermute | solution.py:535
  63.8 1.8 %collective-permute-done.6 = bf16[352,128]{1,0:T(8,128)(2,1)S(1)} collective-permute-done((bf16[352,128]{1,0:T(8,128)(2,1)S(1)}, bf16[352,128]{1,0:T(8,128)(2,1)S(1)}, u32[]{:S(2)}, u32[]{:S(2)}) %collective-permute-start.6) | collective-permute-done | bytes 90144 | tf_op jit(solution)/shard_map/ppermute | solution.py:535
  65.7 4.5 %collective-permute-start.7 = (bf16[88,128]{1,0:T(8,128)(2,1)S(1)}, bf16[88,128]{1,0:T(8,128)(2,1)S(1)}, u32[]{:S(2)}, u32[]{:S(2)}) collective-permute-start(bf16[88,128]{1,0:T(8,128)(2,1)S(1)} %get-tuple-element.107), channel_id=1, source_target_pairs={{0,12},{1,13},{2,14},{3,15},{4,8},{5,9},{6,10},{7,11},{8,4},{9,5},... | collective-permute-start | bytes 67592 | tf_op jit(solution)/shard_map/ppermute | solution.py:535
  70.2 0.6 collective-permute-start.8
  70.9 1.1 %collective-permute-done.7 = bf16[88,128]{1,0:T(8,128)(2,1)S(1)} collective-permute-done((bf16[88,128]{1,0:T(8,128)(2,1)S(1)}, bf16[88,128]{1,0:T(8,128)(2,1)S(1)}, u32[]{:S(2)}, u32[]{:S(2)}) %collective-permute-start.7) | collective-permute-done | bytes 22560 | tf_op jit(solution)/shard_map/ppermute | solution.py:535
  72.0 2.0 %collective-permute-done.9 = bf16[88,128]{1,0:T(8,128)(2,1)S(1)} collective-permute-done((bf16[88,128]{1,0:T(8,128)(2,1)S(1)}, bf16[88,128]{1,0:T(8,128)(2,1)S(1)}, u32[]{:S(2)}, u32[]{:S(2)}) %collective-permute-start.9) | collective-permute-done | bytes 22560 | tf_op jit(solution)/shard_map/ppermute | solution.py:535
  74.0 0.9 collective-permute-done.8
  75.1 1.8 %collective-permute-start.12 = (bf16[216,128]{1,0:T(8,128)(2,1)S(1)}, bf16[216,128]{1,0:T(8,128)(2,1)S(1)}, u32[]{:S(2)}, u32[]{:S(2)}) collective-permute-start(bf16[216,128]{1,0:T(8,128)(2,1)S(1)} %concatenate.14), channel_id=1, source_target_pairs={{0,12},{1,13},{2,14},{3,15},{4,8},{5,9},{6,10},{7,11},{8,4},{9,5},... | collective-permute-start | bytes 165896 | tf_op jit(solution)/shard_map/ppermute | solution.py:542
  76.9 1.8 %collective-permute-start.11 = (bf16[216,128]{1,0:T(8,128)(2,1)S(1)}, bf16[216,128]{1,0:T(8,128)(2,1)S(1)}, u32[]{:S(2)}, u32[]{:S(2)}) collective-permute-start(bf16[216,128]{1,0:T(8,128)(2,1)S(1)} %concatenate.14), channel_id=1, source_target_pairs={{0,8},{1,9},{2,10},{3,11},{4,12},{5,13},{6,14},{7,15},{8,0},{9,1},... | collective-permute-start | bytes 165896 | tf_op jit(solution)/shard_map/ppermute | solution.py:542
  78.7 0.9 collective-permute-start.10
  79.7 1.5 %collective-permute-done.12 = bf16[216,128]{1,0:T(8,128)(2,1)S(1)} collective-permute-done((bf16[216,128]{1,0:T(8,128)(2,1)S(1)}, bf16[216,128]{1,0:T(8,128)(2,1)S(1)}, u32[]{:S(2)}, u32[]{:S(2)}) %collective-permute-start.12) | collective-permute-done | bytes 55328 | tf_op jit(solution)/shard_map/ppermute | solution.py:542
  81.2 1.4 %collective-permute-done.11 = bf16[216,128]{1,0:T(8,128)(2,1)S(1)} collective-permute-done((bf16[216,128]{1,0:T(8,128)(2,1)S(1)}, bf16[216,128]{1,0:T(8,128)(2,1)S(1)}, u32[]{:S(2)}, u32[]{:S(2)}) %collective-permute-start.11) | collective-permute-done | bytes 55328 | tf_op jit(solution)/shard_map/ppermute | solution.py:542
  84.1 0.9 collective-permute-start.14
  84.9 2.1 %collective-permute-start.13 = (bf16[480,128]{1,0:T(8,128)(2,1)S(1)}, bf16[480,128]{1,0:T(8,128)(2,1)S(1)}, u32[]{:S(2)}, u32[]{:S(2)}) collective-permute-start(bf16[480,128]{1,0:T(8,128)(2,1)S(1)} %concatenate.16.refs_0_), channel_id=1, source_target_pairs={{0,1},{1,0},{2,3},{3,2},{4,5},{5,4},{6,7},{7,6},{8,9},{9,8},{10,11... | collective-permute-start | bytes 368648 | tf_op jit(solution)/shard_map/ppermute | solution.py:542
  87.0 0.6 copy.43.refs_7_
  88.3 0.7 copy.46.refs_10_
  89.0 0.7 copy.47.refs_11_
  89.8 0.7 copy.49.refs_16_
  90.5 0.7 copy.50.refs_17_
  91.8 0.6 copy-done.4
  92.5 0.6 copy-done.6
  93.2 3.9 %shard_map.322 = (f32[1,1]{1,0:T(1,128)}, f32[1,1]{1,0:T(1,128)}, f32[1,512]{1,0:T(1,128)}, f32[1,512,64]{2,1,0:T(8,128)}, f32[1,27,128]{2,1,0:T(8,128)}, /*inde...) custom-call(s32[4]{0:T(128)} %pad_add_fusion.order, ...), custom_call_target="tpu_custom_call" | custom-call | tf_op jit(solution)/shard_map/pallas_call | solution.py:562
  97.1 1.4 %copy.62 = bf16[1,128,3]{1,2,0:T(4,128)(2,1)} copy(bf16[1,128,3]{2,1,0:T(8,128)(2,1)} %get-tuple-element.93) | data formatting | bytes 1536
  98.6 1.5 %copy.59 = f32[1,128,3]{1,0,2:T(1,128)} copy(f32[1,128,3]{2,1,0:T(8,128)} %get-tuple-element.90) | data formatting | bytes 3072
  100.1 0.6 copy.60
  100.7 0.6 copy.61
  101.4 1.3 %copy.52 = f32[1,27,128]{2,0,1:T(1,128)} copy(f32[1,27,128]{2,1,0:T(8,128)} %get-tuple-element.78) | data formatting | bytes 27648
  102.7 1.3 %copy.53 = f32[1,27,128]{2,0,1:T(1,128)} copy(f32[1,27,128]{2,1,0:T(8,128)} %get-tuple-element.79) | data formatting | bytes 27648
  104.0 1.3 %copy.54 = f32[1,27,128]{2,0,1:T(1,128)} copy(f32[1,27,128]{2,1,0:T(8,128)} %get-tuple-element.80) | data formatting | bytes 27648
  105.3 1.4 %copy.58 = bf16[1,128,64]{1,2,0:T(8,128)(2,1)} copy(bf16[1,128,64]{2,1,0:T(8,128)(2,1)} %get-tuple-element.85) | data formatting | bytes 32768
  106.8 0.7 copy.55
  107.5 0.7 copy.56
  108.3 0.7 copy.57
  109.0 0.8 copy.51
  (83 shorter events, 5.8 us)
Async XLA Ops:
  0.7 0.7 copy-start.16
  0.7 1.3 %copy-start.12 = (f32[1,128,64]{1,2,0:T(8,128)S(1)}, f32[1,128,64]{1,2,0:T(8,128)}, u32[]{:S(2)}) copy-start(f32[1,128,64]{1,2,0:T(8,128)} %param.25) | copy-start | bytes 98308
  0.7 2.8 %copy-start.3 = (f32[1,512,64]{1,2,0:T(8,128)S(1)}, f32[1,512,64]{1,2,0:T(8,128)}, u32[]{:S(2)}) copy-start(f32[1,512,64]{1,2,0:T(8,128)} %param.21) | copy-start | bytes 393220
  2.0 0.7 copy-start.21
  7.2 4.9 %copy-start.24 = (bf16[16,128]{1,0:T(8,128)(2,1)S(1)}, bf16[16,128]{1,0:T(8,128)(2,1)}, u32[]{:S(2)}) copy-start(bf16[16,128]{1,0:T(8,128)(2,1)} %get-tuple-element.49) | copy-start | bytes 12292
  7.2 6.5 %collective-permute-start.2 = (bf16[1840,128]{1,0:T(8,128)(2,1)}, bf16[1840,128]{1,0:T(8,128)(2,1)S(1)}, u32[]{:S(2)}, u32[]{:S(2)}) collective-permute-start(bf16[1840,128]{1,0:T(8,128)(2,1)} %get-tuple-element.50.mine), channel_id=1, source_target_pairs={{0,16},{16,0},{1,17},{17,1},{2,18},{18,2},{3,19},{19,3},{4,20},{20... | collective-permute-start | bytes 1413128 | tf_op jit(solution)/shard_map/ppermute | solution.py:483
  7.7 6.0 %collective-permute-start = (bf16[48,128]{1,0:T(8,128)(2,1)}, bf16[48,128]{1,0:T(8,128)(2,1)S(1)}, u32[]{:S(2)}, u32[]{:S(2)}) collective-permute-start(bf16[48,128]{1,0:T(8,128)(2,1)} %get-tuple-element.48), channel_id=1, source_target_pairs={{0,1},{1,2},{2,3},{3,4},{4,5},{5,6},{6,7},{7,8},{8,9},{9,10},{10,1... | collective-permute-start | bytes 36872 | tf_op jit(solution)/shard_map/ppermute | solution.py:481
  12.1 0.7 collective-permute-start.1
  12.8 0.9 copy-start.20
  13.7 0.6 copy-start.19
  13.7 0.8 copy-start.1
  50.6 4.8 %collective-permute-start.3 = (bf16[1536,128]{1,0:T(8,128)(2,1)}, bf16[1536,128]{1,0:T(8,128)(2,1)S(1)}, u32[]{:S(2)}, u32[]{:S(2)}) collective-permute-start(bf16[1536,128]{1,0:T(8,128)(2,1)} %get-tuple-element.52), channel_id=1, source_target_pairs={{0,16},{16,0},{1,17},{17,1},{2,18},{18,2},{3,19},{19,3},{4,20},{20... | collective-permute-start | bytes 1179656 | tf_op jit(solution)/shard_map/ppermute | solution.py:523
  56.5 4.5 %copy-start.15 = (bf16[128,128]{1,0:T(8,128)(2,1)S(1)}, bf16[128,128]{1,0:T(8,128)(2,1)}, u32[]{:S(2)}) copy-start(bf16[128,128]{1,0:T(8,128)(2,1)} %get-tuple-element.53) | copy-start | bytes 98308
  56.6 7.2 %collective-permute-start.4 = (bf16[352,128]{1,0:T(8,128)(2,1)S(1)}, bf16[352,128]{1,0:T(8,128)(2,1)S(1)}, u32[]{:S(2)}, u32[]{:S(2)}) collective-permute-start(bf16[352,128]{1,0:T(8,128)(2,1)S(1)} %get-tuple-element.102), channel_id=1, source_target_pairs={{0,3},{1,2},{2,1},{3,0},{4,7},{5,6},{6,5},{7,4},{8,11},{9,10},{10,... | collective-permute-start | bytes 270344 | tf_op jit(solution)/shard_map/ppermute | solution.py:535
  60.3 5.3 %collective-permute-start.6 = (bf16[352,128]{1,0:T(8,128)(2,1)S(1)}, bf16[352,128]{1,0:T(8,128)(2,1)S(1)}, u32[]{:S(2)}, u32[]{:S(2)}) collective-permute-start(bf16[352,128]{1,0:T(8,128)(2,1)S(1)} %get-tuple-element.103), channel_id=1, source_target_pairs={{0,1},{1,0},{2,3},{3,2},{4,5},{5,4},{6,7},{7,6},{8,9},{9,8},{10,11... | collective-permute-start | bytes 270344 | tf_op jit(solution)/shard_map/ppermute | solution.py:535
  61.1 4.6 %collective-permute-start.5 = (bf16[352,128]{1,0:T(8,128)(2,1)S(1)}, bf16[352,128]{1,0:T(8,128)(2,1)S(1)}, u32[]{:S(2)}, u32[]{:S(2)}) collective-permute-start(bf16[352,128]{1,0:T(8,128)(2,1)S(1)} %get-tuple-element.104), channel_id=1, source_target_pairs={{0,2},{1,3},{2,0},{3,1},{4,6},{5,7},{6,4},{7,5},{8,10},{9,11},{10,... | collective-permute-start | bytes 270344 | tf_op jit(solution)/shard_map/ppermute | solution.py:535
  65.7 6.3 %collective-permute-start.7 = (bf16[88,128]{1,0:T(8,128)(2,1)S(1)}, bf16[88,128]{1,0:T(8,128)(2,1)S(1)}, u32[]{:S(2)}, u32[]{:S(2)}) collective-permute-start(bf16[88,128]{1,0:T(8,128)(2,1)S(1)} %get-tuple-element.107), channel_id=1, source_target_pairs={{0,12},{1,13},{2,14},{3,15},{4,8},{5,9},{6,10},{7,11},{8,4},{9,5},... | collective-permute-start | bytes 67592 | tf_op jit(solution)/shard_map/ppermute | solution.py:535
  70.2 3.8 %collective-permute-start.9 = (bf16[88,128]{1,0:T(8,128)(2,1)S(1)}, bf16[88,128]{1,0:T(8,128)(2,1)S(1)}, u32[]{:S(2)}, u32[]{:S(2)}) collective-permute-start(bf16[88,128]{1,0:T(8,128)(2,1)S(1)} %get-tuple-element.108), channel_id=1, source_target_pairs={{0,4},{1,5},{2,6},{3,7},{4,0},{5,1},{6,2},{7,3},{8,12},{9,13},{10,... | collective-permute-start | bytes 67592 | tf_op jit(solution)/shard_map/ppermute | solution.py:535
  70.2 4.7 %collective-permute-start.8 = (bf16[88,128]{1,0:T(8,128)(2,1)S(1)}, bf16[88,128]{1,0:T(8,128)(2,1)S(1)}, u32[]{:S(2)}, u32[]{:S(2)}) collective-permute-start(bf16[88,128]{1,0:T(8,128)(2,1)S(1)} %get-tuple-element.109), channel_id=1, source_target_pairs={{0,8},{1,9},{2,10},{3,11},{4,12},{5,13},{6,14},{7,15},{8,0},{9,1},... | collective-permute-start | bytes 67592 | tf_op jit(solution)/shard_map/ppermute | solution.py:535
  75.1 6.1 %collective-permute-start.12 = (bf16[216,128]{1,0:T(8,128)(2,1)S(1)}, bf16[216,128]{1,0:T(8,128)(2,1)S(1)}, u32[]{:S(2)}, u32[]{:S(2)}) collective-permute-start(bf16[216,128]{1,0:T(8,128)(2,1)S(1)} %concatenate.14), channel_id=1, source_target_pairs={{0,12},{1,13},{2,14},{3,15},{4,8},{5,9},{6,10},{7,11},{8,4},{9,5},... | collective-permute-start | bytes 165896 | tf_op jit(solution)/shard_map/ppermute | solution.py:542
  76.9 5.7 %collective-permute-start.11 = (bf16[216,128]{1,0:T(8,128)(2,1)S(1)}, bf16[216,128]{1,0:T(8,128)(2,1)S(1)}, u32[]{:S(2)}, u32[]{:S(2)}) collective-permute-start(bf16[216,128]{1,0:T(8,128)(2,1)S(1)} %concatenate.14), channel_id=1, source_target_pairs={{0,8},{1,9},{2,10},{3,11},{4,12},{5,13},{6,14},{7,15},{8,0},{9,1},... | collective-permute-start | bytes 165896 | tf_op jit(solution)/shard_map/ppermute | solution.py:542
  78.7 4.5 %collective-permute-start.10 = (bf16[216,128]{1,0:T(8,128)(2,1)S(1)}, bf16[216,128]{1,0:T(8,128)(2,1)S(1)}, u32[]{:S(2)}, u32[]{:S(2)}) collective-permute-start(bf16[216,128]{1,0:T(8,128)(2,1)S(1)} %concatenate.14), channel_id=1, source_target_pairs={{0,4},{1,5},{2,6},{3,7},{4,0},{5,1},{6,2},{7,3},{8,12},{9,13},{10,... | collective-permute-start | bytes 165896 | tf_op jit(solution)/shard_map/ppermute | solution.py:542
  83.3 3.8 %copy-start.17 = (f32[1,27,128]{2,0,1:T(1,128)S(1)}, f32[1,27,128]{2,0,1:T(1,128)}, u32[]{:S(2)}) copy-start(f32[1,27,128]{2,0,1:T(1,128)} %param.23) | copy-start | bytes 41476
  83.3 4.3 %copy-start.18 = (f32[1,27,128]{2,0,1:T(1,128)S(1)}, f32[1,27,128]{2,0,1:T(1,128)}, u32[]{:S(2)}) copy-start(f32[1,27,128]{2,0,1:T(1,128)} %param.24) | copy-start | bytes 41476
  83.5 6.3 %copy-start = (bf16[480,128]{1,0:T(8,128)(2,1)}, bf16[480,128]{1,0:T(8,128)(2,1)S(1)}, u32[]{:S(2)}) copy-start(bf16[480,128]{1,0:T(8,128)(2,1)S(1)} %concatenate.16.refs_0_) | copy-start | bytes 368644
  83.5 4.8 %copy-start.13 = (f32[1,128,64]{1,2,0:T(8,128)S(1)}, f32[1,128,64]{1,2,0:T(8,128)}, u32[]{:S(2)}) copy-start(f32[1,128,64]{1,2,0:T(8,128)} %param.26) | copy-start | bytes 98308
  83.5 8.3 %collective-permute-start.15 = (bf16[480,128]{1,0:T(8,128)(2,1)S(1)}, bf16[480,128]{1,0:T(8,128)(2,1)S(1)}, u32[]{:S(2)}, u32[]{:S(2)}) collective-permute-start(bf16[480,128]{1,0:T(8,128)(2,1)S(1)} %concatenate.16.refs_0_), channel_id=1, source_target_pairs={{0,3},{1,2},{2,1},{3,0},{4,7},{5,6},{6,5},{7,4},{8,11},{9,10},{10,... | collective-permute-start | bytes 368648 | tf_op jit(solution)/shard_map/ppermute | solution.py:542
  84.1 7.8 %collective-permute-start.14 = (bf16[480,128]{1,0:T(8,128)(2,1)S(1)}, bf16[480,128]{1,0:T(8,128)(2,1)S(1)}, u32[]{:S(2)}, u32[]{:S(2)}) collective-permute-start(bf16[480,128]{1,0:T(8,128)(2,1)S(1)} %concatenate.16.refs_0_), channel_id=1, source_target_pairs={{0,2},{1,3},{2,0},{3,1},{4,6},{5,7},{6,4},{7,5},{8,10},{9,11},{10,... | collective-permute-start | bytes 368648 | tf_op jit(solution)/shard_map/ppermute | solution.py:542
  84.9 6.9 %collective-permute-start.13 = (bf16[480,128]{1,0:T(8,128)(2,1)S(1)}, bf16[480,128]{1,0:T(8,128)(2,1)S(1)}, u32[]{:S(2)}, u32[]{:S(2)}) collective-permute-start(bf16[480,128]{1,0:T(8,128)(2,1)S(1)} %concatenate.16.refs_0_), channel_id=1, source_target_pairs={{0,1},{1,0},{2,3},{3,2},{4,5},{5,4},{6,7},{7,6},{8,9},{9,8},{10,11... | collective-permute-start | bytes 368648 | tf_op jit(solution)/shard_map/ppermute | solution.py:542
  88.3 0.8 copy-start.14
  89.0 0.7 copy-start.22
  89.7 0.7 copy-start.23
  91.8 0.7 copy-start.4
  91.8 0.7 copy-start.5
  92.5 0.6 copy-start.6
  97.1 3.0 %copy-start.11 = (f32[1,128,3]{2,1,0:T(8,128)S(1)}, f32[1,128,3]{2,1,0:T(8,128)}, u32[]{:S(2)}) copy-start(f32[1,128,3]{2,1,0:T(8,128)} %get-tuple-element.91) | copy-start | bytes 4612
  98.6 2.2 %copy-start.10 = (f32[1,128,3]{2,1,0:T(8,128)S(1)}, f32[1,128,3]{2,1,0:T(8,128)}, u32[]{:S(2)}) copy-start(f32[1,128,3]{2,1,0:T(8,128)} %get-tuple-element.92) | copy-start | bytes 4612
  100.1 6.7 %copy-start.9 = (f32[1,128,64]{2,1,0:T(8,128)S(1)}, f32[1,128,64]{2,1,0:T(8,128)}, u32[]{:S(2)}) copy-start(f32[1,128,64]{2,1,0:T(8,128)} %get-tuple-element.82) | copy-start | bytes 98308
  100.1 7.4 %copy-start.8 = (f32[1,128,64]{2,1,0:T(8,128)S(1)}, f32[1,128,64]{2,1,0:T(8,128)}, u32[]{:S(2)}) copy-start(f32[1,128,64]{2,1,0:T(8,128)} %get-tuple-element.83) | copy-start | bytes 98308
  100.7 8.3 %copy-start.2 = (f32[1,512,64]{2,1,0:T(8,128)S(1)}, f32[1,512,64]{2,1,0:T(8,128)}, u32[]{:S(2)}) copy-start(f32[1,512,64]{2,1,0:T(8,128)} %get-tuple-element.77) | copy-start | bytes 393220
  107.5 0.8 copy-start.7
where the time goes:
time: 111 us; the launch traced here: 110 us
  Pallas kernels  42.4 us (38%)
  starting transfers between devices  26.3 us (24%)
  local copies, waits for them, and re-layouts  23.1 us (21%)
  waiting for transfers between devices  14.5 us (13%)
  other arithmetic  2.49 us (2%)
    pallas_call x1, Pallas kernels, local(): pl.pallas_call(functools.partial(step_kernel, batches=batches, rows=rows,...  36.1 us
    unnamed x72, local copies, waits for them, and re-layouts  22.5 us
    ppermute x6, starting transfers between devices, local(): lax.ppermute(out, 'dp', xor_pairs(devices, k << start)).astype(F32)  9.6 us
    ppermute x6, waiting for transfers between devices, local(): lax.ppermute(out, 'dp', xor_pairs(devices, k << start)).astype(F32)  8.57 us
    ppermute x6, starting transfers between devices, local(): lax.ppermute(payload, 'dp', xor_pairs(devices, k << start))  7.99 us
    ppermute x1, starting transfers between devices, local(): near = lax.ppermute(near, both, same)  4.4 us
    pallas_call x1, Pallas kernels, local(): pl.pallas_call(functools.partial(update_kernel, stages=len(parts)), out_s...  3.95 us
    ppermute x6, waiting for transfers between devices, local(): lax.ppermute(payload, 'dp', xor_pairs(devices, k << start))  3.47 us
  transfers between devices with their start and end apart: 16, of which 10 were waited for; matrix products, arithmetic and copies ran while one was open for 4% of the time, Pallas kernels for 0%

commit v1 on v0

--- a/solution.py
+++ b/solution.py
@@ -1,5 +1,4 @@
 import functools
-import math
 
 import jax
 import jax.numpy as jnp
@@ -49,10 +48,10 @@
 
 
 def pack_kernel(
-    place, image, mask, codes, count, total, enc, lat, dec, read,
+    image, mask, codes, count, total, enc, lat, dec, read,
     tile, near, across, pack, code_rows, flat,
 ):
-    level = place[0]
+    level = lax.axis_index("level")
     batches, _, band, _ = image.shape
     for b in range(batches):
         base = b * band * 8
@@ -85,20 +84,19 @@
     pack[0:TAPS] = dec[0].astype(BF)
     flat[...] = jnp.zeros_like(flat)
     for t in range(9):
-        flat[8 * t : 8 * t + 3] = enc[0, 3 * t : 3 * t + 3]
+        for c in range(3):
+            flat[8 * t + c : 8 * t + c + 1] = enc[3 * t + c]
     pack[R_ET : R_ET + 128] = flat[...].T.astype(BF)
     flat[...] = jnp.zeros_like(flat)
-    flat[:, 0:64] = lat[0]
-    pack[R_ZN : R_ZN + 128] = flat[...].astype(BF)
-    pack[R_ZT : R_ZT + 64] = flat[...].T[0:64].astype(BF)
-    flat[...] = jnp.zeros_like(flat)
-    flat[:, 0:3] = read[0]
-    pack[R_OT : R_OT + 16] = flat[...].T[0:16].astype(BF)
+    flat[0:64] = lat[0]
+    pack[R_ZT : R_ZT + 64] = lat[0].astype(BF)
+    pack[R_ZN : R_ZN + 128] = flat[...].T.astype(BF)
+    blank = jnp.zeros((13, 128), F32)
+    pack[R_OT : R_OT + 16] = jnp.concatenate([read[0], read[1], read[2], blank], 0).astype(BF)
+    book = total[0] / count[...]
     for quarter in range(4):
-        flat[:, 0:64] = total[0, quarter * 128 : (quarter + 1) * 128]
-        book = flat[...].T[0:64] / count[0:1, quarter * 128 : (quarter + 1) * 128]
         row = R_BT + (quarter % 2) * 128 + (quarter // 2) * 64
-        pack[row : row + 64] = book.astype(BF)
+        pack[row : row + 64] = book[:, quarter * 128 : (quarter + 1) * 128].astype(BF)
     pack[R_CODE : R_CODE + batches * band] = code_rows[...].astype(BF)
 
 
@@ -129,14 +127,18 @@
 
 
 def step_kernel(
-    place, tile, near, across, mine, theirs,
+    tile, near, across, mine, theirs,
     keep_big, keep_small, send,
     t_s, far_s, dn, dt, et, zn, zt, ot, on, bt,
     u_s, p_s, h_s, slope_s, gap_s, da_s, g_d, g_o, g_e, g_z, g_s, l_s,
     *, batches, rows, step_e, step_d, step_b,
 ):
-    level, valid = place[0], place[1]
+    level, me, devices = lax.axis_index("level"), lax.axis_index("dp"), lax.axis_size("dp")
     band, ext = 2 * rows, rows + 4
+    above, below = (me + 1) * band, (me + 2) * band
+    top_ok = (lax.rem(above, CROP) != 0) & (me > 0)
+    bottom_ok = (lax.rem(below, CROP) != 0) & (me < devices - 1)
+    valid = jnp.where(level == 0, top_ok.astype(jnp.int32), bottom_ok.astype(jnp.int32))
     bottom = level == 1
 
     def pair(start, size):
@@ -370,16 +372,17 @@
 
 
 def update_kernel(
-    order, *refs, stages
+    *refs, stages, start
 ):
     (parts, refs) = refs[:stages], refs[stages:]
     (count, total, ew, e1, e2, zw, z1, z2, dw, d1, d2, ow, o1, o2,
      loss_out, valid_out, count_out, total_out,
-     em, es, ep, ec, zm, zs, zp, zc, dm, ds, dp, dc, om, os, op, oc, big, flat) = refs
+     em, es, ep, ec, zm, zs, zp, zc, dm, ds, dp, dc, om, os, op, oc, big, rows) = refs
     share = BIG // stages
+    index = (lax.axis_index("dp") >> start) & (stages - 1)
     small = jnp.zeros((SMALL, W), F32)
     for n, ref in enumerate(parts):
-        big[pl.ds(pl.multiple_of(order[n] * share, 16), share), :] = ref[0:share].astype(F32)
+        big[pl.ds(pl.multiple_of((index ^ n) * share, 16), share), :] = ref[0:share].astype(F32)
         small = small + ref[share : share + SMALL].astype(F32)
     exact = sum(small[S_X + EXACT * i : S_X + EXACT * (i + 1)] for i in range(3))
     loss = jnp.sum(exact[4:5, 0:1])
@@ -390,29 +393,35 @@
     count_out[...] = 0.99 * count[...] + 0.01 * counts
     for quarter in range(4):
         row = TAPS + (quarter % 2) * 128 + (quarter // 2) * 64
-        flat[0:64] = big[row : row + 64]
-        rows = slice(quarter * 128, (quarter + 1) * 128)
-        total_out[0, rows] = 0.99 * total[0, rows] + 0.01 * flat[...].T[:, 0:64]
+        cols = slice(quarter * 128, (quarter + 1) * 128)
+        total_out[0, :, cols] = 0.99 * total[0, :, cols] + 0.01 * big[row : row + 64]
 
     scale = 1.0 - 0.5**STEP
 
-    def adamw(grad, w, first, second, rate, outs):
+    def adamw(grad, weight, first, second, rate):
         grad = grad / valid
-        moment = 0.5 * first[0] + 0.5 * grad
-        square = 0.5 * second[0] + 0.5 * grad * grad
-        weight = w[0]
+        moment = 0.5 * first + 0.5 * grad
+        square = 0.5 * second + 0.5 * grad * grad
         master = weight - rate * (moment / scale / (jnp.sqrt(square / scale) + 1e-08) + 0.01 * weight)
-        outs[0][0] = moment
-        outs[1][0] = square
+        return moment, square, master
+
+    def whole(grad, w, first, second, rate, outs):
+        outs[0][0], outs[1][0], master = adamw(grad, w[0], first[0], second[0], rate)
         outs[2][0] = master
         outs[3][0] = master.astype(BF)
 
-    adamw(small[S_E : S_E + 27], ew, e1, e2, RATES[0], (em, es, ep, ec))
-    flat[0:64] = small[S_Z : S_Z + 64]
-    adamw(flat[...].T[:, 0:64], zw, z1, z2, RATES[1], (zm, zs, zp, zc))
-    adamw(big[0:TAPS], dw, d1, d2, RATES[2], (dm, ds, dp, dc))
-    flat[0:16] = small[S_O : S_O + 16]
-    adamw(flat[...].T[:, 0:3], ow, o1, o2, RATES[3], (om, os, op, oc))
+    def by_row(grad, w, first, second, rate, outs):
+        n = w.shape[0]
+        for i in range(n):
+            outs[0][i], outs[1][i], master = adamw(grad[i : i + 1], w[i], first[i], second[i], rate)
+            outs[2][i] = master
+            rows[i : i + 1] = master
+        outs[3][0] = rows[0:n].astype(BF)
+
+    by_row(small[S_E : S_E + 27], ew, e1, e2, RATES[0], (em, es, ep, ec))
+    whole(small[S_Z : S_Z + 64], zw, z1, z2, RATES[1], (zm, zs, zp, zc))
+    whole(big[0:TAPS], dw, d1, d2, RATES[2], (dm, ds, dp, dc))
+    by_row(small[S_O : S_O + 3], ow, o1, o2, RATES[3], (om, os, op, oc))
 
 
 def radices(devices):
@@ -451,13 +460,17 @@
 ):
     batches, _, band, width = image.shape
     rows = band // 2
-    level, me = lax.axis_index("level"), lax.axis_index("dp")
-    devices = lax.axis_size("dp")
-    row_first = me * band + band
-    top_ok = (row_first % CROP != 0) & (me > 0)
-    bottom_ok = ((row_first + band) % CROP != 0) & (me < devices - 1)
-    valid = jnp.where(level == 0, top_ok, bottom_ok)
-    place = jnp.stack([level, valid.astype(jnp.int32)]).astype(jnp.int32)
+    me, devices = lax.axis_index("dp"), lax.axis_size("dp")
+    ema_sum = jnp.swapaxes(ema_sum, 1, 2)
+    encoder_weight, encoder_first, encoder_second = (
+        jnp.swapaxes(item, 0, 1) for item in (encoder_weight, encoder_first, encoder_second)
+    )
+    latent_weight, latent_first, latent_second = (
+        jnp.swapaxes(item, 1, 2) for item in (latent_weight, latent_first, latent_second)
+    )
+    readout_weight, readout_first, readout_second = (
+        jnp.transpose(item, (2, 0, 1)) for item in (readout_weight, readout_first, readout_second)
+    )
 
     limit = pltpu.CompilerParams(vmem_limit_bytes=56 * 1024 * 1024)
     packed = R_CODE + batches * band
@@ -469,11 +482,11 @@
             jax.ShapeDtypeStruct((16, W), BF),
             jax.ShapeDtypeStruct((packed, W), BF),
         ],
-        in_specs=[SMEM] + [VMEM] * 9,
+        in_specs=[VMEM] * 9,
         out_specs=[VMEM] * 4,
         scratch_shapes=[pltpu.VMEM((batches * band, W), F32), pltpu.VMEM((128, 128), F32)],
         compiler_params=limit,
-    )(place, image, mask, codes, ema_count, ema_sum, encoder_weight, latent_weight, decoder_weight, readout_weight)
+    )(image, mask, codes, ema_count, ema_sum, encoder_weight, latent_weight, decoder_weight, readout_weight)
 
     both = ("level", "dp")
     same = [(d - 1, d) for d in range(1, devices)] + [(devices + d + 1, devices + d) for d in range(devices - 1)]
@@ -491,7 +504,7 @@
             jax.ShapeDtypeStruct((SMALL, W), BF),
             jax.ShapeDtypeStruct((BIG + SMALL, W), BF),
         ],
-        in_specs=[SMEM] + [VMEM] * 5,
+        in_specs=[VMEM] * 5,
         out_specs=[VMEM] * 3,
         scratch_shapes=[
             pltpu.VMEM((batches, ext, 8, W), F32),
@@ -518,7 +531,7 @@
             pltpu.VMEM((144, 256), F32),
         ],
         compiler_params=limit,
-    )(place, tile, near, across, pack, theirs)
+    )(tile, near, across, pack, theirs)
 
     got = lax.ppermute(send, "level", [(0, 1), (1, 0)])
     small = sum_small([keep_small, got[BIG:]])
@@ -540,7 +553,6 @@
         index = (me >> start) & (count - 1)
         payload = jnp.concatenate([big, small], 0)
         parts = [payload] + [lax.ppermute(payload, "dp", xor_pairs(devices, k << start)) for k in range(1, count)]
-        order = jnp.stack([index ^ k for k in range(count)]).astype(jnp.int32)
         if number == len(stages) - 1:
             break
         size = big.shape[0]
@@ -558,16 +570,22 @@
     outs = [jax.ShapeDtypeStruct((1, 1), F32)] * 2
     outs += [jax.ShapeDtypeStruct(ema_count.shape, F32), jax.ShapeDtypeStruct(ema_sum.shape, F32)]
     for item in (encoder_weight, latent_weight, decoder_weight, readout_weight):
-        outs += [jax.ShapeDtypeStruct(item.shape, F32)] * 3 + [jax.ShapeDtypeStruct(item.shape, BF)]
+        copy = item.shape if item.shape[0] == 1 else (1, item.shape[0], item.shape[2])
+        outs += [jax.ShapeDtypeStruct(item.shape, F32)] * 3 + [jax.ShapeDtypeStruct(copy, BF)]
     result = pl.pallas_call(
-        functools.partial(update_kernel, stages=len(parts)),
+        functools.partial(update_kernel, stages=len(parts), start=start),
         out_shape=outs,
-        in_specs=[SMEM] + [VMEM] * (len(parts) + len(state)),
+        in_specs=[VMEM] * (len(parts) + len(state)),
         out_specs=[SMEM] * 2 + [VMEM] * (len(outs) - 2),
-        scratch_shapes=[pltpu.VMEM((BIG, W), F32), pltpu.VMEM((128, 128), F32)],
-        compiler_params=limit,
-    )(order, *parts, *state)
-    return (result[0].reshape(()), result[1].reshape(()), *result[2:])
+        scratch_shapes=[pltpu.VMEM((BIG, W), F32), pltpu.VMEM((32, W), F32)],
+        compiler_params=pltpu.CompilerParams(vmem_limit_bytes=24 * 1024 * 1024),
+    )(*parts, *state)
+    loss, valid, count_new, total_new = result[:4]
+    enc, lat, dec, read = (list(result[4 * n : 4 * n + 4]) for n in range(1, 5))
+    enc[:3] = [jnp.swapaxes(item, 0, 1) for item in enc[:3]]
+    lat = [jnp.swapaxes(item, 1, 2) for item in lat]
+    read = [jnp.transpose(item, (1, 2, 0)) for item in read[:3]] + [jnp.swapaxes(read[3], 1, 2)]
+    return (loss.reshape(()), valid.reshape(()), count_new, jnp.swapaxes(total_new, 1, 2), *enc, *lat, *dec, *read)
 
 
 def solution(mesh):

time: 111 us -> 89 us (0.80)
  local copies, waits for them, and re-layouts: 23.1 us -> 2.01 us
  waiting for transfers between devices: 14.5 us -> 17.6 us
  Pallas kernels: 42.4 us -> 40.5 us
  other arithmetic: 2.49 us -> 1.32 us
    unnamed x72 -> x38, local copies, waits for them, and re-layouts: 22.5 us -> 1.42 us
    ppermute x6, waiting for transfers between devices: 3.47 us -> 6.67 us  [local(): lax.ppermute(payload, 'dp', xor_pairs(devices, k << start))]
    pallas_call x1, Pallas kernels: 3.95 us -> 2.07 us  [local(): pl.pallas_call(functools.partial(update_kernel, stages=len(parts), start=...]
    another operation x7 -> x5, other arithmetic: 1.23 us -> 0.06 us  [the longest x1 0.59 us: local(): order = jnp.stack([index ^ k for k in range(count)]).astype(jnp.int32)]
  transfers between devices with their start and end apart: 16 -> 16, of which waited for: 10 -> 12; matrix products, arithmetic and copies ran while one was open for 4% -> 0% of each run, Pallas kernels for 0% -> 0%
where the time goes in v1:
time: 89 us; the launch traced here: 88.7 us
  Pallas kernels  40.5 us (46%)
  starting transfers between devices  26.3 us (30%)
  waiting for transfers between devices  17.6 us (20%)
  local copies, waits for them, and re-layouts  2.01 us (2%)
  other arithmetic  1.32 us (1%)
  between operations  0.98 us (1%)
    pallas_call x1, Pallas kernels, local(): pl.pallas_call(functools.partial(step_kernel, batches=batches, rows=rows,...  36.2 us
    ppermute x6, starting transfers between devices, local(): lax.ppermute(out, 'dp', xor_pairs(devices, k << start)).astype(F32)  9.58 us
    ppermute x6, waiting for transfers between devices, local(): lax.ppermute(out, 'dp', xor_pairs(devices, k << start)).astype(F32)  8.52 us
    ppermute x6, starting transfers between devices, local(): lax.ppermute(payload, 'dp', xor_pairs(devices, k << start))  7.98 us
    ppermute x6, waiting for transfers between devices, local(): lax.ppermute(payload, 'dp', xor_pairs(devices, k << start))  6.67 us
    ppermute x1, starting transfers between devices, local(): near = lax.ppermute(near, both, same)  4.39 us
    ppermute x1, starting transfers between devices, local(): got = lax.ppermute(send, 'level', [(0, 1), (1, 0)])  3.23 us
    pallas_call x1, Pallas kernels, local(): pl.pallas_call(pack_kernel, out_shape=[jax.ShapeDtypeStruct((batches * ba...  2.2 us
  transfers between devices with their start and end apart: 16, of which 12 were waited for; matrix products, arithmetic and copies ran while one was open for 0% of the time, Pallas kernels for 0%

profile of v1, /device:TPU:0, one launch (start us, length us, event | category | flops | bytes accessed | tf_op | source)
XLA Modules:
  0.0 88.7 jit_solution(7760728278251775633)
XLA Ops:
  0.7 2.2 %shard_map.320 = (f32[768,128]{1,0:T(8,128)}, bf16[48,128]{1,0:T(8,128)(2,1)}, bf16[16,128]{1,0:T(8,128)(2,1)}, bf16[1840,128]{1,0:T(8,128)(2,1)}) custom-call(bf16[3,3,32,128]{3,2,1,0:T(8,128)(2,1)} %image.1, s32[3,32,128]{2,1,0:T(8,128)} %mask.1, s32[1,3,32,128]{3,2,1,0:T(8,128)} %codes.1, f32[1,512]{1,0:T(1,128)} %refs_4_.1, f32[1,64,512]{2,1,0:T(8,128)} %bitcast.68, ...), custom_call_target="tpu_custom_call" | custom-call | tf_op jit(solution)/shard_map/pallas_call | solution.py:477
  2.9 0.5 collective-permute-start.2
  3.3 4.4 %collective-permute-start = (bf16[48,128]{1,0:T(8,128)(2,1)}, bf16[48,128]{1,0:T(8,128)(2,1)S(1)}, u32[]{:S(2)}, u32[]{:S(2)}) collective-permute-start(bf16[48,128]{1,0:T(8,128)(2,1)} %get-tuple-element.48), channel_id=1, source_target_pairs={{0,1},{1,2},{2,3},{3,4},{4,5},{5,6},{6,7},{7,8},{8,9},{9,10},{10,1... | collective-permute-start | bytes 36872 | tf_op jit(solution)/shard_map/ppermute | solution.py:494
  7.7 0.7 collective-permute-start.1
  8.4 0.0 copy-start.17
  8.4 0.9 %collective-permute-done.near = bf16[48,128]{1,0:T(8,128)(2,1)S(1)} collective-permute-done((bf16[48,128]{1,0:T(8,128)(2,1)}, bf16[48,128]{1,0:T(8,128)(2,1)S(1)}, u32[]{:S(2)}, u32[]{:S(2)}) %collective-permute-start) | collective-permute-done | bytes 12320 | tf_op jit(solution)/shard_map/ppermute | solution.py:494
  9.3 0.6 copy-done.16
  9.9 0.2 copy-done.14
  10.1 36.2 %shard_map.321 = (f32[1408,128]{1,0:T(8,128)}, bf16[128,128]{1,0:T(8,128)(2,1)}, bf16[1536,128]{1,0:T(8,128)(2,1)}) custom-call(f32[768,128]{1,0:T(8,128)} %get-tuple-element.47.tile, bf16[48,128]{1,0:T(8,128)(2,1)} %copy-done.16, bf16[16,128]{1,0:T(8,128)(2,1)} %copy-done.17, bf16[1840,128]{1,0:T(8,128)(2,1)} %get-tuple-element.50.mine, ...), custom_call_target="tpu_custom_call" | custom-call | tf_op jit(solution)/shard_map/pallas_call | solution.py:500
  46.3 3.2 %collective-permute-start.3 = (bf16[1536,128]{1,0:T(8,128)(2,1)}, bf16[1536,128]{1,0:T(8,128)(2,1)S(1)}, u32[]{:S(2)}, u32[]{:S(2)}) collective-permute-start(bf16[1536,128]{1,0:T(8,128)(2,1)} %get-tuple-element.52), channel_id=1, source_target_pairs={{0,16},{16,0},{1,17},{17,1},{2,18},{18,2},{3,19},{19,3},{4,20},{20... | collective-permute-start | bytes 1179656 | tf_op jit(solution)/shard_map/ppermute | solution.py:536
  49.5 1.6 %collective-permute-done.3 = bf16[1536,128]{1,0:T(8,128)(2,1)S(1)} collective-permute-done((bf16[1536,128]{1,0:T(8,128)(2,1)}, bf16[1536,128]{1,0:T(8,128)(2,1)S(1)}, u32[]{:S(2)}, u32[]{:S(2)}) %collective-permute-start.3) | collective-permute-done | bytes 393248 | tf_op jit(solution)/shard_map/ppermute | solution.py:536
  51.1 1.2 %convert_add_fusion = f32[1408,128]{1,0:T(8,128)S(1)} fusion(f32[1408,128]{1,0:T(8,128)} %get-tuple-element.51, bf16[1536,128]{1,0:T(8,128)(2,1)S(1)} %collective-permute-done.3), kind=kLoop, calls=%fused_computation | loop fusion | flops 360448 | bytes 1802240 | tf_op jit(solution)/shard_map/add | solution.py:538
  52.3 0.0 copy-start.15
  52.3 3.7 %collective-permute-start.4 = (bf16[352,128]{1,0:T(8,128)(2,1)S(1)}, bf16[352,128]{1,0:T(8,128)(2,1)S(1)}, u32[]{:S(2)}, u32[]{:S(2)}) collective-permute-start(bf16[352,128]{1,0:T(8,128)(2,1)S(1)} %get-tuple-element.82), channel_id=1, source_target_pairs={{0,3},{1,2},{2,1},{3,0},{4,7},{5,6},{6,5},{7,4},{8,11},{9,10},{10,... | collective-permute-start | bytes 270344 | tf_op jit(solution)/shard_map/ppermute | solution.py:548
  56.0 0.7 collective-permute-start.6
  56.8 0.0 copy-start.13
  56.8 2.7 %collective-permute-done.4 = bf16[352,128]{1,0:T(8,128)(2,1)S(1)} collective-permute-done((bf16[352,128]{1,0:T(8,128)(2,1)S(1)}, bf16[352,128]{1,0:T(8,128)(2,1)S(1)}, u32[]{:S(2)}, u32[]{:S(2)}) %collective-permute-start.4) | collective-permute-done | bytes 90144 | tf_op jit(solution)/shard_map/ppermute | solution.py:548
  59.5 1.8 %collective-permute-done.6 = bf16[352,128]{1,0:T(8,128)(2,1)S(1)} collective-permute-done((bf16[352,128]{1,0:T(8,128)(2,1)S(1)}, bf16[352,128]{1,0:T(8,128)(2,1)S(1)}, u32[]{:S(2)}, u32[]{:S(2)}) %collective-permute-start.6) | collective-permute-done | bytes 90144 | tf_op jit(solution)/shard_map/ppermute | solution.py:548
  61.3 0.0 collective-permute-done.5
  61.4 0.0 copy-start.3
  61.4 0.0 copy-start.8
  61.5 4.5 %collective-permute-start.7 = (bf16[88,128]{1,0:T(8,128)(2,1)S(1)}, bf16[88,128]{1,0:T(8,128)(2,1)S(1)}, u32[]{:S(2)}, u32[]{:S(2)}) collective-permute-start(bf16[88,128]{1,0:T(8,128)(2,1)S(1)} %get-tuple-element.87), channel_id=1, source_target_pairs={{0,12},{1,13},{2,14},{3,15},{4,8},{5,9},{6,10},{7,11},{8,4},{9,5},... | collective-permute-start | bytes 67592 | tf_op jit(solution)/shard_map/ppermute | solution.py:548
  66.0 0.0 collective-permute-start.9
  66.0 0.6 collective-permute-start.8
  66.6 0.0 copy-start.1
  66.6 0.0 copy-start
  66.7 1.1 %collective-permute-done.7 = bf16[88,128]{1,0:T(8,128)(2,1)S(1)} collective-permute-done((bf16[88,128]{1,0:T(8,128)(2,1)S(1)}, bf16[88,128]{1,0:T(8,128)(2,1)S(1)}, u32[]{:S(2)}, u32[]{:S(2)}) %collective-permute-start.7) | collective-permute-done | bytes 22560 | tf_op jit(solution)/shard_map/ppermute | solution.py:548
  67.7 2.0 %collective-permute-done.9 = bf16[88,128]{1,0:T(8,128)(2,1)S(1)} collective-permute-done((bf16[88,128]{1,0:T(8,128)(2,1)S(1)}, bf16[88,128]{1,0:T(8,128)(2,1)S(1)}, u32[]{:S(2)}, u32[]{:S(2)}) %collective-permute-start.9) | collective-permute-done | bytes 22560 | tf_op jit(solution)/shard_map/ppermute | solution.py:548
  69.8 0.9 %collective-permute-done.8 = bf16[88,128]{1,0:T(8,128)(2,1)S(1)} collective-permute-done((bf16[88,128]{1,0:T(8,128)(2,1)S(1)}, bf16[88,128]{1,0:T(8,128)(2,1)S(1)}, u32[]{:S(2)}, u32[]{:S(2)}) %collective-permute-start.8) | collective-permute-done | bytes 22560 | tf_op jit(solution)/shard_map/ppermute | solution.py:548
  70.7 0.1 concatenate.14
  70.9 1.8 %collective-permute-start.12 = (bf16[216,128]{1,0:T(8,128)(2,1)S(1)}, bf16[216,128]{1,0:T(8,128)(2,1)S(1)}, u32[]{:S(2)}, u32[]{:S(2)}) collective-permute-start(bf16[216,128]{1,0:T(8,128)(2,1)S(1)} %concatenate.14), channel_id=1, source_target_pairs={{0,12},{1,13},{2,14},{3,15},{4,8},{5,9},{6,10},{7,11},{8,4},{9,5},... | collective-permute-start | bytes 165896 | tf_op jit(solution)/shard_map/ppermute | solution.py:555
  72.6 1.8 %collective-permute-start.11 = (bf16[216,128]{1,0:T(8,128)(2,1)S(1)}, bf16[216,128]{1,0:T(8,128)(2,1)S(1)}, u32[]{:S(2)}, u32[]{:S(2)}) collective-permute-start(bf16[216,128]{1,0:T(8,128)(2,1)S(1)} %concatenate.14), channel_id=1, source_target_pairs={{0,8},{1,9},{2,10},{3,11},{4,12},{5,13},{6,14},{7,15},{8,0},{9,1},... | collective-permute-start | bytes 165896 | tf_op jit(solution)/shard_map/ppermute | solution.py:555
  74.4 0.9 %collective-permute-start.10 = (bf16[216,128]{1,0:T(8,128)(2,1)S(1)}, bf16[216,128]{1,0:T(8,128)(2,1)S(1)}, u32[]{:S(2)}, u32[]{:S(2)}) collective-permute-start(bf16[216,128]{1,0:T(8,128)(2,1)S(1)} %concatenate.14), channel_id=1, source_target_pairs={{0,4},{1,5},{2,6},{3,7},{4,0},{5,1},{6,2},{7,3},{8,12},{9,13},{10,... | collective-permute-start | bytes 165896 | tf_op jit(solution)/shard_map/ppermute | solution.py:555
  75.3 0.1 concatenate.15
  75.4 1.5 %collective-permute-done.12 = bf16[216,128]{1,0:T(8,128)(2,1)S(1)} collective-permute-done((bf16[216,128]{1,0:T(8,128)(2,1)S(1)}, bf16[216,128]{1,0:T(8,128)(2,1)S(1)}, u32[]{:S(2)}, u32[]{:S(2)}) %collective-permute-start.12) | collective-permute-done | bytes 55328 | tf_op jit(solution)/shard_map/ppermute | solution.py:555
  77.0 1.4 %collective-permute-done.11 = bf16[216,128]{1,0:T(8,128)(2,1)S(1)} collective-permute-done((bf16[216,128]{1,0:T(8,128)(2,1)S(1)}, bf16[216,128]{1,0:T(8,128)(2,1)S(1)}, u32[]{:S(2)}, u32[]{:S(2)}) %collective-permute-start.11) | collective-permute-done | bytes 55328 | tf_op jit(solution)/shard_map/ppermute | solution.py:555
  78.3 0.6 collective-permute-done.10
  79.0 0.0 copy-start.4
  79.1 0.2 concatenate.16.refs_0_
  79.2 0.6 collective-permute-start.15
  79.8 0.9 collective-permute-start.14
  80.6 2.1 %collective-permute-start.13 = (bf16[480,128]{1,0:T(8,128)(2,1)S(1)}, bf16[480,128]{1,0:T(8,128)(2,1)S(1)}, u32[]{:S(2)}, u32[]{:S(2)}) collective-permute-start(bf16[480,128]{1,0:T(8,128)(2,1)S(1)} %concatenate.16.refs_0_), channel_id=1, source_target_pairs={{0,1},{1,0},{2,3},{3,2},{4,5},{5,4},{6,7},{7,6},{8,9},{9,8},{10,11... | collective-permute-start | bytes 368648 | tf_op jit(solution)/shard_map/ppermute | solution.py:555
  82.8 2.4 %collective-permute-done.15.refs_3_ = bf16[480,128]{1,0:T(8,128)(2,1)S(1)} collective-permute-done((bf16[480,128]{1,0:T(8,128)(2,1)S(1)}, bf16[480,128]{1,0:T(8,128)(2,1)S(1)}, u32[]{:S(2)}, u32[]{:S(2)}) %collective-permute-start.15) | collective-permute-done | bytes 122912 | tf_op jit(solution)/shard_map/ppermute | solution.py:555
  85.2 0.8 collective-permute-done.14.refs_2_
  86.0 0.0 collective-permute-done.13.refs_1_
  86.1 0.6 copy-done.10
  86.7 0.0 copy-done.11
  86.7 2.1 %shard_map.322 = (f32[1,1]{1,0:T(1,128)}, f32[1,1]{1,0:T(1,128)}, f32[1,512]{1,0:T(1,128)}, f32[1,64,512]{2,1,0:T(8,128)}, f32[27,1,128]{2,1,0:T(1,128)}, /*inde...) custom-call(bf16[480,128]{1,0:T(8,128)(2,1)S(1)} %concatenate.16.ref, ...), custom_call_target="tpu_custom_call" | custom-call | tf_op jit(solution)/shard_map/pallas_call | solution.py:575
  (47 shorter events, 0.4 us)
Async XLA Ops:
  2.9 4.9 %copy-start.18 = (bf16[16,128]{1,0:T(8,128)(2,1)S(1)}, bf16[16,128]{1,0:T(8,128)(2,1)}, u32[]{:S(2)}) copy-start(bf16[16,128]{1,0:T(8,128)(2,1)} %get-tuple-element.49) | copy-start | bytes 12292
  2.9 6.5 %collective-permute-start.2 = (bf16[1840,128]{1,0:T(8,128)(2,1)}, bf16[1840,128]{1,0:T(8,128)(2,1)S(1)}, u32[]{:S(2)}, u32[]{:S(2)}) collective-permute-start(bf16[1840,128]{1,0:T(8,128)(2,1)} %get-tuple-element.50.mine), channel_id=1, source_target_pairs={{0,16},{16,0},{1,17},{17,1},{2,18},{18,2},{3,19},{19,3},{4,20},{20... | collective-permute-start | bytes 1413128 | tf_op jit(solution)/shard_map/ppermute | solution.py:496
  3.3 6.0 %collective-permute-start = (bf16[48,128]{1,0:T(8,128)(2,1)}, bf16[48,128]{1,0:T(8,128)(2,1)S(1)}, u32[]{:S(2)}, u32[]{:S(2)}) collective-permute-start(bf16[48,128]{1,0:T(8,128)(2,1)} %get-tuple-element.48), channel_id=1, source_target_pairs={{0,1},{1,2},{2,3},{3,4},{4,5},{5,6},{6,7},{7,8},{8,9},{9,10},{10,1... | collective-permute-start | bytes 36872 | tf_op jit(solution)/shard_map/ppermute | solution.py:494
  7.7 0.7 collective-permute-start.1
  8.4 0.9 %copy-start.17 = (bf16[16,128]{1,0:T(8,128)(2,1)}, bf16[16,128]{1,0:T(8,128)(2,1)S(1)}, u32[]{:S(2)}) copy-start(bf16[16,128]{1,0:T(8,128)(2,1)S(1)} %collective-permute-done.1.across) | copy-start | bytes 12292
  9.3 0.6 copy-start.16
  9.3 0.8 copy-start.14
  46.3 4.8 %collective-permute-start.3 = (bf16[1536,128]{1,0:T(8,128)(2,1)}, bf16[1536,128]{1,0:T(8,128)(2,1)S(1)}, u32[]{:S(2)}, u32[]{:S(2)}) collective-permute-start(bf16[1536,128]{1,0:T(8,128)(2,1)} %get-tuple-element.52), channel_id=1, source_target_pairs={{0,16},{16,0},{1,17},{17,1},{2,18},{18,2},{3,19},{19,3},{4,20},{20... | collective-permute-start | bytes 1179656 | tf_op jit(solution)/shard_map/ppermute | solution.py:536
  52.3 4.5 %copy-start.15 = (bf16[128,128]{1,0:T(8,128)(2,1)S(1)}, bf16[128,128]{1,0:T(8,128)(2,1)}, u32[]{:S(2)}) copy-start(bf16[128,128]{1,0:T(8,128)(2,1)} %get-tuple-element.53) | copy-start | bytes 98308
  52.3 7.2 %collective-permute-start.4 = (bf16[352,128]{1,0:T(8,128)(2,1)S(1)}, bf16[352,128]{1,0:T(8,128)(2,1)S(1)}, u32[]{:S(2)}, u32[]{:S(2)}) collective-permute-start(bf16[352,128]{1,0:T(8,128)(2,1)S(1)} %get-tuple-element.82), channel_id=1, source_target_pairs={{0,3},{1,2},{2,1},{3,0},{4,7},{5,6},{6,5},{7,4},{8,11},{9,10},{10,... | collective-permute-start | bytes 270344 | tf_op jit(solution)/shard_map/ppermute | solution.py:548
  56.0 5.3 %collective-permute-start.6 = (bf16[352,128]{1,0:T(8,128)(2,1)S(1)}, bf16[352,128]{1,0:T(8,128)(2,1)S(1)}, u32[]{:S(2)}, u32[]{:S(2)}) collective-permute-start(bf16[352,128]{1,0:T(8,128)(2,1)S(1)} %get-tuple-element.83), channel_id=1, source_target_pairs={{0,1},{1,0},{2,3},{3,2},{4,5},{5,4},{6,7},{7,6},{8,9},{9,8},{10,11... | collective-permute-start | bytes 270344 | tf_op jit(solution)/shard_map/ppermute | solution.py:548
  56.8 4.6 %collective-permute-start.5 = (bf16[352,128]{1,0:T(8,128)(2,1)S(1)}, bf16[352,128]{1,0:T(8,128)(2,1)S(1)}, u32[]{:S(2)}, u32[]{:S(2)}) collective-permute-start(bf16[352,128]{1,0:T(8,128)(2,1)S(1)} %get-tuple-element.84), channel_id=1, source_target_pairs={{0,2},{1,3},{2,0},{3,1},{4,6},{5,7},{6,4},{7,5},{8,10},{9,11},{10,... | collective-permute-start | bytes 270344 | tf_op jit(solution)/shard_map/ppermute | solution.py:548
  56.8 29.2 %copy-start.7 = (f32[1,128,64]{1,2,0:T(8,128)S(1)}, f32[1,128,64]{1,2,0:T(8,128)}, u32[]{:S(2)}) copy-start(f32[1,128,64]{1,2,0:T(8,128)} %param.27) | copy-start | bytes 98308
  56.8 29.2 %copy-start.12 = (f32[1,128,3]{1,0,2:T(1,128)S(1)}, f32[1,128,3]{1,0,2:T(1,128)}, u32[]{:S(2)}) copy-start(f32[1,128,3]{1,0,2:T(1,128)} %param.32) | copy-start | bytes 4612
  56.8 29.2 %copy-start.13 = (f32[1,128,3]{1,0,2:T(1,128)S(1)}, f32[1,128,3]{1,0,2:T(1,128)}, u32[]{:S(2)}) copy-start(f32[1,128,3]{1,0,2:T(1,128)} %param.33) | copy-start | bytes 4612
  61.4 24.6 %copy-start.2 = (f32[1,1152,128]{2,1,0:T(8,128)S(1)}, f32[1,1152,128]{2,1,0:T(8,128)}, u32[]{:S(2)}) copy-start(f32[1,1152,128]{2,1,0:T(8,128)} %refs_14_.1) | copy-start | bytes 1769476
  61.4 24.7 %copy-start.6 = (f32[1,128,64]{1,2,0:T(8,128)S(1)}, f32[1,128,64]{1,2,0:T(8,128)}, u32[]{:S(2)}) copy-start(f32[1,128,64]{1,2,0:T(8,128)} %param.26) | copy-start | bytes 98308
  61.4 24.7 %copy-start.9 = (f32[1,27,128]{2,0,1:T(1,128)S(1)}, f32[1,27,128]{2,0,1:T(1,128)}, u32[]{:S(2)}) copy-start(f32[1,27,128]{2,0,1:T(1,128)} %param.24) | copy-start | bytes 41476
  61.4 24.6 %copy-start.3 = (f32[1,512,64]{1,2,0:T(8,128)S(1)}, f32[1,512,64]{1,2,0:T(8,128)}, u32[]{:S(2)}) copy-start(f32[1,512,64]{1,2,0:T(8,128)} %param.21) | copy-start | bytes 393220
  61.4 24.6 %copy-start.8 = (f32[1,27,128]{2,0,1:T(1,128)S(1)}, f32[1,27,128]{2,0,1:T(1,128)}, u32[]{:S(2)}) copy-start(f32[1,27,128]{2,0,1:T(1,128)} %param.23) | copy-start | bytes 41476
  61.5 6.3 %collective-permute-start.7 = (bf16[88,128]{1,0:T(8,128)(2,1)S(1)}, bf16[88,128]{1,0:T(8,128)(2,1)S(1)}, u32[]{:S(2)}, u32[]{:S(2)}) collective-permute-start(bf16[88,128]{1,0:T(8,128)(2,1)S(1)} %get-tuple-element.87), channel_id=1, source_target_pairs={{0,12},{1,13},{2,14},{3,15},{4,8},{5,9},{6,10},{7,11},{8,4},{9,5},... | collective-permute-start | bytes 67592 | tf_op jit(solution)/shard_map/ppermute | solution.py:548
  66.0 3.8 %collective-permute-start.9 = (bf16[88,128]{1,0:T(8,128)(2,1)S(1)}, bf16[88,128]{1,0:T(8,128)(2,1)S(1)}, u32[]{:S(2)}, u32[]{:S(2)}) collective-permute-start(bf16[88,128]{1,0:T(8,128)(2,1)S(1)} %get-tuple-element.88), channel_id=1, source_target_pairs={{0,4},{1,5},{2,6},{3,7},{4,0},{5,1},{6,2},{7,3},{8,12},{9,13},{10,... | collective-permute-start | bytes 67592 | tf_op jit(solution)/shard_map/ppermute | solution.py:548
  66.0 4.7 %collective-permute-start.8 = (bf16[88,128]{1,0:T(8,128)(2,1)S(1)}, bf16[88,128]{1,0:T(8,128)(2,1)S(1)}, u32[]{:S(2)}, u32[]{:S(2)}) collective-permute-start(bf16[88,128]{1,0:T(8,128)(2,1)S(1)} %get-tuple-element.89), channel_id=1, source_target_pairs={{0,8},{1,9},{2,10},{3,11},{4,12},{5,13},{6,14},{7,15},{8,0},{9,1},... | collective-permute-start | bytes 67592 | tf_op jit(solution)/shard_map/ppermute | solution.py:548
  66.6 19.4 %copy-start.5 = (f32[1,27,128]{2,0,1:T(1,128)S(1)}, f32[1,27,128]{2,0,1:T(1,128)}, u32[]{:S(2)}) copy-start(f32[1,27,128]{2,0,1:T(1,128)} %param.22) | copy-start | bytes 41476
  66.6 19.4 %copy-start.1 = (f32[1,1152,128]{2,1,0:T(8,128)S(1)}, f32[1,1152,128]{2,1,0:T(8,128)}, u32[]{:S(2)}) copy-start(f32[1,1152,128]{2,1,0:T(8,128)} %refs_13_.1) | copy-start | bytes 1769476
  66.6 19.4 %copy-start = (f32[1,1152,128]{2,1,0:T(8,128)S(1)}, f32[1,1152,128]{2,1,0:T(8,128)}, u32[]{:S(2)}) copy-start(f32[1,1152,128]{2,1,0:T(8,128)} %refs_12_.1) | copy-start | bytes 1769476
  70.9 6.1 %collective-permute-start.12 = (bf16[216,128]{1,0:T(8,128)(2,1)S(1)}, bf16[216,128]{1,0:T(8,128)(2,1)S(1)}, u32[]{:S(2)}, u32[]{:S(2)}) collective-permute-start(bf16[216,128]{1,0:T(8,128)(2,1)S(1)} %concatenate.14), channel_id=1, source_target_pairs={{0,12},{1,13},{2,14},{3,15},{4,8},{5,9},{6,10},{7,11},{8,4},{9,5},... | collective-permute-start | bytes 165896 | tf_op jit(solution)/shard_map/ppermute | solution.py:555
  72.6 5.7 %collective-permute-start.11 = (bf16[216,128]{1,0:T(8,128)(2,1)S(1)}, bf16[216,128]{1,0:T(8,128)(2,1)S(1)}, u32[]{:S(2)}, u32[]{:S(2)}) collective-permute-start(bf16[216,128]{1,0:T(8,128)(2,1)S(1)} %concatenate.14), channel_id=1, source_target_pairs={{0,8},{1,9},{2,10},{3,11},{4,12},{5,13},{6,14},{7,15},{8,0},{9,1},... | collective-permute-start | bytes 165896 | tf_op jit(solution)/shard_map/ppermute | solution.py:555
  74.4 4.5 %collective-permute-start.10 = (bf16[216,128]{1,0:T(8,128)(2,1)S(1)}, bf16[216,128]{1,0:T(8,128)(2,1)S(1)}, u32[]{:S(2)}, u32[]{:S(2)}) collective-permute-start(bf16[216,128]{1,0:T(8,128)(2,1)S(1)} %concatenate.14), channel_id=1, source_target_pairs={{0,4},{1,5},{2,6},{3,7},{4,0},{5,1},{6,2},{7,3},{8,12},{9,13},{10,... | collective-permute-start | bytes 165896 | tf_op jit(solution)/shard_map/ppermute | solution.py:555
  79.0 7.0 %copy-start.4 = (f32[1,128,64]{1,2,0:T(8,128)S(1)}, f32[1,128,64]{1,2,0:T(8,128)}, u32[]{:S(2)}) copy-start(f32[1,128,64]{1,2,0:T(8,128)} %param.25) | copy-start | bytes 98308
  79.2 5.9 %collective-permute-start.15 = (bf16[480,128]{1,0:T(8,128)(2,1)S(1)}, bf16[480,128]{1,0:T(8,128)(2,1)S(1)}, u32[]{:S(2)}, u32[]{:S(2)}) collective-permute-start(bf16[480,128]{1,0:T(8,128)(2,1)S(1)} %concatenate.16.refs_0_), channel_id=1, source_target_pairs={{0,3},{1,2},{2,1},{3,0},{4,7},{5,6},{6,5},{7,4},{8,11},{9,10},{10,... | collective-permute-start | bytes 368648 | tf_op jit(solution)/shard_map/ppermute | solution.py:555
  79.8 6.2 %collective-permute-start.14 = (bf16[480,128]{1,0:T(8,128)(2,1)S(1)}, bf16[480,128]{1,0:T(8,128)(2,1)S(1)}, u32[]{:S(2)}, u32[]{:S(2)}) collective-permute-start(bf16[480,128]{1,0:T(8,128)(2,1)S(1)} %concatenate.16.refs_0_), channel_id=1, source_target_pairs={{0,2},{1,3},{2,0},{3,1},{4,6},{5,7},{6,4},{7,5},{8,10},{9,11},{10,... | collective-permute-start | bytes 368648 | tf_op jit(solution)/shard_map/ppermute | solution.py:555
  80.6 5.3 %collective-permute-start.13 = (bf16[480,128]{1,0:T(8,128)(2,1)S(1)}, bf16[480,128]{1,0:T(8,128)(2,1)S(1)}, u32[]{:S(2)}, u32[]{:S(2)}) collective-permute-start(bf16[480,128]{1,0:T(8,128)(2,1)S(1)} %concatenate.16.refs_0_), channel_id=1, source_target_pairs={{0,1},{1,0},{2,3},{3,2},{4,5},{5,4},{6,7},{7,6},{8,9},{9,8},{10,11... | collective-permute-start | bytes 368648 | tf_op jit(solution)/shard_map/ppermute | solution.py:555
  86.0 0.7 copy-start.10
  86.0 0.7 copy-start.11

commit v2 on v1

--- a/solution.py
+++ b/solution.py
@@ -14,6 +14,7 @@
 F32 = jnp.float32
 BF = jnp.bfloat16
 W = 128
+STEP_MIB, BACK_MIB = 56, 56
 NOBODY = 300.0
 
 TAPS = 9 * 128
@@ -25,13 +26,15 @@
 R_CODE = R_BT + 256
 BIG = TAPS + 256
 S_Z, S_E, S_O, S_X = 0, 64, 96, 112
-SMALL = 128
+LATE, SMALL = 96, 128
 EXACT = 5
+PATCH = 96
 
 NN = (((1,), (0,)), ((), ()))
 NT = (((1,), (1,)), ((), ()))
 VMEM = pl.BlockSpec(memory_space=pltpu.VMEM)
 SMEM = pl.BlockSpec(memory_space=pltpu.SMEM)
+AWAY = pl.BlockSpec(memory_space=pl.ANY)
 
 
 def dot(a, b, dims=NN):
@@ -45,6 +48,11 @@
         out.append(piece)
         value = value - piece.astype(F32)
     return out
+
+
+def patch_row(t):
+    dr, dc = t // 3, t % 3
+    return ((dr // 2) * 3 + dc) * 16 + (dr % 2) * 8
 
 
 def pack_kernel(
@@ -85,7 +93,8 @@
     flat[...] = jnp.zeros_like(flat)
     for t in range(9):
         for c in range(3):
-            flat[8 * t + c : 8 * t + c + 1] = enc[3 * t + c]
+            row = patch_row(t) + c
+            flat[row : row + 1] = enc[3 * t + c]
     pack[R_ET : R_ET + 128] = flat[...].T.astype(BF)
     flat[...] = jnp.zeros_like(flat)
     flat[0:64] = lat[0]
@@ -120,18 +129,47 @@
     return sum(v[:, i : i + width] for i in range(0, v.shape[1], width))
 
 
-def silu_parts(v):
-    s = 0.5 * jnp.tanh(0.5 * v) + 0.5
-    out = v * s
-    return out, s + out * (1.0 - s)
+def silu_parts(half):
+    p = jnp.tanh(half) + 1.0
+    out = half * p
+    return out, p + out * (2.0 - p)
+
+
+def patches(x_s, row, n):
+    return jnp.concatenate([x_s[dc, :, at(row + pair, n)] for pair in (0, 2) for dc in range(3)], 0)
+
+
+def giver(bottom, send):
+    def give(start, one, zero, keep, offset, shift=0):
+        n = one.shape[0]
+        keep[start - shift : start - shift + n] = jnp.where(bottom, one, zero).astype(keep.dtype)
+        start = offset + start - shift
+        send[start : start + n] = jnp.where(bottom, zero, one).astype(BF)
+
+    return give
+
+
+def spread_back(dn, da):
+    rows = da.shape[1] // W - 2
+    near = jnp.concatenate([da[:, (2 - dr) * W : (2 - dr + rows) * W] for dr in range(3)], 0)
+    spread = dot(dn[...], near)
+    _, _, after = sides(spread[0:128])
+    before, _, _ = sides(spread[256:384])
+    return after + spread[128:256] + before
+
+
+def encoder_back(du, gap, h, slope, x, zn, g_z, g_e):
+    dz = (du + gap).astype(BF)
+    g_z[...] += dot(dz, h, NT)
+    dpre = (dot(zn[...], dz) * slope).astype(BF)
+    g_e[...] += dot(x, dpre, NT)
 
 
 def step_kernel(
     tile, near, across, mine, theirs,
-    keep_big, keep_small, send,
-    t_s, far_s, dn, dt, et, zn, zt, ot, on, bt,
-    u_s, p_s, h_s, slope_s, gap_s, da_s, g_d, g_o, g_e, g_z, g_s, l_s,
-    *, batches, rows, step_e, step_d, step_b,
+    keep_big, keep_small, send, h_out, slope_out, gap_out, da_out, x_out, dn_out, zn_out,
+    t_s, far_s, dt, et, zt, ot, on, bt, u_s, h_s, slope_s, gap_s, da_s, x_s, dn, zn, g_d, g_o, g_s, l_s, sems, fixed_sems,
+    *, batches, rows,
 ):
     level, me, devices = lax.axis_index("level"), lax.axis_index("dp"), lax.axis_size("dp")
     band, ext = 2 * rows, rows + 4
@@ -148,15 +186,17 @@
     for t in range(9):
         one, zero = pair(t * 128, 128)
         zero = jnp.concatenate([jnp.zeros((64, 128), BF), zero[0:64]], 0)
-        dn[t * 128 : (t + 1) * 128, 0:128] = one
-        dn[t * 128 : (t + 1) * 128, 128:256] = zero
-        dt[0:128, t * 128 : (t + 1) * 128] = one.astype(F32).T.astype(BF)
-        dt[128:256, t * 128 : (t + 1) * 128] = zero.astype(F32).T.astype(BF)
+        dr, dc = t // 3, t % 3
+        dn[dc * 128 : (dc + 1) * 128, dr * 256 : dr * 256 + 128] = one
+        dn[dc * 128 : (dc + 1) * 128, dr * 256 + 128 : (dr + 1) * 256] = zero
+        dt[0:128, t * 128 : (t + 1) * 128] = (0.5 * one.astype(F32)).T.astype(BF)
+        dt[128:256, t * 128 : (t + 1) * 128] = (0.5 * zero.astype(F32)).T.astype(BF)
     one, zero = pair(R_ET, 128)
-    et[0:128], et[128:256] = one, zero
+    et[0:128] = (0.5 * one.astype(F32)).astype(BF)
+    et[128:256] = (0.5 * zero.astype(F32)).astype(BF)
     one, zero = pair(R_ZN, 128)
-    zn[0:128] = one
-    zn[128:256] = pltpu.roll(zero.astype(F32), 64, 1).astype(BF)
+    zn[0:128] = (0.5 * one.astype(F32)).astype(BF)
+    zn[128:256] = pltpu.roll(0.5 * zero.astype(F32), 64, 1).astype(BF)
     one, zero = pair(R_ZT, 64)
     blank = jnp.zeros((64, 128), BF)
     zt[0:64] = jnp.concatenate([one, blank], 1)
@@ -171,11 +211,18 @@
         0,
     )
     ot[...] = out_t.astype(BF)
-    on[...] = out_t.T.astype(BF)
+    on[...] = (0.5 * out_t).T.astype(BF)
     for half in range(2):
         one, zero = pair(R_BT + half * 128, 128)
         bt[0, :, half * 128 : (half + 1) * 128] = one
         bt[1, :, half * 128 : (half + 1) * 128] = zero
+
+    fixed = [
+        pltpu.make_async_copy(a, o, fixed_sems.at[n])
+        for n, (a, o) in enumerate(((x_s, x_out), (dn, dn_out), (zn, zn_out)))
+    ]
+    fixed[1].start()
+    fixed[2].start()
 
     far_s[0 : batches * band] = theirs[R_CODE : R_CODE + batches * band].astype(F32)
     far_s[batches * band : batches * band + across.shape[0]] = across[...].astype(F32)
@@ -206,17 +253,8 @@
             other = jnp.where(valid > 0, far_s[row : row + 1], NOBODY)
             lay(b, jnp.where(bottom, rows + 2 + r, r), shown, other)
 
-    for ref in (g_d, g_o, g_e, g_z, g_s, l_s):
+    for ref in (g_d, g_o, g_s, l_s):
         ref[...] = jnp.zeros_like(ref)
-
-    def patch(i, _):
-        b, e = i // rows, i % rows + 2
-        views = [view for dr in range(3) for view in sides(t_s[b, e + dr - 1])]
-        value = jnp.concatenate(views + [jnp.zeros((56, W), F32)], 0)
-        p_s[:, at(i, 1)] = value.astype(BF)
-        return 0
-
-    lax.fori_loop(0, batches * rows, patch, 0, unroll=2)
 
     def lookup(b, e, n):
         here = jnp.concatenate([t_s[b, e + i] for i in range(n)], 1)
@@ -236,128 +274,93 @@
             u_s[k, :, at(b * ext + e, n)] = view.astype(BF)
         return here, u, onehots, highs
 
-    def outer(i, _):
-        lookup(i // 2, (i % 2) * (rows + 2), 2)
-        return 0
-
-    lax.fori_loop(0, batches * 2, outer, 0)
-
-    def encode(i, _):
-        n = step_e
-        b, e = i // (rows // n), (i % (rows // n)) * n + 2
-        here, u, onehots, highs = lookup(b, e, n)
-        own = at(i * n, n)
-        h, slope = silu_parts(dot(et[...], p_s[:, own]))
-        slope_s[:, own] = slope
+    pairs = ((h_s, h_out), (slope_s, slope_out), (gap_s, gap_out), (da_s, da_out))
+
+    def leave(b, which=range(4)):
+        return [pltpu.make_async_copy(pairs[n][0].at[b], pairs[n][1].at[b], sems.at[n, b]) for n in which]
+
+    def encode(b, _):
+        runs = [jnp.concatenate([t_s[b, e], t_s[b, e + 1]], 0) for e in range(1, rows + 3)]
+        for dc, view in enumerate(sides(jnp.concatenate(runs, 1))):
+            x_s[dc, :, at(b * (rows + 2), rows + 2)] = view.astype(BF)
+        here, u, onehots, highs = lookup(b, 0, ext)
+        inner = slice(2 * W, (2 + rows) * W)
+        here, u = here[:, inner], u[:, inner]
+        h, slope = silu_parts(dot(et[:, 0:PATCH], patches(x_s, b * (rows + 2), rows)))
+        slope_s[b] = slope
         h = h.astype(BF)
-        h_s[:, own] = h
+        h_s[b] = h
         z = dot(zt[...], h)
         k = here[3:4]
         gap = z - u
         kept = k * gap
         l_s[0:128] += fold(kept * gap, 256)
-        gap_s[:, own] = 0.5 * kept
+        gap_s[b] = 0.5 * kept
         z = k * z.astype(BF).astype(F32)
-        row = lax.broadcasted_iota(jnp.int32, (16, n * W), 0)
+        row = lax.broadcasted_iota(jnp.int32, (16, rows * W), 0)
         for v in range(2):
             part_z = z[v * 64 : v * 64 + 64]
-            low_k = jnp.where(highs[v], 0.0, k)
-            high_k = jnp.where(highs[v], k, 0.0)
+            high = highs[v][:, inner]
+            low_k = jnp.where(high, 0.0, k)
+            high_k = jnp.where(high, k, 0.0)
             left = jnp.concatenate(
                 [
-                    jnp.where(highs[v], 0.0, part_z),
-                    jnp.where(highs[v], part_z, 0.0),
+                    jnp.where(high, 0.0, part_z),
+                    jnp.where(high, part_z, 0.0),
                     jnp.where(row == 0, low_k, jnp.where(row == 1, high_k, 0.0)),
                 ],
                 0,
             ).astype(BF)
-            g_s[v] += dot(left, onehots[v], NT)
+            g_s[v] += dot(left, onehots[v][:, inner], NT)
+        for copy in leave(b, range(3)):
+            copy.start()
         return 0
 
-    lax.fori_loop(0, batches * (rows // step_e), encode, 0)
-
-    def decode(b, spans, own):
-        views = []
-        for dr in range(3):
-            for dc in range(3):
-                runs = [u_s[dc, :, at(b * ext + e + dr - 1, n)] for e, n in spans]
-                views.append(runs[0] if len(runs) == 1 else jnp.concatenate(runs, 1))
-        u = jnp.concatenate(views, 0)
+    lax.fori_loop(0, batches, encode, 0)
+    fixed[0].start()
+
+    def decode(b, _):
+        u = jnp.concatenate(
+            [u_s[dc, :, at(b * ext + dr, rows + 2)] for dr in range(3) for dc in range(3)], 0
+        )
+        inner = slice(W, (1 + rows) * W)
         g, slope = silu_parts(dot(dt[...], u))
         g = g.astype(BF)
         y = dot(ot[...], g)
-        here = jnp.concatenate([t_s[b, e + i] for e, n in spans for i in range(n)], 1)
+        here = jnp.concatenate([t_s[b, e] for e in range(1, rows + 3)], 1)
         k = here[3:4]
         x = jnp.where(lax.broadcasted_iota(jnp.int32, here.shape, 0) < 3, here, 0.0)
         diff = y - jnp.concatenate([x, x], 0)
         kept = k * diff
         dy = (2.0 * kept).astype(BF)
-        da = dot(on[...], dy) * slope
-        for dc, view in enumerate(sides(da)):
-            first = 0
-            for e, n in spans:
-                da_s[dc, :, at(b * (rows + 2) + e - 1, n)] = view[:, first : first + n * W].astype(BF)
-                first += n * W
-        if own:
-            l_s[128:144] += fold(kept * diff, 256)
-            g_o[...] += dot(dy, g, NT)
-            g_d[...] += dot(u, da.astype(BF), NT)
-
-    def edge(b, _):
-        decode(b, [(1, 1), (rows + 2, 1)], False)
+        da = (dot(on[...], dy) * slope).astype(BF)
+        da_s[b] = da
+        l_s[128:144] += fold((kept * diff)[:, inner], 256)
+        g_o[...] += dot(dy[:, inner], g[:, inner], NT)
+        g_d[...] += dot(u[:, inner], da[:, inner], NT)
+        leave(b, [3])[0].start()
         return 0
 
-    lax.fori_loop(0, batches, edge, 0)
-
-    def middle(i, _):
-        n = step_d
-        decode(i // (rows // n), [((i % (rows // n)) * n + 2, n)], True)
-        return 0
-
-    lax.fori_loop(0, batches * (rows // step_d), middle, 0)
-
-    def back(i, _):
-        n = step_b
-        b, r = i // (rows // n), (i % (rows // n)) * n
-        own = at(i * n, n)
-        du = jnp.zeros((128, n * W), F32)
-        for dr in range(3):
-            for dc in range(3):
-                t = 3 * dr + dc
-                view = da_s[2 - dc, :, at(b * (rows + 2) + r + 2 - dr, n)]
-                du = du + dot(dn[t * 128 : (t + 1) * 128], view)
-        dz = (du + gap_s[:, own]).astype(BF)
-        g_z[...] += dot(dz, h_s[:, own], NT)
-        dpre = (dot(zn[...], dz) * slope_s[:, own]).astype(BF)
-        g_e[...] += dot(p_s[:, own], dpre, NT)
-        return 0
-
-    lax.fori_loop(0, batches * (rows // step_b), back, 0)
-
-    def give(start, one, zero, keep, offset):
-        n = one.shape[0]
-        keep[start : start + n] = jnp.where(bottom, one, zero).astype(keep.dtype)
-        send[offset + start : offset + start + n] = jnp.where(bottom, zero, one).astype(BF)
-
+    lax.fori_loop(0, batches, decode, 0)
+    give = giver(bottom, send)
     for t in range(9):
         top = jnp.concatenate([g_d[t * 128 + 64 : (t + 1) * 128, 128:256], jnp.zeros((64, 128), F32)], 0)
         give(t * 128, g_d[t * 128 : (t + 1) * 128, 0:128], top, keep_big, 0)
     for half in range(2):
         cols = slice(half * 128, (half + 1) * 128)
         give(TAPS + half * 128, g_s[0, 0:128, cols], g_s[1, 0:128, cols], keep_big, 0)
-    give(S_Z, g_z[0:64, 0:128], g_z[64:128, 128:256], keep_small, BIG)
-    enc = []
-    for cols in (slice(0, 128), slice(128, 256)):
-        runs = [g_e[8 * t : 8 * t + 3, cols] for t in range(9)]
-        enc.append(jnp.concatenate(runs + [jnp.zeros((5, 128), F32)], 0))
-    give(S_E, enc[0], enc[1], keep_small, BIG)
+    pad = keep_big.shape[0]
+    if pad > BIG:
+        keep_big[BIG:pad] = jnp.zeros((pad - BIG, W), F32)
+        send[BIG:pad] = jnp.zeros((pad - BIG, W), BF)
     blank = jnp.zeros((8, 128), F32)
     give(
         S_O,
         jnp.concatenate([g_o[0:8, 0:128], blank], 0),
         jnp.concatenate([g_o[8:16, 128:256], blank], 0),
         keep_small,
-        BIG,
+        pad,
+        LATE,
     )
     valid_sum = jnp.sum(g_s[0, 128:130])
     loss = 0.25 * jnp.sum(l_s[0:128]) + jnp.sum(l_s[128:144])
@@ -368,7 +371,56 @@
         runs = [g_s[v, 128 + hi : 129 + hi, half * 128 : (half + 1) * 128] for hi in range(2) for half in range(2)]
         pieces = part(jnp.concatenate(runs + [other], 0), 3)
         exact.append(jnp.concatenate([p.astype(F32) for p in pieces] + [jnp.zeros((1, 128), F32)], 0))
-    give(S_X, exact[0], exact[1], keep_small, BIG)
+    give(S_X, exact[0], exact[1], keep_small, pad, LATE)
+    for copy in fixed + [copy for b in range(batches) for copy in leave(b)]:
+        copy.wait()
+
+
+def back_kernel(
+    h_in, slope_in, gap_in, da_in, x_in, dn_in, zn_in, _,
+    keep, send, h_s, slope_s, gap_s, da_s, x_s, dn, zn, g_e, g_z, sems, fixed_sems,
+    *, batches, rows,
+):
+    bottom = lax.axis_index("level") == 1
+    pairs = ((h_in, h_s), (slope_in, slope_s), (gap_in, gap_s), (da_in, da_s))
+
+    def fetch(b):
+        return [pltpu.make_async_copy(a.at[b], o.at[b], sems.at[n, b]) for n, (a, o) in enumerate(pairs)]
+
+    fixed = [
+        pltpu.make_async_copy(a, o, fixed_sems.at[n])
+        for n, (a, o) in enumerate(((dn_in, dn), (zn_in, zn), (x_in, x_s)))
+    ]
+    count = h_s.shape[0]
+    copies = [fetch(b) for b in range(count)]
+    for copy in [fixed[0], copies[0][3], copies[0][2], fixed[1], *copies[0][:2], fixed[2]]:
+        copy.start()
+    g_e[...] = jnp.zeros_like(g_e)
+    g_z[...] = jnp.zeros_like(g_z)
+    fixed[0].wait()
+    copies[0][3].wait()
+    for b in range(1, count):
+        for n in (3, 2, 0, 1):
+            copies[b][n].start()
+    du = spread_back(dn, da_s[0])
+    for copy in [fixed[1], fixed[2]]:
+        copy.wait()
+    for b in range(count):
+        for copy in copies[b][:3]:
+            copy.wait()
+        if b + 1 < count:
+            copies[b + 1][3].wait()
+        row = b * (rows + 2)
+        encoder_back(du, gap_s[b], h_s[b], slope_s[b], patches(x_s, row, rows), zn, g_z, g_e)
+        if b + 1 < count:
+            du = spread_back(dn, da_s[b + 1])
+    give = giver(bottom, send)
+    give(S_Z, g_z[0:64, 0:128], g_z[64:128, 128:256], keep, 0)
+    enc = []
+    for cols in (slice(0, 128), slice(128, 256)):
+        runs = [g_e[patch_row(t) : patch_row(t) + 3, cols] for t in range(9)]
+        enc.append(jnp.concatenate(runs + [jnp.zeros((5, 128), F32)], 0))
+    give(S_E, enc[0], enc[1], keep, 0)
 
 
 def update_kernel(
@@ -378,11 +430,15 @@
     (count, total, ew, e1, e2, zw, z1, z2, dw, d1, d2, ow, o1, o2,
      loss_out, valid_out, count_out, total_out,
      em, es, ep, ec, zm, zs, zp, zc, dm, ds, dp, dc, om, os, op, oc, big, rows) = refs
-    share = BIG // stages
+    share = big.shape[0] // stages
     index = (lax.axis_index("dp") >> start) & (stages - 1)
+    size = big.shape[0] // lax.axis_size("dp")
     small = jnp.zeros((SMALL, W), F32)
     for n, ref in enumerate(parts):
-        big[pl.ds(pl.multiple_of((index ^ n) * share, 16), share), :] = ref[0:share].astype(F32)
+        value = ref[0:share].astype(F32)
+        for h in range(share // size):
+            row = pl.multiple_of((h * stages + (index ^ n)) * size, 8)
+            big[pl.ds(row, size), :] = value[h * size : (h + 1) * size]
         small = small + ref[share : share + SMALL].astype(F32)
     exact = sum(small[S_X + EXACT * i : S_X + EXACT * (i + 1)] for i in range(3))
     loss = jnp.sum(exact[4:5, 0:1])
@@ -441,14 +497,14 @@
     return lax.reduce_precision(value, 8, 7)
 
 
-def sum_small(parts):
+def sum_small(parts, first):
     total = sum(item.astype(F32) for item in parts)
-    value = sum(total[S_X + EXACT * i : S_X + EXACT * (i + 1)] for i in range(3))
+    value = sum(total[first + EXACT * i : first + EXACT * (i + 1)] for i in range(3))
     high = lowered(value)
     middle = lowered(value - high)
     low = value - high - middle
-    rest = total[S_X + 3 * EXACT :]
-    return jnp.concatenate([total[:S_X], high, middle, low, rest], 0).astype(BF)
+    rest = total[first + 3 * EXACT :]
+    return jnp.concatenate([total[:first], high, middle, low, rest], 0).astype(BF)
 
 
 def local(
@@ -472,21 +528,26 @@
         jnp.transpose(item, (2, 0, 1)) for item in (readout_weight, readout_first, readout_second)
     )
 
-    limit = pltpu.CompilerParams(vmem_limit_bytes=56 * 1024 * 1024)
+    def limit(mib):
+        return pltpu.CompilerParams(vmem_limit_bytes=mib * 1024 * 1024)
+
+    def outside(*items):
+        return [pltpu.with_memory_space_constraint(item, pltpu.HBM) for item in items]
+
     packed = R_CODE + batches * band
     tile, near, across, pack = pl.pallas_call(
         pack_kernel,
         out_shape=[
-            jax.ShapeDtypeStruct((batches * band * 8, W), F32),
-            jax.ShapeDtypeStruct((batches * 16, W), BF),
-            jax.ShapeDtypeStruct((16, W), BF),
-            jax.ShapeDtypeStruct((packed, W), BF),
+            pltpu.VMEM((batches * band * 8, W), F32),
+            pltpu.VMEM((batches * 16, W), BF),
+            pltpu.VMEM((16, W), BF),
+            pltpu.VMEM((packed, W), BF),
         ],
         in_specs=[VMEM] * 9,
         out_specs=[VMEM] * 4,
         scratch_shapes=[pltpu.VMEM((batches * band, W), F32), pltpu.VMEM((128, 128), F32)],
-        compiler_params=limit,
-    )(image, mask, codes, ema_count, ema_sum, encoder_weight, latent_weight, decoder_weight, readout_weight)
+        compiler_params=limit(56),
+    )(*outside(image, mask, codes, ema_count, ema_sum, encoder_weight, latent_weight, decoder_weight, readout_weight))
 
     both = ("level", "dp")
     same = [(d - 1, d) for d in range(1, devices)] + [(devices + d + 1, devices + d) for d in range(devices - 1)]
@@ -497,70 +558,90 @@
 
     ext = rows + 4
     pixels = batches * rows * W
-    keep_big, keep_small, send = pl.pallas_call(
-        functools.partial(step_kernel, batches=batches, rows=rows, step_e=rows, step_d=rows, step_b=rows // 2),
+    framed = batches * (rows + 2) * W
+    held = [
+        ((batches, 256, rows * W), BF),
+        ((batches, 256, rows * W), F32),
+        ((batches, 128, rows * W), F32),
+        ((batches, 256, (rows + 2) * W), BF),
+    ]
+    fixed = [((3, 16, framed), BF), ((384, 768), BF), ((256, 128), BF)]
+    size = -(-BIG // (8 * devices)) * 8
+    padded = size * devices
+    shape = jax.ShapeDtypeStruct
+    keep, early, send, *kept = pl.pallas_call(
+        functools.partial(step_kernel, batches=batches, rows=rows),
         out_shape=[
-            jax.ShapeDtypeStruct((BIG, W), F32),
-            jax.ShapeDtypeStruct((SMALL, W), BF),
-            jax.ShapeDtypeStruct((BIG + SMALL, W), BF),
+            pltpu.VMEM((padded, W), F32),
+            pltpu.VMEM((SMALL - LATE, W), BF),
+            pltpu.VMEM((padded + SMALL - LATE, W), BF),
+            *[shape(*item) for item in held + fixed],
         ],
         in_specs=[VMEM] * 5,
-        out_specs=[VMEM] * 3,
+        out_specs=[VMEM] * 3 + [AWAY] * 7,
         scratch_shapes=[
             pltpu.VMEM((batches, ext, 8, W), F32),
             pltpu.VMEM((batches * band + 16, W), F32),
-            pltpu.VMEM((TAPS, 256), BF),
             pltpu.VMEM((256, TAPS), BF),
-            pltpu.VMEM((256, 128), BF),
             pltpu.VMEM((256, 128), BF),
             pltpu.VMEM((128, 256), BF),
             pltpu.VMEM((16, 256), BF),
             pltpu.VMEM((256, 16), BF),
             pltpu.VMEM((2, 128, 256), BF),
             pltpu.VMEM((3, 128, batches * ext * W), BF),
-            pltpu.VMEM((128, pixels), BF),
-            pltpu.VMEM((256, pixels), BF),
-            pltpu.VMEM((256, pixels), F32),
-            pltpu.VMEM((128, pixels), F32),
-            pltpu.VMEM((3, 256, batches * (rows + 2) * W), BF),
+            *[pltpu.VMEM(*item) for item in held + fixed],
             pltpu.VMEM((TAPS, 256), F32),
             pltpu.VMEM((16, 256), F32),
-            pltpu.VMEM((128, 256), F32),
-            pltpu.VMEM((128, 256), F32),
             pltpu.VMEM((2, 144, 256), F32),
             pltpu.VMEM((144, 256), F32),
+            pltpu.SemaphoreType.DMA((4, batches)),
+            pltpu.SemaphoreType.DMA((3,)),
         ],
-        compiler_params=limit,
-    )(tile, near, across, pack, theirs)
-
-    got = lax.ppermute(send, "level", [(0, 1), (1, 0)])
-    small = sum_small([keep_small, got[BIG:]])
-    big = keep_big + got[:BIG].astype(F32)
-
+        compiler_params=limit(STEP_MIB),
+    )(*[pltpu.with_memory_space_constraint(item, pltpu.VMEM) for item in (tile, near, across, pack, theirs)])
+
+    swap = [(0, 1), (1, 0)]
+    got = lax.ppermute(send, "level", swap)
+    early = sum_small([early, got[padded:]], S_X - LATE)
+    big = (keep + got[:padded].astype(F32)).astype(BF)
+    big = lax.all_to_all(big.reshape(devices, size, W), "dp", 0, 0)
+
+    late, send = pl.pallas_call(
+        functools.partial(back_kernel, batches=batches, rows=rows),
+        out_shape=[pltpu.VMEM((LATE, W), BF), pltpu.VMEM((LATE, W), BF)],
+        in_specs=[AWAY] * 8,
+        out_specs=[VMEM] * 2,
+        scratch_shapes=[
+            *[pltpu.VMEM(*item) for item in held + fixed],
+            pltpu.VMEM((PATCH, 256), F32),
+            pltpu.VMEM((128, 256), F32),
+            pltpu.SemaphoreType.DMA((4, batches)),
+            pltpu.SemaphoreType.DMA((3,)),
+        ],
+        compiler_params=limit(BACK_MIB),
+        cost_estimate=pl.CostEstimate(flops=2 * pixels * 98304 * 4, bytes_accessed=1 << 20, transcendentals=0),
+    )(*outside(*kept), got)
+    big, send = lax.optimization_barrier((big, send))
+    got = lax.ppermute(send, "level", swap)
+    late = (late.astype(F32) + got.astype(F32)).astype(BF)
+    small = jnp.concatenate([late, early], 0)
+
+    big = jnp.sum(big.astype(F32), 0).astype(BF)[None]
     stages = radices(devices)
-    for start, width_bits in stages:
-        count = 1 << width_bits
-        index = (me >> start) & (count - 1)
-        pieces = big.reshape(count, -1, W)
-        total = lax.dynamic_index_in_dim(pieces, index, 0, False)
-        for k in range(count - 1, 0, -1):
-            out = lax.dynamic_index_in_dim(pieces, index ^ k, 0, False).astype(BF)
-            total = total + lax.ppermute(out, "dp", xor_pairs(devices, k << start)).astype(F32)
-        big = total
-    big = big.astype(BF)
     for number, (start, width_bits) in enumerate(reversed(stages)):
         count = 1 << width_bits
         index = (me >> start) & (count - 1)
-        payload = jnp.concatenate([big, small], 0)
+        payload = jnp.concatenate([big.reshape(-1, W), small], 0)
         parts = [payload] + [lax.ppermute(payload, "dp", xor_pairs(devices, k << start)) for k in range(1, count)]
         if number == len(stages) - 1:
             break
-        size = big.shape[0]
-        stacked = jnp.zeros((count, size, W), BF)
+        high = big.shape[0]
+        stacked = jnp.zeros((high, count, size, W), BF)
         for k in range(count):
-            stacked = lax.dynamic_update_index_in_dim(stacked, parts[k][:size], index ^ k, 0)
-        big = stacked.reshape(count * size, W)
-        small = sum_small([item[size:] for item in parts])
+            piece = parts[k][: high * size].reshape(high, size, W)
+            stacked = lax.dynamic_update_index_in_dim(stacked, piece, index ^ k, 1)
+        small = sum_small([item[high * size :] for item in parts], S_X)
+        big = stacked.reshape(high * count, size, W)
 
     state = (
         ema_count, ema_sum,
@@ -577,8 +658,8 @@
         out_shape=outs,
         in_specs=[VMEM] * (len(parts) + len(state)),
         out_specs=[SMEM] * 2 + [VMEM] * (len(outs) - 2),
-        scratch_shapes=[pltpu.VMEM((BIG, W), F32), pltpu.VMEM((32, W), F32)],
-        compiler_params=pltpu.CompilerParams(vmem_limit_bytes=24 * 1024 * 1024),
+        scratch_shapes=[pltpu.VMEM((padded, W), F32), pltpu.VMEM((32, W), F32)],
+        compiler_params=limit(16),
     )(*parts, *state)
     loss, valid, count_new, total_new = result[:4]
     enc, lat, dec, read = (list(result[4 * n : 4 * n + 4]) for n in range(1, 5))

time: 89 us -> 74.7 us (0.84)
  Pallas kernels: 40.5 us -> 34 us
  waiting for transfers between devices: 17.6 us -> 13.3 us
  starting transfers between devices: 26.3 us -> 24.4 us
  local copies, waits for them, and re-layouts: 2.01 us -> 0.63 us
    ppermute x7 -> x2, starting transfers between devices: 12.8 us -> 3.48 us  [local(): got = lax.ppermute(send, 'level', swap)]
    ppermute x7 -> x2, waiting for transfers between devices: 10.1 us -> 2.42 us  [local(): got = lax.ppermute(send, 'level', swap)]
    all_to_all x0 -> x1, starting transfers between devices: none -> 7.36 us  [local(): big = lax.all_to_all(big.reshape(devices, size, W), 'dp', 0, 0)]
    pallas_call x2 -> x3, Pallas kernels: 38.4 us -> 31.8 us  [the longest x1 20.6 us: local(): pl.pallas_call(functools.partial(step_kernel, batches=batches, rows=rows)...]
    all_to_all x0 -> x1, waiting for transfers between devices: none -> 2.2 us  [local(): big = lax.all_to_all(big.reshape(devices, size, W), 'dp', 0, 0)]
    unnamed x38 -> x30, local copies, waits for them, and re-layouts: 1.42 us -> 0.09 us
    ppermute x6, waiting for transfers between devices: 6.67 us -> 7.97 us  [local(): lax.ppermute(payload, 'dp', xor_pairs(devices, k << start))]
    add x2 -> x0, other arithmetic: 1.22 us -> none  [the longest x1 1.17 us: local(): big = keep_big + got[:BIG].astype(F32)]
  transfers between devices with their start and end apart: 16 -> 12, of which waited for: 12 -> 8; matrix products, arithmetic and copies ran while one was open for 0% -> 0% of each run, Pallas kernels for 0% -> 13%
where the time goes in v2:
time: 74.7 us; the launch traced here: 74.5 us
  Pallas kernels  34 us (46%)
  starting transfers between devices  24.4 us (33%)
  waiting for transfers between devices  13.3 us (18%)
  between operations  1.17 us (2%)
  other arithmetic  0.99 us (1%)
    pallas_call x1, Pallas kernels, local(): pl.pallas_call(functools.partial(step_kernel, batches=batches, rows=rows)...  20.6 us
    pallas_call x1, Pallas kernels, local(): pl.pallas_call(functools.partial(back_kernel, batches=batches, rows=rows)...  9.83 us
    ppermute x6, starting transfers between devices, local(): lax.ppermute(payload, 'dp', xor_pairs(devices, k << start))  7.98 us
    ppermute x6, waiting for transfers between devices, local(): lax.ppermute(payload, 'dp', xor_pairs(devices, k << start))  7.97 us
    all_to_all x1, starting transfers between devices, local(): big = lax.all_to_all(big.reshape(devices, size, W), 'dp', 0, 0)  7.36 us
    ppermute x1, starting transfers between devices, local(): near = lax.ppermute(near, both, same)  4.41 us
    ppermute x2, starting transfers between devices, local(): got = lax.ppermute(send, 'level', swap)  3.48 us
    ppermute x2, waiting for transfers between devices, local(): got = lax.ppermute(send, 'level', swap)  2.42 us
  transfers between devices with their start and end apart: 12, of which 8 were waited for; matrix products, arithmetic and copies ran while one was open for 0% of the time, Pallas kernels for 13%

profile of v2, /device:TPU:0, one launch (start us, length us, event | category | flops | bytes accessed | tf_op | source)
XLA Modules:
  0.0 74.5 jit_solution(16716958185142616055)
XLA Ops:
  0.7 1.4 %shard_map.320 = (f32[768,128]{1,0:T(8,128)S(1)}, bf16[48,128]{1,0:T(8,128)(2,1)S(1)}, bf16[16,128]{1,0:T(8,128)(2,1)S(1)}, bf16[1840,128]{1,0:T(8,128)(2,1)S(1)}) custom-call(bf16[3,3,32,128]{3,2,1,0:T(8,128)(2,1)} %image.1, s32[3,32,128]{2,1,0:T(8,128)} %mask.1, s32[1,3,32,128]{3,2,1,0:T(8,128)} %codes.1, f32[1,512]{1,0:T(1,128)} %refs_4_.1, ...), custom_call_target="tpu_custom_call" | custom-call | tf_op jit(solution)/shard_map/pallas_call | solution.py:538
  2.1 0.5 collective-permute-start.2
  2.6 4.4 %collective-permute-start = (bf16[48,128]{1,0:T(8,128)(2,1)S(1)}, bf16[48,128]{1,0:T(8,128)(2,1)S(1)}, u32[]{:S(2)}, u32[]{:S(2)}) collective-permute-start(bf16[48,128]{1,0:T(8,128)(2,1)S(1)} %get-tuple-element.59), channel_id=1, source_target_pairs={{0,1},{1,2},{2,3},{3,4},{4,5},{5,6},{6,7},{7,8},{8,9},{9,10},{10,1... | collective-permute-start | bytes 36872 | tf_op jit(solution)/shard_map/ppermute | solution.py:555
  7.0 0.7 collective-permute-start.1
  7.7 0.0 collective-permute-done.1.across
  7.7 0.7 collective-permute-done.near
  8.4 0.0 collective-permute-done.2.theirs
  8.4 20.6 %shard_map.321 = (f32[1408,128]{1,0:T(8,128)S(1)}, bf16[32,128]{1,0:T(8,128)(2,1)S(1)}, bf16[1440,128]{1,0:T(8,128)(2,1)S(1)}, bf16[3,256,2048]{2,1,0:T(8,128)(2...) custom-call(f32[768,128]{1,0:T(8,128)S(1)} %get-tuple-element.58.til, ...), custom_call_target="tpu_custom_call" | custom-call | tf_op jit(solution)/shard_map/pallas_call | solution.py:572
  29.0 3.5 %collective-permute-start.3 = (bf16[1440,128]{1,0:T(8,128)(2,1)S(1)}, bf16[1440,128]{1,0:T(8,128)(2,1)S(1)}, u32[]{:S(2)}, u32[]{:S(2)}) collective-permute-start(bf16[1440,128]{1,0:T(8,128)(2,1)S(1)} %get-tuple-element.63), channel_id=1, source_target_pairs={{0,16},{16,0},{1,17},{17,1},{2,18},{18,2},{3,19},{19,3},{4,20},{20... | collective-permute-start | bytes 1105928 | tf_op jit(solution)/shard_map/ppermute | solution.py:604
  32.5 1.3 %collective-permute-done.3._ = bf16[1440,128]{1,0:T(8,128)(2,1)S(1)} collective-permute-done((bf16[1440,128]{1,0:T(8,128)(2,1)S(1)}, bf16[1440,128]{1,0:T(8,128)(2,1)S(1)}, u32[]{:S(2)}, u32[]{:S(2)}) %collective-permute-start.3) | collective-permute-done | bytes 368672 | tf_op jit(solution)/shard_map/ppermute | solution.py:604
  33.8 0.9 %add_convert_fusion = bf16[1408,128]{1,0:T(8,128)(2,1)} fusion(f32[1408,128]{1,0:T(8,128)S(1)} %get-tuple-element.62, bf16[1440,128]{1,0:T(8,128)(2,1)S(1)} %collective-permute-done.3._), kind=kLoop, calls=%fused_computation | loop fusion | flops 540672 | bytes 1441792 | tf_op jit(solution)/shard_map/convert_element_type | solution.py:606
  34.6 7.4 %all-to-all-start = ((bf16[16,88,128]{2,1,0:T(8,128)(2,1)}), bf16[16,88,128]{2,1,0:T(8,128)(2,1)S(1)}, u32[]{:S(2)}, u32[]{:S(2)}) async-start(bf16[16,88,128]{2,1,0:T(8,128)(2,1)} %bitcast.4), calls=%async_computation | async-start | bytes 720896 | tf_op jit(solution)/shard_map/all_to_all | solution.py:607
  42.0 0.0 copy-done.14
  42.0 0.0 copy-start
  42.1 0.0 copy-start.1
  42.1 0.0 copy-start.2
  42.1 0.0 copy-start.3
  42.1 0.0 copy-start.4
  42.1 0.0 copy-start.5
  42.1 0.0 copy-start.6
  42.1 0.0 copy-start.7
  42.1 0.0 copy-start.8
  42.2 0.0 copy-start.9
  42.2 0.0 copy-start.10
  42.2 0.0 copy-start.11
  42.2 0.0 copy-start.12
  42.2 0.0 copy-start.13
  42.2 9.8 %shard_map.322 = (bf16[96,128]{1,0:T(8,128)(2,1)S(1)}, bf16[96,128]{1,0:T(8,128)(2,1)S(1)}) custom-call(bf16[3,256,2048]{2,1,0:T(8,128)(2,1)} %get-tuple-element.64.h_in, f32[3,256,2048]{2,1,0:T(8,128)} %get-tuple-element.65.slope_in, f32[3,128,2048]{2,1,0:T(8,128)} %get-tuple-element.66.gap_in, bf16[3,256,2304]{2,1,0:T(8,128)(2,1)} %get-tuple-element.67.da_in, ...), custom_call_target="tpu_custom_call" | custom-call | flops 4831838208 | bytes 1048576 | tf_op jit(solution)/shard_map/pallas_call | solution.py:609
  52.1 2.2 %all-to-all-done = bf16[16,88,128]{2,1,0:T(8,128)(2,1)S(1)} async-done(((bf16[16,88,128]{2,1,0:T(8,128)(2,1)}), bf16[16,88,128]{2,1,0:T(8,128)(2,1)S(1)}, u32[]{:S(2)}, u32[]{:S(2)}) %all-to-all-start) | async-done | bytes 360480 | tf_op jit(solution)/shard_map/all_to_all | solution.py:607
  54.3 0.0 collective-permute-start.4
  54.3 0.1 reduce_sum.12
  54.3 1.1 %collective-permute-done.4 = bf16[96,128]{1,0:T(8,128)(2,1)S(1)} collective-permute-done((bf16[96,128]{1,0:T(8,128)(2,1)S(1)}, bf16[96,128]{1,0:T(8,128)(2,1)S(1)}, u32[]{:S(2)}, u32[]{:S(2)}) %collective-permute-start.4) | collective-permute-done | bytes 24608 | tf_op jit(solution)/shard_map/ppermute | solution.py:625
  55.5 0.2 concatenate.17
  55.6 1.1 %collective-permute-start.5 = (bf16[216,128]{1,0:T(8,128)(2,1)S(1)}, bf16[216,128]{1,0:T(8,128)(2,1)S(1)}, u32[]{:S(2)}, u32[]{:S(2)}) collective-permute-start(bf16[216,128]{1,0:T(8,128)(2,1)S(1)} %concatenate.17), channel_id=1, source_target_pairs={{0,4},{1,5},{2,6},{3,7},{4,0},{5,1},{6,2},{7,3},{8,12},{9,13},{10,... | collective-permute-start | bytes 165896 | tf_op jit(solution)/shard_map/ppermute | solution.py:635
  56.7 1.1 %collective-permute-start.6 = (bf16[216,128]{1,0:T(8,128)(2,1)S(1)}, bf16[216,128]{1,0:T(8,128)(2,1)S(1)}, u32[]{:S(2)}, u32[]{:S(2)}) collective-permute-start(bf16[216,128]{1,0:T(8,128)(2,1)S(1)} %concatenate.17), channel_id=1, source_target_pairs={{0,8},{1,9},{2,10},{3,11},{4,12},{5,13},{6,14},{7,15},{8,0},{9,1},... | collective-permute-start | bytes 165896 | tf_op jit(solution)/shard_map/ppermute | solution.py:635
  57.8 2.2 %collective-permute-start.7 = (bf16[216,128]{1,0:T(8,128)(2,1)S(1)}, bf16[216,128]{1,0:T(8,128)(2,1)S(1)}, u32[]{:S(2)}, u32[]{:S(2)}) collective-permute-start(bf16[216,128]{1,0:T(8,128)(2,1)S(1)} %concatenate.17), channel_id=1, source_target_pairs={{0,12},{1,13},{2,14},{3,15},{4,8},{5,9},{6,10},{7,11},{8,4},{9,5},... | collective-permute-start | bytes 165896 | tf_op jit(solution)/shard_map/ppermute | solution.py:635
  60.1 0.1 concatenate.18
  60.2 0.0 collective-permute-done.5
  60.2 3.9 %collective-permute-done.6 = bf16[216,128]{1,0:T(8,128)(2,1)S(1)} collective-permute-done((bf16[216,128]{1,0:T(8,128)(2,1)S(1)}, bf16[216,128]{1,0:T(8,128)(2,1)S(1)}, u32[]{:S(2)}, u32[]{:S(2)}) %collective-permute-start.6) | collective-permute-done | bytes 55328 | tf_op jit(solution)/shard_map/ppermute | solution.py:635
  64.2 0.0 collective-permute-done.7
  64.3 0.2 concatenate.19.refs_0_
  64.5 2.0 %collective-permute-start.10 = (bf16[480,128]{1,0:T(8,128)(2,1)S(1)}, bf16[480,128]{1,0:T(8,128)(2,1)S(1)}, u32[]{:S(2)}, u32[]{:S(2)}) collective-permute-start(bf16[480,128]{1,0:T(8,128)(2,1)S(1)} %concatenate.19.refs_0_), channel_id=1, source_target_pairs={{0,3},{1,2},{2,1},{3,0},{4,7},{5,6},{6,5},{7,4},{8,11},{9,10},{10,... | collective-permute-start | bytes 368648 | tf_op jit(solution)/shard_map/ppermute | solution.py:635
  66.5 0.7 collective-permute-start.8
  67.2 0.8 %collective-permute-start.9 = (bf16[480,128]{1,0:T(8,128)(2,1)S(1)}, bf16[480,128]{1,0:T(8,128)(2,1)S(1)}, u32[]{:S(2)}, u32[]{:S(2)}) collective-permute-start(bf16[480,128]{1,0:T(8,128)(2,1)S(1)} %concatenate.19.refs_0_), channel_id=1, source_target_pairs={{0,2},{1,3},{2,0},{3,1},{4,6},{5,7},{6,4},{7,5},{8,10},{9,11},{10,... | collective-permute-start | bytes 368648 | tf_op jit(solution)/shard_map/ppermute | solution.py:635
  68.0 2.4 %collective-permute-done.10.refs_3_ = bf16[480,128]{1,0:T(8,128)(2,1)S(1)} collective-permute-done((bf16[480,128]{1,0:T(8,128)(2,1)S(1)}, bf16[480,128]{1,0:T(8,128)(2,1)S(1)}, u32[]{:S(2)}, u32[]{:S(2)}) %collective-permute-start.10) | collective-permute-done | bytes 122912 | tf_op jit(solution)/shard_map/ppermute | solution.py:635
  70.4 1.0 %collective-permute-done.8.refs_1_ = bf16[480,128]{1,0:T(8,128)(2,1)S(1)} collective-permute-done((bf16[480,128]{1,0:T(8,128)(2,1)S(1)}, bf16[480,128]{1,0:T(8,128)(2,1)S(1)}, u32[]{:S(2)}, u32[]{:S(2)}) %collective-permute-start.8) | collective-permute-done | bytes 122912 | tf_op jit(solution)/shard_map/ppermute | solution.py:635
  71.4 0.7 collective-permute-done.9.refs_2_
  72.2 2.1 %shard_map.323 = (f32[1,1]{1,0:T(1,128)}, f32[1,1]{1,0:T(1,128)}, f32[1,512]{1,0:T(1,128)}, f32[1,64,512]{2,1,0:T(8,128)}, f32[27,1,128]{2,1,0:T(1,128)}, /*inde...) custom-call(bf16[480,128]{1,0:T(8,128)(2,1)S(1)} %concatenate.19.ref, ...), custom_call_target="tpu_custom_call" | custom-call | tf_op jit(solution)/shard_map/pallas_call | solution.py:656
  (31 shorter events, 0.2 us)
Async XLA Ops:
  2.1 6.3 %collective-permute-start.2 = (bf16[1840,128]{1,0:T(8,128)(2,1)S(1)}, bf16[1840,128]{1,0:T(8,128)(2,1)S(1)}, u32[]{:S(2)}, u32[]{:S(2)}) collective-permute-start(bf16[1840,128]{1,0:T(8,128)(2,1)S(1)} %get-tuple-element.61.mine), channel_id=1, source_target_pairs={{0,16},{16,0},{1,17},{17,1},{2,18},{18,2},{3,19},{19,3},{4,20},{20... | collective-permute-start | bytes 1413128 | tf_op jit(solution)/shard_map/ppermute | solution.py:557
  2.6 5.8 %collective-permute-start = (bf16[48,128]{1,0:T(8,128)(2,1)S(1)}, bf16[48,128]{1,0:T(8,128)(2,1)S(1)}, u32[]{:S(2)}, u32[]{:S(2)}) collective-permute-start(bf16[48,128]{1,0:T(8,128)(2,1)S(1)} %get-tuple-element.59), channel_id=1, source_target_pairs={{0,1},{1,2},{2,3},{3,4},{4,5},{5,6},{6,7},{7,8},{8,9},{9,10},{10,1... | collective-permute-start | bytes 36872 | tf_op jit(solution)/shard_map/ppermute | solution.py:555
  7.0 0.7 collective-permute-start.1
  29.0 4.8 %collective-permute-start.3 = (bf16[1440,128]{1,0:T(8,128)(2,1)S(1)}, bf16[1440,128]{1,0:T(8,128)(2,1)S(1)}, u32[]{:S(2)}, u32[]{:S(2)}) collective-permute-start(bf16[1440,128]{1,0:T(8,128)(2,1)S(1)} %get-tuple-element.63), channel_id=1, source_target_pairs={{0,16},{16,0},{1,17},{17,1},{2,18},{18,2},{3,19},{19,3},{4,20},{20... | collective-permute-start | bytes 1105928 | tf_op jit(solution)/shard_map/ppermute | solution.py:604
  33.8 8.3 %copy-start.14 = (bf16[1440,128]{1,0:T(8,128)(2,1)}, bf16[1440,128]{1,0:T(8,128)(2,1)S(1)}, u32[]{:S(2)}) copy-start(bf16[1440,128]{1,0:T(8,128)(2,1)S(1)} %collective-permute-done.3._) | copy-start | bytes 1105924
  34.6 19.6 %all-to-all-start = ((bf16[16,88,128]{2,1,0:T(8,128)(2,1)}), bf16[16,88,128]{2,1,0:T(8,128)(2,1)S(1)}, u32[]{:S(2)}, u32[]{:S(2)}) async-start(bf16[16,88,128]{2,1,0:T(8,128)(2,1)} %bitcast.4), calls=%async_computation | async-start | bytes 720896 | tf_op jit(solution)/shard_map/all_to_all | solution.py:607
  42.0 30.0 %copy-start = (f32[1,1152,128]{2,1,0:T(8,128)S(1)}, f32[1,1152,128]{2,1,0:T(8,128)}, u32[]{:S(2)}) copy-start(f32[1,1152,128]{2,1,0:T(8,128)} %refs_12_.1) | copy-start | bytes 1769476
  42.1 30.0 %copy-start.1 = (f32[1,1152,128]{2,1,0:T(8,128)S(1)}, f32[1,1152,128]{2,1,0:T(8,128)}, u32[]{:S(2)}) copy-start(f32[1,1152,128]{2,1,0:T(8,128)} %refs_13_.1) | copy-start | bytes 1769476
  42.1 30.0 %copy-start.2 = (f32[1,1152,128]{2,1,0:T(8,128)S(1)}, f32[1,1152,128]{2,1,0:T(8,128)}, u32[]{:S(2)}) copy-start(f32[1,1152,128]{2,1,0:T(8,128)} %refs_14_.1) | copy-start | bytes 1769476
  42.1 30.0 %copy-start.3 = (f32[1,512,64]{1,2,0:T(8,128)S(1)}, f32[1,512,64]{1,2,0:T(8,128)}, u32[]{:S(2)}) copy-start(f32[1,512,64]{1,2,0:T(8,128)} %param.21) | copy-start | bytes 393220
  42.1 30.0 %copy-start.4 = (f32[1,128,64]{1,2,0:T(8,128)S(1)}, f32[1,128,64]{1,2,0:T(8,128)}, u32[]{:S(2)}) copy-start(f32[1,128,64]{1,2,0:T(8,128)} %param.25) | copy-start | bytes 98308
  42.1 30.0 %copy-start.5 = (f32[1,27,128]{2,0,1:T(1,128)S(1)}, f32[1,27,128]{2,0,1:T(1,128)}, u32[]{:S(2)}) copy-start(f32[1,27,128]{2,0,1:T(1,128)} %param.22) | copy-start | bytes 41476
  42.1 30.0 %copy-start.6 = (f32[1,128,64]{1,2,0:T(8,128)S(1)}, f32[1,128,64]{1,2,0:T(8,128)}, u32[]{:S(2)}) copy-start(f32[1,128,64]{1,2,0:T(8,128)} %param.26) | copy-start | bytes 98308
  42.1 30.0 %copy-start.7 = (f32[1,128,64]{1,2,0:T(8,128)S(1)}, f32[1,128,64]{1,2,0:T(8,128)}, u32[]{:S(2)}) copy-start(f32[1,128,64]{1,2,0:T(8,128)} %param.27) | copy-start | bytes 98308
  42.1 30.0 %copy-start.8 = (f32[1,27,128]{2,0,1:T(1,128)S(1)}, f32[1,27,128]{2,0,1:T(1,128)}, u32[]{:S(2)}) copy-start(f32[1,27,128]{2,0,1:T(1,128)} %param.23) | copy-start | bytes 41476
  42.2 30.0 %copy-start.9 = (f32[1,27,128]{2,0,1:T(1,128)S(1)}, f32[1,27,128]{2,0,1:T(1,128)}, u32[]{:S(2)}) copy-start(f32[1,27,128]{2,0,1:T(1,128)} %param.24) | copy-start | bytes 41476
  42.2 30.0 %copy-start.10 = (f32[1,512]{1,0:T(1,128)S(1)}, f32[1,512]{1,0:T(1,128)}, u32[]{:S(2)}) copy-start(f32[1,512]{1,0:T(1,128)} %refs_4_.1) | copy-start | bytes 6148
  42.2 30.0 %copy-start.11 = (f32[1,128,3]{1,0,2:T(1,128)S(1)}, f32[1,128,3]{1,0,2:T(1,128)}, u32[]{:S(2)}) copy-start(f32[1,128,3]{1,0,2:T(1,128)} %param.31) | copy-start | bytes 4612
  42.2 30.0 %copy-start.12 = (f32[1,128,3]{1,0,2:T(1,128)S(1)}, f32[1,128,3]{1,0,2:T(1,128)}, u32[]{:S(2)}) copy-start(f32[1,128,3]{1,0,2:T(1,128)} %param.32) | copy-start | bytes 4612
  42.2 30.0 %copy-start.13 = (f32[1,128,3]{1,0,2:T(1,128)S(1)}, f32[1,128,3]{1,0,2:T(1,128)}, u32[]{:S(2)}) copy-start(f32[1,128,3]{1,0,2:T(1,128)} %param.33) | copy-start | bytes 4612
  54.3 1.2 %collective-permute-start.4 = (bf16[96,128]{1,0:T(8,128)(2,1)S(1)}, bf16[96,128]{1,0:T(8,128)(2,1)S(1)}, u32[]{:S(2)}, u32[]{:S(2)}) collective-permute-start(bf16[96,128]{1,0:T(8,128)(2,1)S(1)} %get-tuple-element.74), channel_id=1, source_target_pairs={{0,16},{16,0},{1,17},{17,1},{2,18},{18,2},{3,19},{19,3},{4,20},{20... | collective-permute-start | bytes 73736 | tf_op jit(solution)/shard_map/ppermute | solution.py:625
  55.6 4.6 %collective-permute-start.5 = (bf16[216,128]{1,0:T(8,128)(2,1)S(1)}, bf16[216,128]{1,0:T(8,128)(2,1)S(1)}, u32[]{:S(2)}, u32[]{:S(2)}) collective-permute-start(bf16[216,128]{1,0:T(8,128)(2,1)S(1)} %concatenate.17), channel_id=1, source_target_pairs={{0,4},{1,5},{2,6},{3,7},{4,0},{5,1},{6,2},{7,3},{8,12},{9,13},{10,... | collective-permute-start | bytes 165896 | tf_op jit(solution)/shard_map/ppermute | solution.py:635
  56.7 7.5 %collective-permute-start.6 = (bf16[216,128]{1,0:T(8,128)(2,1)S(1)}, bf16[216,128]{1,0:T(8,128)(2,1)S(1)}, u32[]{:S(2)}, u32[]{:S(2)}) collective-permute-start(bf16[216,128]{1,0:T(8,128)(2,1)S(1)} %concatenate.17), channel_id=1, source_target_pairs={{0,8},{1,9},{2,10},{3,11},{4,12},{5,13},{6,14},{7,15},{8,0},{9,1},... | collective-permute-start | bytes 165896 | tf_op jit(solution)/shard_map/ppermute | solution.py:635
  57.8 6.3 %collective-permute-start.7 = (bf16[216,128]{1,0:T(8,128)(2,1)S(1)}, bf16[216,128]{1,0:T(8,128)(2,1)S(1)}, u32[]{:S(2)}, u32[]{:S(2)}) collective-permute-start(bf16[216,128]{1,0:T(8,128)(2,1)S(1)} %concatenate.17), channel_id=1, source_target_pairs={{0,12},{1,13},{2,14},{3,15},{4,8},{5,9},{6,10},{7,11},{8,4},{9,5},... | collective-permute-start | bytes 165896 | tf_op jit(solution)/shard_map/ppermute | solution.py:635
  64.5 5.9 %collective-permute-start.10 = (bf16[480,128]{1,0:T(8,128)(2,1)S(1)}, bf16[480,128]{1,0:T(8,128)(2,1)S(1)}, u32[]{:S(2)}, u32[]{:S(2)}) collective-permute-start(bf16[480,128]{1,0:T(8,128)(2,1)S(1)} %concatenate.19.refs_0_), channel_id=1, source_target_pairs={{0,3},{1,2},{2,1},{3,0},{4,7},{5,6},{6,5},{7,4},{8,11},{9,10},{10,... | collective-permute-start | bytes 368648 | tf_op jit(solution)/shard_map/ppermute | solution.py:635
  66.5 4.9 %collective-permute-start.8 = (bf16[480,128]{1,0:T(8,128)(2,1)S(1)}, bf16[480,128]{1,0:T(8,128)(2,1)S(1)}, u32[]{:S(2)}, u32[]{:S(2)}) collective-permute-start(bf16[480,128]{1,0:T(8,128)(2,1)S(1)} %concatenate.19.refs_0_), channel_id=1, source_target_pairs={{0,1},{1,0},{2,3},{3,2},{4,5},{5,4},{6,7},{7,6},{8,9},{9,8},{10,11... | collective-permute-start | bytes 368648 | tf_op jit(solution)/shard_map/ppermute | solution.py:635
  67.2 4.9 %collective-permute-start.9 = (bf16[480,128]{1,0:T(8,128)(2,1)S(1)}, bf16[480,128]{1,0:T(8,128)(2,1)S(1)}, u32[]{:S(2)}, u32[]{:S(2)}) collective-permute-start(bf16[480,128]{1,0:T(8,128)(2,1)S(1)} %concatenate.19.refs_0_), channel_id=1, source_target_pairs={{0,2},{1,3},{2,0},{3,1},{4,6},{5,7},{6,4},{7,5},{8,10},{9,11},{10,... | collective-permute-start | bytes 368648 | tf_op jit(solution)/shard_map/ppermute | solution.py:635

commit v3 on v2

--- a/solution.py
+++ b/solution.py
@@ -23,7 +23,7 @@
 R_ZT = R_ZN + 128
 R_OT = R_ZT + 64
 R_BT = R_OT + 16
-R_CODE = R_BT + 256
+PACKED = R_BT + 256
 BIG = TAPS + 256
 S_Z, S_E, S_O, S_X = 0, 64, 96, 112
 LATE, SMALL = 96, 128
@@ -55,40 +55,31 @@
     return ((dr // 2) * 3 + dc) * 16 + (dr % 2) * 8
 
 
-def pack_kernel(
-    image, mask, codes, count, total, enc, lat, dec, read,
-    tile, near, across, pack, code_rows, flat,
-):
+def rows_kernel(image, mask, codes, others, tile, near):
     level = lax.axis_index("level")
     batches, _, band, _ = image.shape
+
+    def fitted(code):
+        return jnp.where(code < 256, code, code - 512).astype(F32)
+
     for b in range(batches):
         base = b * band * 8
         shown = image[b].astype(F32)
         for c in range(3):
             tile[pl.ds(base + c, band, stride=8), :] = shown[c]
         tile[pl.ds(base + 3, band, stride=8), :] = mask[b].astype(F32)
-        code = codes[0, b]
-        code = jnp.where(code < 256, code, code - 512).astype(F32)
-        code_rows[b * band : (b + 1) * band] = code
-        tile[pl.ds(base + 4, band, stride=8), :] = code
-        for c in range(5, 8):
+        mine, theirs = fitted(codes[0, b]), fitted(others[0, b])
+        tile[pl.ds(base + 4, band, stride=8), :] = jnp.where(level == 1, mine, theirs)
+        tile[pl.ds(base + 5, band, stride=8), :] = jnp.where(level == 1, theirs, mine)
+        for c in range(6, 8):
             tile[pl.ds(base + c, band, stride=8), :] = jnp.zeros((band, W), F32)
-    ends = []
     for b in range(batches):
         row = jnp.where(level == 0, band - 2, 0)
         start = pl.multiple_of((b * band + row) * 8, 8)
         near[b * 16 : (b + 1) * 16] = tile[pl.ds(start, 16), :].astype(BF)
-        for r in range(2):
-            ends.append(
-                jnp.where(
-                    level == 0,
-                    code_rows[b * band + r : b * band + r + 1],
-                    code_rows[(b + 1) * band - 2 + r : (b + 1) * band - 1 + r],
-                )
-            )
-    fill = across.shape[0] - len(ends)
-    across[...] = jnp.concatenate(ends + [jnp.zeros((fill, W), F32)], 0).astype(BF)
-
+
+
+def pack_kernel(count, total, enc, lat, dec, read, pack, flat):
     pack[0:TAPS] = dec[0].astype(BF)
     flat[...] = jnp.zeros_like(flat)
     for t in range(9):
@@ -106,7 +97,6 @@
     for quarter in range(4):
         row = R_BT + (quarter % 2) * 128 + (quarter // 2) * 64
         pack[row : row + 64] = book[:, quarter * 128 : (quarter + 1) * 128].astype(BF)
-    pack[R_CODE : R_CODE + batches * band] = code_rows[...].astype(BF)
 
 
 def sides(v):
@@ -135,6 +125,44 @@
     return out, p + out * (2.0 - p)
 
 
+def one_hots(here):
+    ids = lax.broadcasted_iota(jnp.int32, (256, here.shape[1]), 0).astype(F32)
+    onehots, highs = [], []
+    for v in range(2):
+        code = here[4 + v : 5 + v]
+        high = code < 0.0
+        low = jnp.where(high, code + 256.0, code)
+        onehots.append(jnp.where(ids == low, 1.0, 0.0).astype(BF))
+        highs.append(high)
+    return onehots, highs
+
+
+def quantized(here, bt):
+    quants = []
+    for onehot, high, book in zip(*one_hots(here), bt):
+        both = dot(book, onehot)
+        quants.append(jnp.where(high, both[64:128], both[0:64]))
+    return jnp.concatenate(quants, 0)
+
+
+def books(mine, theirs, bottom):
+    a, b = (jnp.concatenate([pack[R_BT : R_BT + 128], pack[R_BT + 128 : R_BT + 256]], 1) for pack in (mine, theirs))
+    return jnp.where(bottom, a, b), jnp.where(bottom, b, a)
+
+
+def lookup_kernel(tile, mine, theirs, u_c, *, batches, rows):
+    level = lax.axis_index("level")
+    bt = books(mine, theirs, level == 1)
+
+    def batch(b, _):
+        first = b * 2 * rows + level * (rows - 2)
+        runs = [tile[pl.ds(pl.multiple_of((first + i) * 8, 8), 8), :] for i in range(rows + 2)]
+        u_c[:, at(b * (rows + 2), rows + 2)] = quantized(jnp.concatenate(runs, 1), bt).astype(BF)
+        return 0
+
+    lax.fori_loop(0, batches, batch, 0)
+
+
 def patches(x_s, row, n):
     return jnp.concatenate([x_s[dc, :, at(row + pair, n)] for pair in (0, 2) for dc in range(3)], 0)
 
@@ -166,9 +194,9 @@
 
 
 def step_kernel(
-    tile, near, across, mine, theirs,
+    tile, near, mine, theirs, u_c,
     keep_big, keep_small, send, h_out, slope_out, gap_out, da_out, x_out, dn_out, zn_out,
-    t_s, far_s, dt, et, zt, ot, on, bt, u_s, h_s, slope_s, gap_s, da_s, x_s, dn, zn, g_d, g_o, g_s, l_s, sems, fixed_sems,
+    t_s, dt, et, zt, ot, on, u_s, h_s, slope_s, gap_s, da_s, x_s, dn, zn, g_d, g_o, g_s, l_s, sems, fixed_sems,
     *, batches, rows,
 ):
     level, me, devices = lax.axis_index("level"), lax.axis_index("dp"), lax.axis_size("dp")
@@ -212,11 +240,7 @@
     )
     ot[...] = out_t.astype(BF)
     on[...] = (0.5 * out_t).T.astype(BF)
-    for half in range(2):
-        one, zero = pair(R_BT + half * 128, 128)
-        bt[0, :, half * 128 : (half + 1) * 128] = one
-        bt[1, :, half * 128 : (half + 1) * 128] = zero
-
+    bt = books(mine, theirs, bottom)
     fixed = [
         pltpu.make_async_copy(a, o, fixed_sems.at[n])
         for n, (a, o) in enumerate(((x_s, x_out), (dn, dn_out), (zn, zn_out)))
@@ -224,55 +248,34 @@
     fixed[1].start()
     fixed[2].start()
 
-    far_s[0 : batches * band] = theirs[R_CODE : R_CODE + batches * band].astype(F32)
-    far_s[batches * band : batches * band + across.shape[0]] = across[...].astype(F32)
     sub = lax.broadcasted_iota(jnp.int32, (8, W), 0)
-    own_sub = jnp.where(bottom, 4, 5)
-
-    def lay(b, e, shown, other):
-        code = shown[4:5]
-        t_s[b, e] = jnp.where(sub < 4, shown, jnp.where(sub == own_sub, code, other))
+    nothing = jnp.where((sub == 4) | (sub == 5), NOBODY, 0.0)
 
     def inner(i, _):
         b, e = i // (rows + 2), i % (rows + 2)
         row = b * band + level * (rows - 2) + e
-        lay(
-            b,
-            e + jnp.where(bottom, 0, 2),
-            tile[pl.ds(pl.multiple_of(row * 8, 8), 8), :],
-            far_s[pl.ds(row, 1), :],
-        )
+        t_s[b, e + jnp.where(bottom, 0, 2)] = tile[pl.ds(pl.multiple_of(row * 8, 8), 8), :]
         return 0
 
-    lax.fori_loop(0, batches * (rows + 2), inner, 0, unroll=2)
+    lax.fori_loop(0, batches * (rows + 2), inner, 0, unroll=6)
     for b in range(batches):
         both = near[b * 16 : (b + 1) * 16].astype(F32)
         for r in range(2):
-            row = batches * band + b * 2 + r
-            shown = jnp.where(valid > 0, both[r * 8 : (r + 1) * 8], jnp.where(sub == 4, NOBODY, 0.0))
-            other = jnp.where(valid > 0, far_s[row : row + 1], NOBODY)
-            lay(b, jnp.where(bottom, rows + 2 + r, r), shown, other)
+            shown = jnp.where(valid > 0, both[r * 8 : (r + 1) * 8], nothing)
+            t_s[b, jnp.where(bottom, rows + 2 + r, r)] = shown
 
     for ref in (g_d, g_o, g_s, l_s):
         ref[...] = jnp.zeros_like(ref)
 
-    def lookup(b, e, n):
-        here = jnp.concatenate([t_s[b, e + i] for i in range(n)], 1)
-        ids = lax.broadcasted_iota(jnp.int32, (256, n * W), 0).astype(F32)
-        quants, onehots, highs = [], [], []
-        for v in range(2):
-            code = here[4 + v : 5 + v]
-            high = code < 0.0
-            low = jnp.where(high, code + 256.0, code)
-            onehot = jnp.where(ids == low, 1.0, 0.0).astype(BF)
-            both = dot(bt[v], onehot)
-            quants.append(jnp.where(high, both[64:128], both[0:64]))
-            onehots.append(onehot)
-            highs.append(high)
-        u = jnp.concatenate(quants, 0)
+    def spread_rows(u, b, e, n):
         for k, view in enumerate(sides(u)):
             u_s[k, :, at(b * ext + e, n)] = view.astype(BF)
-        return here, u, onehots, highs
+
+    outer = jnp.where(bottom, rows + 2, 0)
+    here = jnp.concatenate([t_s[b, outer + r] for b in range(batches) for r in range(2)], 1)
+    u = quantized(here, bt)
+    for b in range(batches):
+        spread_rows(u[:, b * 2 * W : (b + 1) * 2 * W], b, outer, 2)
 
     pairs = ((h_s, h_out), (slope_s, slope_out), (gap_s, gap_out), (da_s, da_out))
 
@@ -283,9 +286,10 @@
         runs = [jnp.concatenate([t_s[b, e], t_s[b, e + 1]], 0) for e in range(1, rows + 3)]
         for dc, view in enumerate(sides(jnp.concatenate(runs, 1))):
             x_s[dc, :, at(b * (rows + 2), rows + 2)] = view.astype(BF)
-        here, u, onehots, highs = lookup(b, 0, ext)
-        inner = slice(2 * W, (2 + rows) * W)
-        here, u = here[:, inner], u[:, inner]
+        spread_rows(u_c[:, at(b * (rows + 2), rows + 2)].astype(F32), b, jnp.where(bottom, 0, 2), rows + 2)
+        u = u_c[:, at(b * (rows + 2) + 2 * level, rows)].astype(F32)
+        here = jnp.concatenate([t_s[b, 2 + i] for i in range(rows)], 1)
+        onehots, highs = one_hots(here)
         h, slope = silu_parts(dot(et[:, 0:PATCH], patches(x_s, b * (rows + 2), rows)))
         slope_s[b] = slope
         h = h.astype(BF)
@@ -300,7 +304,7 @@
         row = lax.broadcasted_iota(jnp.int32, (16, rows * W), 0)
         for v in range(2):
             part_z = z[v * 64 : v * 64 + 64]
-            high = highs[v][:, inner]
+            high = highs[v]
             low_k = jnp.where(high, 0.0, k)
             high_k = jnp.where(high, k, 0.0)
             left = jnp.concatenate(
@@ -311,7 +315,7 @@
                 ],
                 0,
             ).astype(BF)
-            g_s[v] += dot(left, onehots[v][:, inner], NT)
+            g_s[v] += dot(left, onehots[v], NT)
         for copy in leave(b, range(3)):
             copy.start()
         return 0
@@ -335,10 +339,10 @@
         dy = (2.0 * kept).astype(BF)
         da = (dot(on[...], dy) * slope).astype(BF)
         da_s[b] = da
+        leave(b, [3])[0].start()
         l_s[128:144] += fold((kept * diff)[:, inner], 256)
-        g_o[...] += dot(dy[:, inner], g[:, inner], NT)
+        g_o[...] += dot(g[:, inner], dy[:, inner], NT)
         g_d[...] += dot(u[:, inner], da[:, inner], NT)
-        leave(b, [3])[0].start()
         return 0
 
     lax.fori_loop(0, batches, decode, 0)
@@ -353,11 +357,12 @@
     if pad > BIG:
         keep_big[BIG:pad] = jnp.zeros((pad - BIG, W), F32)
         send[BIG:pad] = jnp.zeros((pad - BIG, W), BF)
+    readouts = g_o[...].T
     blank = jnp.zeros((8, 128), F32)
     give(
         S_O,
-        jnp.concatenate([g_o[0:8, 0:128], blank], 0),
-        jnp.concatenate([g_o[8:16, 128:256], blank], 0),
+        jnp.concatenate([readouts[0:8, 0:128], blank], 0),
+        jnp.concatenate([readouts[8:16, 128:256], blank], 0),
         keep_small,
         pad,
         LATE,
@@ -424,20 +429,24 @@
 
 
 def update_kernel(
-    *refs, stages, start
+    *refs, stages, start, other
 ):
     (parts, refs) = refs[:stages], refs[stages:]
     (count, total, ew, e1, e2, zw, z1, z2, dw, d1, d2, ow, o1, o2,
      loss_out, valid_out, count_out, total_out,
      em, es, ep, ec, zm, zs, zp, zc, dm, ds, dp, dc, om, os, op, oc, big, rows) = refs
     share = big.shape[0] // stages
-    index = (lax.axis_index("dp") >> start) & (stages - 1)
+    top = lax.axis_index("level") == 0
+    index = (lax.axis_index("dp") >> jnp.where(top, start, other)) & (stages - 1)
     size = big.shape[0] // lax.axis_size("dp")
     small = jnp.zeros((SMALL, W), F32)
     for n, ref in enumerate(parts):
         value = ref[0:share].astype(F32)
         for h in range(share // size):
-            row = pl.multiple_of((h * stages + (index ^ n)) * size, 8)
+            place = h * stages + (index ^ n)
+            if other != start:
+                place = jnp.where(top, place, (index ^ n) * (share // size) + h)
+            row = pl.multiple_of(place * size, 8)
             big[pl.ds(row, size), :] = value[h * size : (h + 1) * size]
         small = small + ref[share : share + SMALL].astype(F32)
     exact = sum(small[S_X + EXACT * i : S_X + EXACT * (i + 1)] for i in range(3))
@@ -489,8 +498,8 @@
     return [k << start for k in range(1, 1 << width)]
 
 
-def xor_pairs(devices, by):
-    return [(i, i ^ by) for i in range(devices)]
+def xor_pairs(devices, by, other):
+    return [(i, i ^ by) for i in range(devices)] + [(devices + i, devices + (i ^ other)) for i in range(devices)]
 
 
 def lowered(value):
@@ -534,28 +543,43 @@
     def outside(*items):
         return [pltpu.with_memory_space_constraint(item, pltpu.HBM) for item in items]
 
-    packed = R_CODE + batches * band
-    tile, near, across, pack = pl.pallas_call(
+    def inside_vmem(item):
+        return pltpu.with_memory_space_constraint(item, pltpu.VMEM)
+
+    swap = [(0, 1), (1, 0)]
+    others = lax.ppermute(codes, "level", swap)
+    weights = outside(ema_count, ema_sum, encoder_weight, latent_weight, decoder_weight, readout_weight)
+    pack = pl.pallas_call(
         pack_kernel,
-        out_shape=[
-            pltpu.VMEM((batches * band * 8, W), F32),
-            pltpu.VMEM((batches * 16, W), BF),
-            pltpu.VMEM((16, W), BF),
-            pltpu.VMEM((packed, W), BF),
-        ],
-        in_specs=[VMEM] * 9,
-        out_specs=[VMEM] * 4,
-        scratch_shapes=[pltpu.VMEM((batches * band, W), F32), pltpu.VMEM((128, 128), F32)],
+        out_shape=pltpu.VMEM((PACKED, W), BF),
+        in_specs=[VMEM] * 6,
+        out_specs=VMEM,
+        scratch_shapes=[pltpu.VMEM((128, 128), F32)],
         compiler_params=limit(56),
-    )(*outside(image, mask, codes, ema_count, ema_sum, encoder_weight, latent_weight, decoder_weight, readout_weight))
+    )(*weights)
+    others, pack = lax.optimization_barrier((others, pack))
+    tile, near = pl.pallas_call(
+        rows_kernel,
+        out_shape=[pltpu.VMEM((batches * band * 8, W), F32), pltpu.VMEM((batches * 16, W), BF)],
+        in_specs=[VMEM] * 4,
+        out_specs=[VMEM] * 2,
+        compiler_params=limit(56),
+    )(*outside(image, mask, codes), others)
 
     both = ("level", "dp")
-    same = [(d - 1, d) for d in range(1, devices)] + [(devices + d + 1, devices + d) for d in range(devices - 1)]
-    cross = [(devices + d - 1, d) for d in range(1, devices)] + [(d + 1, devices + d) for d in range(devices - 1)]
-    near = lax.ppermute(near, both, same)
-    across = lax.ppermute(across, both, cross)
-    theirs = lax.ppermute(pack, "level", [(0, 1), (1, 0)])
-
+    inside = [d for d in range(1, devices) if (d + 1) * band % CROP != 0]
+    pairs = [(d - 1, d) for d in inside] + [(devices + d, devices + d - 1) for d in inside]
+    near = lax.ppermute(near, both, pairs)
+    theirs = lax.ppermute(pack, "level", swap)
+
+    u_c = pl.pallas_call(
+        functools.partial(lookup_kernel, batches=batches, rows=rows),
+        out_shape=pltpu.VMEM((128, batches * (rows + 2) * W), BF),
+        in_specs=[VMEM] * 3,
+        out_specs=VMEM,
+        compiler_params=limit(40),
+        cost_estimate=pl.CostEstimate(flops=3 << 30, bytes_accessed=1 << 20, transcendentals=0),
+    )(*[inside_vmem(item) for item in (tile, pack, theirs)])
     ext = rows + 4
     pixels = batches * rows * W
     framed = batches * (rows + 2) * W
@@ -581,26 +605,23 @@
         out_specs=[VMEM] * 3 + [AWAY] * 7,
         scratch_shapes=[
             pltpu.VMEM((batches, ext, 8, W), F32),
-            pltpu.VMEM((batches * band + 16, W), F32),
             pltpu.VMEM((256, TAPS), BF),
             pltpu.VMEM((256, 128), BF),
             pltpu.VMEM((128, 256), BF),
             pltpu.VMEM((16, 256), BF),
             pltpu.VMEM((256, 16), BF),
-            pltpu.VMEM((2, 128, 256), BF),
             pltpu.VMEM((3, 128, batches * ext * W), BF),
             *[pltpu.VMEM(*item) for item in held + fixed],
             pltpu.VMEM((TAPS, 256), F32),
-            pltpu.VMEM((16, 256), F32),
+            pltpu.VMEM((256, 16), F32),
             pltpu.VMEM((2, 144, 256), F32),
             pltpu.VMEM((144, 256), F32),
             pltpu.SemaphoreType.DMA((4, batches)),
             pltpu.SemaphoreType.DMA((3,)),
         ],
         compiler_params=limit(STEP_MIB),
-    )(*[pltpu.with_memory_space_constraint(item, pltpu.VMEM) for item in (tile, near, across, pack, theirs)])
-
-    swap = [(0, 1), (1, 0)]
+    )(*[inside_vmem(item) for item in (tile, near, pack, theirs, u_c)])
+
     got = lax.ppermute(send, "level", swap)
     early = sum_small([early, got[padded:]], S_X - LATE)
     big = (keep + got[:padded].astype(F32)).astype(BF)
@@ -628,11 +649,15 @@
 
     big = jnp.sum(big.astype(F32), 0).astype(BF)[None]
     stages = radices(devices)
+    crossed = len(stages) == 2 and stages[0][1] == stages[1][1]
     for number, (start, width_bits) in enumerate(reversed(stages)):
         count = 1 << width_bits
-        index = (me >> start) & (count - 1)
+        other = stages[number][0] if crossed else start
+        index = (me >> jnp.where(lax.axis_index("level") == 0, start, other)) & (count - 1)
         payload = jnp.concatenate([big.reshape(-1, W), small], 0)
-        parts = [payload] + [lax.ppermute(payload, "dp", xor_pairs(devices, k << start)) for k in range(1, count)]
+        parts = [payload] + [
+            lax.ppermute(payload, both, xor_pairs(devices, k << start, k << other)) for k in range(1, count)
+        ]
         if number == len(stages) - 1:
             break
         high = big.shape[0]
@@ -654,7 +679,7 @@
         copy = item.shape if item.shape[0] == 1 else (1, item.shape[0], item.shape[2])
         outs += [jax.ShapeDtypeStruct(item.shape, F32)] * 3 + [jax.ShapeDtypeStruct(copy, BF)]
     result = pl.pallas_call(
-        functools.partial(update_kernel, stages=len(parts), start=start),
+        functools.partial(update_kernel, stages=len(parts), start=start, other=other),
         out_shape=outs,
         in_specs=[VMEM] * (len(parts) + len(state)),
         out_specs=[SMEM] * 2 + [VMEM] * (len(outs) - 2),

time: 74.7 us -> 72.5 us (0.971)
  starting transfers between devices: 24.4 us -> 20.7 us
  Pallas kernels: 34 us -> 35.4 us
    ppermute x2, starting transfers between devices: 3.48 us -> 0.07 us  [local(): got = lax.ppermute(send, 'level', swap)]
    pallas_call x1 -> x3, Pallas kernels: 1.41 us -> 3.83 us  [the longest x1 1.51 us: local(): pl.pallas_call(functools.partial(lookup_kernel, batches=batches, rows=row...]
    pallas_call x1, Pallas kernels: 20.6 us -> 19.6 us  [local(): pl.pallas_call(functools.partial(step_kernel, batches=batches, rows=rows)...]
    ppermute x9, waiting for transfers between devices: 8.68 us -> 7.88 us  [the longest x6 7.87 us: local(): lax.ppermute(payload, both, xor_pairs(devices, k << start, k << other))]
  transfers between devices with their start and end apart: 12 -> 12, of which waited for: 8 -> 8; matrix products, arithmetic and copies ran while one was open for 0% -> 0% of each run, Pallas kernels for 13% -> 19%
where the time goes in v3:
time: 72.5 us; the launch traced here: 72.2 us
  Pallas kernels  35.4 us (49%)
  starting transfers between devices  20.7 us (29%)
  waiting for transfers between devices  12.8 us (18%)
  between operations  1.23 us (2%)
  local copies, waits for them, and re-layouts  1.13 us (2%)
  other arithmetic  0.99 us (1%)
    pallas_call x1, Pallas kernels, local(): pl.pallas_call(functools.partial(step_kernel, batches=batches, rows=rows)...  19.6 us
    pallas_call x1, Pallas kernels, local(): pl.pallas_call(functools.partial(back_kernel, batches=batches, rows=rows)...  9.84 us
    ppermute x6, starting transfers between devices, local(): lax.ppermute(payload, both, xor_pairs(devices, k << start, k << other))  7.98 us
    ppermute x6, waiting for transfers between devices, local(): lax.ppermute(payload, both, xor_pairs(devices, k << start, k << other))  7.87 us
    all_to_all x1, starting transfers between devices, local(): big = lax.all_to_all(big.reshape(devices, size, W), 'dp', 0, 0)  7.49 us
    ppermute x1, starting transfers between devices, local(): near = lax.ppermute(near, both, pairs)  4.48 us
    ppermute x2, waiting for transfers between devices, local(): got = lax.ppermute(send, 'level', swap)  2.76 us
    all_to_all x1, waiting for transfers between devices, local(): big = lax.all_to_all(big.reshape(devices, size, W), 'dp', 0, 0)  2.19 us
  transfers between devices with their start and end apart: 12, of which 8 were waited for; matrix products, arithmetic and copies ran while one was open for 0% of the time, Pallas kernels for 19%

profile of v3, /device:TPU:0, one launch (start us, length us, event | category | flops | bytes accessed | tf_op | source)
XLA Modules:
  0.0 72.2 jit_solution(15539376849031702149)
XLA Ops:
  0.7 0.5 collective-permute-start
  1.2 1.3 %shard_map.320.mine = bf16[1744,128]{1,0:T(8,128)(2,1)S(1)} custom-call(f32[1,512]{1,0:T(1,128)} %refs_4_.1, f32[1,64,512]{2,1,0:T(8,128)} %bitcast.40, f32[27,1,128]{2,1,0:T(1,128)} %bitcast.44, f32[1,64,128]{2,1,0:T(8,128)} %bitcast.42, f32[1,1152,128]{2,1,0:T(8,128)} %refs_12_.1, f32[3,1,128]{2,1,0:T(1,128)} %bitcast.50), custom_call_target="tpu_custom_call" | custom-call | tf_op jit(solution)/shard_map/pallas_call | solution.py:552
  2.5 0.0 collective-permute-done.others
  2.5 0.0 copy-start.15
  2.5 0.1 collective-permute-start.2
  2.7 0.5 copy-done.15
  3.1 1.0 %shard_map.321 = (f32[768,128]{1,0:T(8,128)S(1)}, bf16[48,128]{1,0:T(8,128)(2,1)S(1)}) custom-call(bf16[3,3,32,128]{3,2,1,0:T(8,128)(2,1)} %image.1, s32[3,32,128]{2,1,0:T(8,128)} %mask.1, s32[1,3,32,128]{3,2,1,0:T(8,128)} %codes.1, s32[1,3,32,128]{3,2,1,0:T(8,128)} %copy-done.15), custom_call_target="tpu_custom_call" | custom-call | tf_op jit(solution)/shard_map/pallas_call | solution.py:561
  4.1 4.5 %collective-permute-start.1 = (bf16[48,128]{1,0:T(8,128)(2,1)S(1)}, bf16[48,128]{1,0:T(8,128)(2,1)S(1)}, u32[]{:S(2)}, u32[]{:S(2)}) collective-permute-start(bf16[48,128]{1,0:T(8,128)(2,1)S(1)} %get-tuple-element.60), channel_id=1, source_target_pairs={{0,1},{1,2},{3,4},{4,5},{5,6},{7,8},{8,9},{9,10},{11,12},{12,13},{... | collective-permute-start | bytes 36872 | tf_op jit(solution)/shard_map/ppermute | solution.py:572
  8.6 0.0 collective-permute-done.2.theirs
  8.6 1.5 %shard_map.322.u_c = bf16[128,6912]{1,0:T(8,128)(2,1)S(1)} custom-call(f32[768,128]{1,0:T(8,128)S(1)} %get-tuple-element.59.tile, bf16[1744,128]{1,0:T(8,128)(2,1)S(1)} %shard_map.320.mine, bf16[1744,128]{1,0:T(8,128)(2,1)S(1)} %collective-permute-done.2.theirs), custom_call_target="tpu_custom_call" | custom-call | flops 3221225472 | bytes 1048576 | tf_op jit(solution)/shard_map/pallas_call | solution.py:575
  10.2 19.6 %shard_map.323 = (f32[1408,128]{1,0:T(8,128)S(1)}, bf16[32,128]{1,0:T(8,128)(2,1)S(1)}, bf16[1440,128]{1,0:T(8,128)(2,1)S(1)}, bf16[3,256,2048]{2,1,0:T(8,128)(2...) custom-call(f32[768,128]{1,0:T(8,128)S(1)} %get-tuple-element.59.til, ...), custom_call_target="tpu_custom_call" | custom-call | tf_op jit(solution)/shard_map/pallas_call | solution.py:596
  29.8 0.1 collective-permute-start.3
  29.9 1.6 %collective-permute-done.3._ = bf16[1440,128]{1,0:T(8,128)(2,1)S(1)} collective-permute-done((bf16[1440,128]{1,0:T(8,128)(2,1)S(1)}, bf16[1440,128]{1,0:T(8,128)(2,1)S(1)}, u32[]{:S(2)}, u32[]{:S(2)}) %collective-permute-start.3) | collective-permute-done | bytes 368672 | tf_op jit(solution)/shard_map/ppermute | solution.py:625
  31.5 0.9 %add_convert_fusion = bf16[1408,128]{1,0:T(8,128)(2,1)} fusion(f32[1408,128]{1,0:T(8,128)S(1)} %get-tuple-element.62, bf16[1440,128]{1,0:T(8,128)(2,1)S(1)} %collective-permute-done.3._), kind=kLoop, calls=%fused_computation | loop fusion | flops 540672 | bytes 1441792 | tf_op jit(solution)/shard_map/convert_element_type | solution.py:627
  32.4 7.5 %all-to-all-start = ((bf16[16,88,128]{2,1,0:T(8,128)(2,1)}), bf16[16,88,128]{2,1,0:T(8,128)(2,1)S(1)}, u32[]{:S(2)}, u32[]{:S(2)}) async-start(bf16[16,88,128]{2,1,0:T(8,128)(2,1)} %bitcast.4), calls=%async_computation | async-start | bytes 720896 | tf_op jit(solution)/shard_map/all_to_all | solution.py:628
  39.9 0.0 copy-start
  39.9 0.0 copy-start.1
  40.0 0.0 copy-start.2
  40.0 0.0 copy-start.3
  40.0 0.0 copy-start.4
  40.0 0.0 copy-start.5
  40.0 0.0 copy-start.6
  40.0 0.0 copy-start.7
  40.0 0.0 copy-start.8
  40.0 0.0 copy-start.9
  40.1 0.0 copy-start.10
  40.1 0.0 copy-start.11
  40.1 0.0 copy-start.12
  40.1 0.0 copy-start.13
  40.1 9.8 %shard_map.324 = (bf16[96,128]{1,0:T(8,128)(2,1)S(1)}, bf16[96,128]{1,0:T(8,128)(2,1)S(1)}) custom-call(bf16[3,256,2048]{2,1,0:T(8,128)(2,1)} %get-tuple-element.64.h_in, f32[3,256,2048]{2,1,0:T(8,128)} %get-tuple-element.65.slope_in, f32[3,128,2048]{2,1,0:T(8,128)} %get-tuple-element.66.gap_in, bf16[3,256,2304]{2,1,0:T(8,128)(2,1)} %get-tuple-element.67.da_in, ...), custom_call_target="tpu_custom_call" | custom-call | flops 4831838208 | bytes 1048576 | tf_op jit(solution)/shard_map/pallas_call | solution.py:630
  49.9 2.2 %all-to-all-done = bf16[16,88,128]{2,1,0:T(8,128)(2,1)S(1)} async-done(((bf16[16,88,128]{2,1,0:T(8,128)(2,1)}), bf16[16,88,128]{2,1,0:T(8,128)(2,1)S(1)}, u32[]{:S(2)}, u32[]{:S(2)}) %all-to-all-start) | async-done | bytes 360480 | tf_op jit(solution)/shard_map/all_to_all | solution.py:628
  52.2 0.1 reduce_sum.12
  52.2 1.1 %collective-permute-done.4 = bf16[96,128]{1,0:T(8,128)(2,1)S(1)} collective-permute-done((bf16[96,128]{1,0:T(8,128)(2,1)S(1)}, bf16[96,128]{1,0:T(8,128)(2,1)S(1)}, u32[]{:S(2)}, u32[]{:S(2)}) %collective-permute-start.4) | collective-permute-done | bytes 24608 | tf_op jit(solution)/shard_map/ppermute | solution.py:646
  53.4 0.2 concatenate.17
  53.5 1.1 %collective-permute-start.5 = (bf16[216,128]{1,0:T(8,128)(2,1)S(1)}, bf16[216,128]{1,0:T(8,128)(2,1)S(1)}, u32[]{:S(2)}, u32[]{:S(2)}) collective-permute-start(bf16[216,128]{1,0:T(8,128)(2,1)S(1)} %concatenate.17), channel_id=1, source_target_pairs={{0,4},{1,5},{2,6},{3,7},{4,0},{5,1},{6,2},{7,3},{8,12},{9,13},{10,... | collective-permute-start | bytes 165896 | tf_op jit(solution)/shard_map/ppermute | solution.py:659
  54.6 1.1 %collective-permute-start.6 = (bf16[216,128]{1,0:T(8,128)(2,1)S(1)}, bf16[216,128]{1,0:T(8,128)(2,1)S(1)}, u32[]{:S(2)}, u32[]{:S(2)}) collective-permute-start(bf16[216,128]{1,0:T(8,128)(2,1)S(1)} %concatenate.17), channel_id=1, source_target_pairs={{0,8},{1,9},{2,10},{3,11},{4,12},{5,13},{6,14},{7,15},{8,0},{9,1},... | collective-permute-start | bytes 165896 | tf_op jit(solution)/shard_map/ppermute | solution.py:659
  55.7 2.2 %collective-permute-start.7 = (bf16[216,128]{1,0:T(8,128)(2,1)S(1)}, bf16[216,128]{1,0:T(8,128)(2,1)S(1)}, u32[]{:S(2)}, u32[]{:S(2)}) collective-permute-start(bf16[216,128]{1,0:T(8,128)(2,1)S(1)} %concatenate.17), channel_id=1, source_target_pairs={{0,12},{1,13},{2,14},{3,15},{4,8},{5,9},{6,10},{7,11},{8,4},{9,5},... | collective-permute-start | bytes 165896 | tf_op jit(solution)/shard_map/ppermute | solution.py:659
  58.0 0.1 concatenate.18
  58.1 2.1 %collective-permute-done.6 = bf16[216,128]{1,0:T(8,128)(2,1)S(1)} collective-permute-done((bf16[216,128]{1,0:T(8,128)(2,1)S(1)}, bf16[216,128]{1,0:T(8,128)(2,1)S(1)}, u32[]{:S(2)}, u32[]{:S(2)}) %collective-permute-start.6) | collective-permute-done | bytes 55328 | tf_op jit(solution)/shard_map/ppermute | solution.py:659
  60.3 1.4 %collective-permute-done.7 = bf16[216,128]{1,0:T(8,128)(2,1)S(1)} collective-permute-done((bf16[216,128]{1,0:T(8,128)(2,1)S(1)}, bf16[216,128]{1,0:T(8,128)(2,1)S(1)}, u32[]{:S(2)}, u32[]{:S(2)}) %collective-permute-start.7) | collective-permute-done | bytes 55328 | tf_op jit(solution)/shard_map/ppermute | solution.py:659
  61.8 0.2 concatenate.19.refs_0_
  62.0 2.4 %collective-permute-start.10 = (bf16[480,128]{1,0:T(8,128)(2,1)S(1)}, bf16[480,128]{1,0:T(8,128)(2,1)S(1)}, u32[]{:S(2)}, u32[]{:S(2)}) collective-permute-start(bf16[480,128]{1,0:T(8,128)(2,1)S(1)} %concatenate.19.refs_0_), channel_id=1, source_target_pairs={{0,3},{1,2},{2,1},{3,0},{4,7},{5,6},{6,5},{7,4},{8,11},{9,10},{10,... | collective-permute-start | bytes 368648 | tf_op jit(solution)/shard_map/ppermute | solution.py:659
  64.4 0.6 collective-permute-start.8
  65.0 0.6 collective-permute-start.9
  65.5 2.3 %collective-permute-done.10.refs_3_ = bf16[480,128]{1,0:T(8,128)(2,1)S(1)} collective-permute-done((bf16[480,128]{1,0:T(8,128)(2,1)S(1)}, bf16[480,128]{1,0:T(8,128)(2,1)S(1)}, u32[]{:S(2)}, u32[]{:S(2)}) %collective-permute-start.10) | collective-permute-done | bytes 122912 | tf_op jit(solution)/shard_map/ppermute | solution.py:659
  67.8 1.5 %collective-permute-done.8.refs_1_ = bf16[480,128]{1,0:T(8,128)(2,1)S(1)} collective-permute-done((bf16[480,128]{1,0:T(8,128)(2,1)S(1)}, bf16[480,128]{1,0:T(8,128)(2,1)S(1)}, u32[]{:S(2)}, u32[]{:S(2)}) %collective-permute-start.8) | collective-permute-done | bytes 122912 | tf_op jit(solution)/shard_map/ppermute | solution.py:659
  69.3 0.6 collective-permute-done.9.refs_2_
  70.0 2.1 %shard_map.325 = (f32[1,1]{1,0:T(1,128)}, f32[1,1]{1,0:T(1,128)}, f32[1,512]{1,0:T(1,128)}, f32[1,64,512]{2,1,0:T(8,128)}, f32[27,1,128]{2,1,0:T(1,128)}, /*inde...) custom-call(bf16[480,128]{1,0:T(8,128)(2,1)S(1)} %concatenate.19.ref, ...), custom_call_target="tpu_custom_call" | custom-call | tf_op jit(solution)/shard_map/pallas_call | solution.py:681
  (35 shorter events, 0.2 us)
Async XLA Ops:
  0.7 1.9 %collective-permute-start = (s32[1,3,32,128]{3,2,1,0:T(8,128)}, s32[1,3,32,128]{3,2,1,0:T(8,128)S(1)}, u32[]{:S(2)}, u32[]{:S(2)}) collective-permute-start(s32[1,3,32,128]{3,2,1,0:T(8,128)} %codes.1), channel_id=1, source_target_pairs={{0,16},{16,0},{1,17},{17,1},{2,18},{18,2},{3,19},{19,3},{4,20},{20... | collective-permute-start | bytes 147464 | tf_op jit(solution)/shard_map/ppermute | solution.py:550
  2.5 0.6 copy-start.15
  2.5 6.1 %collective-permute-start.2 = (bf16[1744,128]{1,0:T(8,128)(2,1)S(1)}, bf16[1744,128]{1,0:T(8,128)(2,1)S(1)}, u32[]{:S(2)}, u32[]{:S(2)}) collective-permute-start(bf16[1744,128]{1,0:T(8,128)(2,1)S(1)} %shard_map.320.mine), channel_id=1, source_target_pairs={{0,16},{16,0},{1,17},{17,1},{2,18},{18,2},{3,19},{19,3},{4,20},{20... | collective-permute-start | bytes 1339400 | tf_op jit(solution)/shard_map/ppermute | solution.py:573
  4.1 6.0 %collective-permute-start.1 = (bf16[48,128]{1,0:T(8,128)(2,1)S(1)}, bf16[48,128]{1,0:T(8,128)(2,1)S(1)}, u32[]{:S(2)}, u32[]{:S(2)}) collective-permute-start(bf16[48,128]{1,0:T(8,128)(2,1)S(1)} %get-tuple-element.60), channel_id=1, source_target_pairs={{0,1},{1,2},{3,4},{4,5},{5,6},{7,8},{8,9},{9,10},{11,12},{12,13},{... | collective-permute-start | bytes 36872 | tf_op jit(solution)/shard_map/ppermute | solution.py:572
  29.8 1.8 %collective-permute-start.3 = (bf16[1440,128]{1,0:T(8,128)(2,1)S(1)}, bf16[1440,128]{1,0:T(8,128)(2,1)S(1)}, u32[]{:S(2)}, u32[]{:S(2)}) collective-permute-start(bf16[1440,128]{1,0:T(8,128)(2,1)S(1)} %get-tuple-element.63), channel_id=1, source_target_pairs={{0,16},{16,0},{1,17},{17,1},{2,18},{18,2},{3,19},{19,3},{4,20},{20... | collective-permute-start | bytes 1105928 | tf_op jit(solution)/shard_map/ppermute | solution.py:625
  31.5 8.4 %copy-start.14 = (bf16[1440,128]{1,0:T(8,128)(2,1)}, bf16[1440,128]{1,0:T(8,128)(2,1)S(1)}, u32[]{:S(2)}) copy-start(bf16[1440,128]{1,0:T(8,128)(2,1)S(1)} %collective-permute-done.3._) | copy-start | bytes 1105924
  32.4 19.7 %all-to-all-start = ((bf16[16,88,128]{2,1,0:T(8,128)(2,1)}), bf16[16,88,128]{2,1,0:T(8,128)(2,1)S(1)}, u32[]{:S(2)}, u32[]{:S(2)}) async-start(bf16[16,88,128]{2,1,0:T(8,128)(2,1)} %bitcast.4), calls=%async_computation | async-start | bytes 720896 | tf_op jit(solution)/shard_map/all_to_all | solution.py:628
  39.9 29.9 %copy-start = (f32[1,1152,128]{2,1,0:T(8,128)S(1)}, f32[1,1152,128]{2,1,0:T(8,128)}, u32[]{:S(2)}) copy-start(f32[1,1152,128]{2,1,0:T(8,128)} %refs_12_.1) | copy-start | bytes 1769476
  39.9 29.9 %copy-start.1 = (f32[1,1152,128]{2,1,0:T(8,128)S(1)}, f32[1,1152,128]{2,1,0:T(8,128)}, u32[]{:S(2)}) copy-start(f32[1,1152,128]{2,1,0:T(8,128)} %refs_13_.1) | copy-start | bytes 1769476
  40.0 29.9 %copy-start.2 = (f32[1,1152,128]{2,1,0:T(8,128)S(1)}, f32[1,1152,128]{2,1,0:T(8,128)}, u32[]{:S(2)}) copy-start(f32[1,1152,128]{2,1,0:T(8,128)} %refs_14_.1) | copy-start | bytes 1769476
  40.0 29.9 %copy-start.3 = (f32[1,512,64]{1,2,0:T(8,128)S(1)}, f32[1,512,64]{1,2,0:T(8,128)}, u32[]{:S(2)}) copy-start(f32[1,512,64]{1,2,0:T(8,128)} %param.21) | copy-start | bytes 393220
  40.0 29.9 %copy-start.4 = (f32[1,128,64]{1,2,0:T(8,128)S(1)}, f32[1,128,64]{1,2,0:T(8,128)}, u32[]{:S(2)}) copy-start(f32[1,128,64]{1,2,0:T(8,128)} %param.25) | copy-start | bytes 98308
  40.0 29.9 %copy-start.5 = (f32[1,27,128]{2,0,1:T(1,128)S(1)}, f32[1,27,128]{2,0,1:T(1,128)}, u32[]{:S(2)}) copy-start(f32[1,27,128]{2,0,1:T(1,128)} %param.22) | copy-start | bytes 41476
  40.0 29.9 %copy-start.6 = (f32[1,128,64]{1,2,0:T(8,128)S(1)}, f32[1,128,64]{1,2,0:T(8,128)}, u32[]{:S(2)}) copy-start(f32[1,128,64]{1,2,0:T(8,128)} %param.26) | copy-start | bytes 98308
  40.0 29.9 %copy-start.7 = (f32[1,128,64]{1,2,0:T(8,128)S(1)}, f32[1,128,64]{1,2,0:T(8,128)}, u32[]{:S(2)}) copy-start(f32[1,128,64]{1,2,0:T(8,128)} %param.27) | copy-start | bytes 98308
  40.0 29.9 %copy-start.8 = (f32[1,27,128]{2,0,1:T(1,128)S(1)}, f32[1,27,128]{2,0,1:T(1,128)}, u32[]{:S(2)}) copy-start(f32[1,27,128]{2,0,1:T(1,128)} %param.23) | copy-start | bytes 41476
  40.0 29.9 %copy-start.9 = (f32[1,27,128]{2,0,1:T(1,128)S(1)}, f32[1,27,128]{2,0,1:T(1,128)}, u32[]{:S(2)}) copy-start(f32[1,27,128]{2,0,1:T(1,128)} %param.24) | copy-start | bytes 41476
  40.1 29.9 %copy-start.10 = (f32[1,512]{1,0:T(1,128)S(1)}, f32[1,512]{1,0:T(1,128)}, u32[]{:S(2)}) copy-start(f32[1,512]{1,0:T(1,128)} %refs_4_.1) | copy-start | bytes 6148
  40.1 29.9 %copy-start.11 = (f32[1,128,3]{1,0,2:T(1,128)S(1)}, f32[1,128,3]{1,0,2:T(1,128)}, u32[]{:S(2)}) copy-start(f32[1,128,3]{1,0,2:T(1,128)} %param.31) | copy-start | bytes 4612
  40.1 29.9 %copy-start.12 = (f32[1,128,3]{1,0,2:T(1,128)S(1)}, f32[1,128,3]{1,0,2:T(1,128)}, u32[]{:S(2)}) copy-start(f32[1,128,3]{1,0,2:T(1,128)} %param.32) | copy-start | bytes 4612
  40.1 29.9 %copy-start.13 = (f32[1,128,3]{1,0,2:T(1,128)S(1)}, f32[1,128,3]{1,0,2:T(1,128)}, u32[]{:S(2)}) copy-start(f32[1,128,3]{1,0,2:T(1,128)} %param.33) | copy-start | bytes 4612
  52.1 1.2 %collective-permute-start.4 = (bf16[96,128]{1,0:T(8,128)(2,1)S(1)}, bf16[96,128]{1,0:T(8,128)(2,1)S(1)}, u32[]{:S(2)}, u32[]{:S(2)}) collective-permute-start(bf16[96,128]{1,0:T(8,128)(2,1)S(1)} %get-tuple-element.74), channel_id=1, source_target_pairs={{0,16},{16,0},{1,17},{17,1},{2,18},{18,2},{3,19},{19,3},{4,20},{20... | collective-permute-start | bytes 73736 | tf_op jit(solution)/shard_map/ppermute | solution.py:646
  53.5 4.6 %collective-permute-start.5 = (bf16[216,128]{1,0:T(8,128)(2,1)S(1)}, bf16[216,128]{1,0:T(8,128)(2,1)S(1)}, u32[]{:S(2)}, u32[]{:S(2)}) collective-permute-start(bf16[216,128]{1,0:T(8,128)(2,1)S(1)} %concatenate.17), channel_id=1, source_target_pairs={{0,4},{1,5},{2,6},{3,7},{4,0},{5,1},{6,2},{7,3},{8,12},{9,13},{10,... | collective-permute-start | bytes 165896 | tf_op jit(solution)/shard_map/ppermute | solution.py:659
  54.6 5.6 %collective-permute-start.6 = (bf16[216,128]{1,0:T(8,128)(2,1)S(1)}, bf16[216,128]{1,0:T(8,128)(2,1)S(1)}, u32[]{:S(2)}, u32[]{:S(2)}) collective-permute-start(bf16[216,128]{1,0:T(8,128)(2,1)S(1)} %concatenate.17), channel_id=1, source_target_pairs={{0,8},{1,9},{2,10},{3,11},{4,12},{5,13},{6,14},{7,15},{8,0},{9,1},... | collective-permute-start | bytes 165896 | tf_op jit(solution)/shard_map/ppermute | solution.py:659
  55.7 6.0 %collective-permute-start.7 = (bf16[216,128]{1,0:T(8,128)(2,1)S(1)}, bf16[216,128]{1,0:T(8,128)(2,1)S(1)}, u32[]{:S(2)}, u32[]{:S(2)}) collective-permute-start(bf16[216,128]{1,0:T(8,128)(2,1)S(1)} %concatenate.17), channel_id=1, source_target_pairs={{0,12},{1,13},{2,14},{3,15},{4,8},{5,9},{6,10},{7,11},{8,4},{9,5},... | collective-permute-start | bytes 165896 | tf_op jit(solution)/shard_map/ppermute | solution.py:659
  62.0 5.8 %collective-permute-start.10 = (bf16[480,128]{1,0:T(8,128)(2,1)S(1)}, bf16[480,128]{1,0:T(8,128)(2,1)S(1)}, u32[]{:S(2)}, u32[]{:S(2)}) collective-permute-start(bf16[480,128]{1,0:T(8,128)(2,1)S(1)} %concatenate.19.refs_0_), channel_id=1, source_target_pairs={{0,3},{1,2},{2,1},{3,0},{4,7},{5,6},{6,5},{7,4},{8,11},{9,10},{10,... | collective-permute-start | bytes 368648 | tf_op jit(solution)/shard_map/ppermute | solution.py:659
  64.4 4.9 %collective-permute-start.8 = (bf16[480,128]{1,0:T(8,128)(2,1)S(1)}, bf16[480,128]{1,0:T(8,128)(2,1)S(1)}, u32[]{:S(2)}, u32[]{:S(2)}) collective-permute-start(bf16[480,128]{1,0:T(8,128)(2,1)S(1)} %concatenate.19.refs_0_), channel_id=1, source_target_pairs={{0,1},{1,0},{2,3},{3,2},{4,5},{5,4},{6,7},{7,6},{8,9},{9,8},{10,11... | collective-permute-start | bytes 368648 | tf_op jit(solution)/shard_map/ppermute | solution.py:659
  65.0 4.9 %collective-permute-start.9 = (bf16[480,128]{1,0:T(8,128)(2,1)S(1)}, bf16[480,128]{1,0:T(8,128)(2,1)S(1)}, u32[]{:S(2)}, u32[]{:S(2)}) collective-permute-start(bf16[480,128]{1,0:T(8,128)(2,1)S(1)} %concatenate.19.refs_0_), channel_id=1, source_target_pairs={{0,2},{1,3},{2,0},{3,1},{4,6},{5,7},{6,4},{7,5},{8,10},{9,11},{10,... | collective-permute-start | bytes 368648 | tf_op jit(solution)/shard_map/ppermute | solution.py:659

commit v4 on v3

--- a/solution.py
+++ b/solution.py
@@ -426,6 +426,26 @@
         runs = [g_e[patch_row(t) : patch_row(t) + 3, cols] for t in range(9)]
         enc.append(jnp.concatenate(runs + [jnp.zeros((5, 128), F32)], 0))
     give(S_E, enc[0], enc[1], keep, 0)
+
+
+def exact_sum(total, first):
+    value = sum(total[first + EXACT * i : first + EXACT * (i + 1)] for i in range(3))
+    pieces = [piece.astype(F32) for piece in part(value, 3)]
+    return jnp.concatenate([total[:first], *pieces, total[first + 3 * EXACT :]], 0).astype(BF)
+
+
+def merge_kernel(keep, early, got, big, early_out):
+    size = keep.shape[0]
+    big[...] = (keep[...] + got[0:size].astype(F32)).astype(BF)
+    total = early[...].astype(F32) + got[size : size + SMALL - LATE].astype(F32)
+    early_out[...] = exact_sum(total, S_X - LATE)
+
+
+def sum_kernel(parts, out):
+    total = parts[0].astype(F32)
+    for i in range(1, parts.shape[0]):
+        total = total + parts[i].astype(F32)
+    out[...] = total.astype(BF)
 
 
 def update_kernel(
@@ -623,8 +643,13 @@
     )(*[inside_vmem(item) for item in (tile, near, pack, theirs, u_c)])
 
     got = lax.ppermute(send, "level", swap)
-    early = sum_small([early, got[padded:]], S_X - LATE)
-    big = (keep + got[:padded].astype(F32)).astype(BF)
+    big, early = pl.pallas_call(
+        merge_kernel,
+        out_shape=[pltpu.VMEM((padded, W), BF), pltpu.VMEM((SMALL - LATE, W), BF)],
+        in_specs=[VMEM] * 3,
+        out_specs=[VMEM] * 2,
+        compiler_params=limit(32),
+    )(*[inside_vmem(item) for item in (keep, early, got)])
     big = lax.all_to_all(big.reshape(devices, size, W), "dp", 0, 0)
 
     late, send = pl.pallas_call(
@@ -642,12 +667,18 @@
         compiler_params=limit(BACK_MIB),
         cost_estimate=pl.CostEstimate(flops=2 * pixels * 98304 * 4, bytes_accessed=1 << 20, transcendentals=0),
     )(*outside(*kept), got)
-    big, send = lax.optimization_barrier((big, send))
     got = lax.ppermute(send, "level", swap)
     late = (late.astype(F32) + got.astype(F32)).astype(BF)
     small = jnp.concatenate([late, early], 0)
 
-    big = jnp.sum(big.astype(F32), 0).astype(BF)[None]
+    big = pl.pallas_call(
+        sum_kernel,
+        out_shape=pltpu.VMEM((size, W), BF),
+        in_specs=[VMEM],
+        out_specs=VMEM,
+        compiler_params=limit(32),
+        cost_estimate=pl.CostEstimate(flops=1 << 34, bytes_accessed=1 << 20, transcendentals=0),
+    )(inside_vmem(big))[None]
     stages = radices(devices)
     crossed = len(stages) == 2 and stages[0][1] == stages[1][1]
     for number, (start, width_bits) in enumerate(reversed(stages)):
@@ -662,10 +693,11 @@
             break
         high = big.shape[0]
         stacked = jnp.zeros((high, count, size, W), BF)
-        for k in range(count):
+        far_first = [0, *range(count - 1, 0, -1)]
+        for k in far_first:
             piece = parts[k][: high * size].reshape(high, size, W)
             stacked = lax.dynamic_update_index_in_dim(stacked, piece, index ^ k, 1)
-        small = sum_small([item[high * size :] for item in parts], S_X)
+        small = sum_small([parts[k][high * size :] for k in far_first], S_X)
         big = stacked.reshape(high * count, size, W)
 
     state = (

time: 72.5 us -> 70.6 us (0.974)
  waiting for transfers between devices: 12.8 us -> 11.5 us
  other arithmetic: 0.99 us -> 0.06 us
    pallas_call x0 -> x2, Pallas kernels: none -> 0.91 us  [the longest x1 0.85 us: local(): pl.pallas_call(merge_kernel, out_shape=[pltpu.VMEM((padded, W), BF), pltp...]
    all_to_all x1, waiting for transfers between devices: 2.19 us -> 1.29 us  [local(): big = lax.all_to_all(big.reshape(devices, size, W), 'dp', 0, 0)]
    convert_element_type x1 -> x0, other arithmetic: 0.85 us -> none  [local(): big = (keep + got[:padded].astype(F32)).astype(BF)]
where the time goes in v4:
time: 70.6 us; the launch traced here: 70.3 us
  Pallas kernels  36 us (51%)
  starting transfers between devices  20.7 us (29%)
  waiting for transfers between devices  11.5 us (16%)
  between operations  1.22 us (2%)
  local copies, waits for them, and re-layouts  0.82 us (1%)
    pallas_call x1, Pallas kernels, local(): pl.pallas_call(functools.partial(step_kernel, batches=batches, rows=rows)...  19.6 us
    pallas_call x1, Pallas kernels, local(): pl.pallas_call(functools.partial(back_kernel, batches=batches, rows=rows)...  9.5 us
    ppermute x6, starting transfers between devices, local(): lax.ppermute(payload, both, xor_pairs(devices, k << start, k << other))  7.99 us
    all_to_all x1, starting transfers between devices, local(): big = lax.all_to_all(big.reshape(devices, size, W), 'dp', 0, 0)  7.49 us
    ppermute x6, waiting for transfers between devices, local(): lax.ppermute(payload, both, xor_pairs(devices, k << start, k << other))  7.4 us
    ppermute x1, starting transfers between devices, local(): near = lax.ppermute(near, both, pairs)  4.48 us
    ppermute x2, waiting for transfers between devices, local(): got = lax.ppermute(send, 'level', swap)  2.83 us
    pallas_call x1, Pallas kernels, local(): pl.pallas_call(functools.partial(update_kernel, stages=len(parts), start=...  2.12 us
  transfers between devices with their start and end apart: 12, of which 8 were waited for; matrix products, arithmetic and copies ran while one was open for 0% of the time, Pallas kernels for 19%

profile of v4, /device:TPU:0, one launch (start us, length us, event | category | flops | bytes accessed | tf_op | source)
XLA Modules:
  0.0 70.3 jit_solution(13265918528476295807)
XLA Ops:
  0.7 0.5 collective-permute-start
  1.2 1.3 %shard_map.320.mine = bf16[1744,128]{1,0:T(8,128)(2,1)S(1)} custom-call(f32[1,512]{1,0:T(1,128)} %refs_4_.1, f32[1,64,512]{2,1,0:T(8,128)} %bitcast.40, f32[27,1,128]{2,1,0:T(1,128)} %bitcast.44, f32[1,64,128]{2,1,0:T(8,128)} %bitcast.42, f32[1,1152,128]{2,1,0:T(8,128)} %refs_12_.1, f32[3,1,128]{2,1,0:T(1,128)} %bitcast.50), custom_call_target="tpu_custom_call" | custom-call | tf_op jit(solution)/shard_map/pallas_call | solution.py:572
  2.5 0.0 collective-permute-done.others
  2.5 0.0 copy-start.15
  2.5 0.1 collective-permute-start.2
  2.7 0.5 copy-done.15
  3.1 1.0 %shard_map.321 = (f32[768,128]{1,0:T(8,128)S(1)}, bf16[48,128]{1,0:T(8,128)(2,1)S(1)}) custom-call(bf16[3,3,32,128]{3,2,1,0:T(8,128)(2,1)} %image.1, s32[3,32,128]{2,1,0:T(8,128)} %mask.1, s32[1,3,32,128]{3,2,1,0:T(8,128)} %codes.1, s32[1,3,32,128]{3,2,1,0:T(8,128)} %copy-done.15), custom_call_target="tpu_custom_call" | custom-call | tf_op jit(solution)/shard_map/pallas_call | solution.py:581
  4.1 4.5 %collective-permute-start.1 = (bf16[48,128]{1,0:T(8,128)(2,1)S(1)}, bf16[48,128]{1,0:T(8,128)(2,1)S(1)}, u32[]{:S(2)}, u32[]{:S(2)}) collective-permute-start(bf16[48,128]{1,0:T(8,128)(2,1)S(1)} %get-tuple-element.60), channel_id=1, source_target_pairs={{0,1},{1,2},{3,4},{4,5},{5,6},{7,8},{8,9},{9,10},{11,12},{12,13},{... | collective-permute-start | bytes 36872 | tf_op jit(solution)/shard_map/ppermute | solution.py:592
  8.6 0.0 collective-permute-done.2.theirs
  8.6 1.5 %shard_map.322.u_c = bf16[128,6912]{1,0:T(8,128)(2,1)S(1)} custom-call(f32[768,128]{1,0:T(8,128)S(1)} %get-tuple-element.59.tile, bf16[1744,128]{1,0:T(8,128)(2,1)S(1)} %shard_map.320.mine, bf16[1744,128]{1,0:T(8,128)(2,1)S(1)} %collective-permute-done.2.theirs), custom_call_target="tpu_custom_call" | custom-call | flops 3221225472 | bytes 1048576 | tf_op jit(solution)/shard_map/pallas_call | solution.py:595
  10.2 19.6 %shard_map.323 = (f32[1408,128]{1,0:T(8,128)S(1)}, bf16[32,128]{1,0:T(8,128)(2,1)S(1)}, bf16[1440,128]{1,0:T(8,128)(2,1)S(1)}, bf16[3,256,2048]{2,1,0:T(8,128)(2...) custom-call(f32[768,128]{1,0:T(8,128)S(1)} %get-tuple-element.59.til, ...), custom_call_target="tpu_custom_call" | custom-call | tf_op jit(solution)/shard_map/pallas_call | solution.py:616
  29.8 0.1 collective-permute-start.3
  29.9 1.7 %collective-permute-done.3.got._ = bf16[1440,128]{1,0:T(8,128)(2,1)S(1)} collective-permute-done((bf16[1440,128]{1,0:T(8,128)(2,1)S(1)}, bf16[1440,128]{1,0:T(8,128)(2,1)S(1)}, u32[]{:S(2)}, u32[]{:S(2)}) %collective-permute-start.3) | collective-permute-done | bytes 368672 | tf_op jit(solution)/shard_map/ppermute | solution.py:645
  31.5 0.9 %shard_map.324 = (bf16[1408,128]{1,0:T(8,128)(2,1)}, bf16[32,128]{1,0:T(8,128)(2,1)S(1)}) custom-call(f32[1408,128]{1,0:T(8,128)S(1)} %get-tuple-element.62.keep, bf16[32,128]{1,0:T(8,128)(2,1)S(1)} %get-tuple-element.63.early, bf16[1440,128]{1,0:T(8,128)(2,1)S(1)} %collective-permute-done.3.got._), custom_call_target="tpu_custom_call" | custom-call | tf_op jit(solution)/shard_map/pallas_call | solution.py:646
  32.4 7.5 %all-to-all-start = ((bf16[16,88,128]{2,1,0:T(8,128)(2,1)}), bf16[16,88,128]{2,1,0:T(8,128)(2,1)S(1)}, u32[]{:S(2)}, u32[]{:S(2)}) async-start(bf16[16,88,128]{2,1,0:T(8,128)(2,1)} %bitcast.4), calls=%async_computation | async-start | bytes 720896 | tf_op jit(solution)/shard_map/all_to_all | solution.py:653
  39.9 9.5 %shard_map.326 = (bf16[96,128]{1,0:T(8,128)(2,1)S(1)}, bf16[96,128]{1,0:T(8,128)(2,1)S(1)}) custom-call(bf16[3,256,2048]{2,1,0:T(8,128)(2,1)} %get-tuple-element.66.h_in, f32[3,256,2048]{2,1,0:T(8,128)} %get-tuple-element.67.slope_in, f32[3,128,2048]{2,1,0:T(8,128)} %get-tuple-element.68.gap_in, bf16[3,256,2304]{2,1,0:T(8,128)(2,1)} %get-tuple-element.69.da_in, ...), custom_call_target="tpu_custom_call" | custom-call | flops 4831838208 | bytes 1048576 | tf_op jit(solution)/shard_map/pallas_call | solution.py:655
  49.4 0.1 collective-permute-start.4
  49.5 1.2 %collective-permute-done.4 = bf16[96,128]{1,0:T(8,128)(2,1)S(1)} collective-permute-done((bf16[96,128]{1,0:T(8,128)(2,1)S(1)}, bf16[96,128]{1,0:T(8,128)(2,1)S(1)}, u32[]{:S(2)}, u32[]{:S(2)}) %collective-permute-start.4) | collective-permute-done | bytes 24608 | tf_op jit(solution)/shard_map/ppermute | solution.py:670
  50.7 0.0 copy-start
  50.7 0.0 copy-start.1
  50.7 0.0 copy-start.2
  50.7 0.0 copy-start.3
  50.7 0.0 copy-start.5
  50.7 0.0 copy-start.6
  50.8 0.0 copy-start.7
  50.8 0.0 copy-start.8
  50.8 0.0 copy-start.9
  50.8 0.0 copy-start.10
  50.8 0.0 copy-start.11
  50.8 0.0 copy-start.12
  50.8 0.0 copy-start.13
  50.8 0.0 copy-start.14
  50.9 1.3 %all-to-all-done.parts = bf16[16,88,128]{2,1,0:T(8,128)(2,1)S(1)} async-done(((bf16[16,88,128]{2,1,0:T(8,128)(2,1)}), bf16[16,88,128]{2,1,0:T(8,128)(2,1)S(1)}, u32[]{:S(2)}, u32[]{:S(2)}) %all-to-all-start) | async-done | bytes 360480 | tf_op jit(solution)/shard_map/all_to_all | solution.py:653
  52.1 0.1 shard_map.325
  52.2 2.5 %collective-permute-start.5 = (bf16[216,128]{1,0:T(8,128)(2,1)S(1)}, bf16[216,128]{1,0:T(8,128)(2,1)S(1)}, u32[]{:S(2)}, u32[]{:S(2)}) collective-permute-start(bf16[216,128]{1,0:T(8,128)(2,1)S(1)} %pad_maximum_fusion), channel_id=1, source_target_pairs={{0,12},{1,13},{2,14},{3,15},{4,8},{5,9},{6,10},{7,11},{8,4},{9,5},... | collective-permute-start | bytes 165896 | tf_op jit(solution)/shard_map/ppermute | solution.py:690
  54.7 0.1 collective-permute-start.6
  54.8 1.9 %collective-permute-start.7 = (bf16[216,128]{1,0:T(8,128)(2,1)S(1)}, bf16[216,128]{1,0:T(8,128)(2,1)S(1)}, u32[]{:S(2)}, u32[]{:S(2)}) collective-permute-start(bf16[216,128]{1,0:T(8,128)(2,1)S(1)} %pad_maximum_fusion), channel_id=1, source_target_pairs={{0,4},{1,5},{2,6},{3,7},{4,0},{5,1},{6,2},{7,3},{8,12},{9,13},{10,... | collective-permute-start | bytes 165896 | tf_op jit(solution)/shard_map/ppermute | solution.py:690
  56.7 1.5 %collective-permute-done.5 = bf16[216,128]{1,0:T(8,128)(2,1)S(1)} collective-permute-done((bf16[216,128]{1,0:T(8,128)(2,1)S(1)}, bf16[216,128]{1,0:T(8,128)(2,1)S(1)}, u32[]{:S(2)}, u32[]{:S(2)}) %collective-permute-start.5) | collective-permute-done | bytes 55328 | tf_op jit(solution)/shard_map/ppermute | solution.py:690
  58.2 1.6 %collective-permute-done.6 = bf16[216,128]{1,0:T(8,128)(2,1)S(1)} collective-permute-done((bf16[216,128]{1,0:T(8,128)(2,1)S(1)}, bf16[216,128]{1,0:T(8,128)(2,1)S(1)}, u32[]{:S(2)}, u32[]{:S(2)}) %collective-permute-start.6) | collective-permute-done | bytes 55328 | tf_op jit(solution)/shard_map/ppermute | solution.py:690
  59.8 0.0 collective-permute-done.7
  59.9 0.2 concatenate.15.refs_0_
  60.1 2.4 %collective-permute-start.10 = (bf16[480,128]{1,0:T(8,128)(2,1)S(1)}, bf16[480,128]{1,0:T(8,128)(2,1)S(1)}, u32[]{:S(2)}, u32[]{:S(2)}) collective-permute-start(bf16[480,128]{1,0:T(8,128)(2,1)S(1)} %concatenate.15.refs_0_), channel_id=1, source_target_pairs={{0,3},{1,2},{2,1},{3,0},{4,7},{5,6},{6,5},{7,4},{8,11},{9,10},{10,... | collective-permute-start | bytes 368648 | tf_op jit(solution)/shard_map/ppermute | solution.py:690
  62.5 0.6 collective-permute-start.8
  63.1 0.6 collective-permute-start.9
  63.6 2.3 %collective-permute-done.10.refs_3_ = bf16[480,128]{1,0:T(8,128)(2,1)S(1)} collective-permute-done((bf16[480,128]{1,0:T(8,128)(2,1)S(1)}, bf16[480,128]{1,0:T(8,128)(2,1)S(1)}, u32[]{:S(2)}, u32[]{:S(2)}) %collective-permute-start.10) | collective-permute-done | bytes 122912 | tf_op jit(solution)/shard_map/ppermute | solution.py:690
  65.9 1.5 %collective-permute-done.8.refs_1_ = bf16[480,128]{1,0:T(8,128)(2,1)S(1)} collective-permute-done((bf16[480,128]{1,0:T(8,128)(2,1)S(1)}, bf16[480,128]{1,0:T(8,128)(2,1)S(1)}, u32[]{:S(2)}, u32[]{:S(2)}) %collective-permute-start.8) | collective-permute-done | bytes 122912 | tf_op jit(solution)/shard_map/ppermute | solution.py:690
  67.4 0.6 collective-permute-done.9.refs_2_
  68.1 2.1 %shard_map.327 = (f32[1,1]{1,0:T(1,128)}, f32[1,1]{1,0:T(1,128)}, f32[1,512]{1,0:T(1,128)}, f32[1,64,512]{2,1,0:T(8,128)}, f32[27,1,128]{2,1,0:T(1,128)}, /*inde...) custom-call(bf16[480,128]{1,0:T(8,128)(2,1)S(1)} %concatenate.15.ref, ...), custom_call_target="tpu_custom_call" | custom-call | tf_op jit(solution)/shard_map/pallas_call | solution.py:713
  (29 shorter events, 0.2 us)
Async XLA Ops:
  0.7 1.9 %collective-permute-start = (s32[1,3,32,128]{3,2,1,0:T(8,128)}, s32[1,3,32,128]{3,2,1,0:T(8,128)S(1)}, u32[]{:S(2)}, u32[]{:S(2)}) collective-permute-start(s32[1,3,32,128]{3,2,1,0:T(8,128)} %codes.1), channel_id=1, source_target_pairs={{0,16},{16,0},{1,17},{17,1},{2,18},{18,2},{3,19},{19,3},{4,20},{20... | collective-permute-start | bytes 147464 | tf_op jit(solution)/shard_map/ppermute | solution.py:570
  2.5 0.6 copy-start.15
  2.5 6.1 %collective-permute-start.2 = (bf16[1744,128]{1,0:T(8,128)(2,1)S(1)}, bf16[1744,128]{1,0:T(8,128)(2,1)S(1)}, u32[]{:S(2)}, u32[]{:S(2)}) collective-permute-start(bf16[1744,128]{1,0:T(8,128)(2,1)S(1)} %shard_map.320.mine), channel_id=1, source_target_pairs={{0,16},{16,0},{1,17},{17,1},{2,18},{18,2},{3,19},{19,3},{4,20},{20... | collective-permute-start | bytes 1339400 | tf_op jit(solution)/shard_map/ppermute | solution.py:593
  4.1 6.0 %collective-permute-start.1 = (bf16[48,128]{1,0:T(8,128)(2,1)S(1)}, bf16[48,128]{1,0:T(8,128)(2,1)S(1)}, u32[]{:S(2)}, u32[]{:S(2)}) collective-permute-start(bf16[48,128]{1,0:T(8,128)(2,1)S(1)} %get-tuple-element.60), channel_id=1, source_target_pairs={{0,1},{1,2},{3,4},{4,5},{5,6},{7,8},{8,9},{9,10},{11,12},{12,13},{... | collective-permute-start | bytes 36872 | tf_op jit(solution)/shard_map/ppermute | solution.py:592
  29.8 1.8 %collective-permute-start.3 = (bf16[1440,128]{1,0:T(8,128)(2,1)S(1)}, bf16[1440,128]{1,0:T(8,128)(2,1)S(1)}, u32[]{:S(2)}, u32[]{:S(2)}) collective-permute-start(bf16[1440,128]{1,0:T(8,128)(2,1)S(1)} %get-tuple-element.64), channel_id=1, source_target_pairs={{0,16},{16,0},{1,17},{17,1},{2,18},{18,2},{3,19},{19,3},{4,20},{20... | collective-permute-start | bytes 1105928 | tf_op jit(solution)/shard_map/ppermute | solution.py:645
  31.5 8.4 %copy-start.4 = (bf16[1440,128]{1,0:T(8,128)(2,1)}, bf16[1440,128]{1,0:T(8,128)(2,1)S(1)}, u32[]{:S(2)}) copy-start(bf16[1440,128]{1,0:T(8,128)(2,1)S(1)} %collective-permute-done.3.got._) | copy-start | bytes 1105924
  32.4 19.7 %all-to-all-start = ((bf16[16,88,128]{2,1,0:T(8,128)(2,1)}), bf16[16,88,128]{2,1,0:T(8,128)(2,1)S(1)}, u32[]{:S(2)}, u32[]{:S(2)}) async-start(bf16[16,88,128]{2,1,0:T(8,128)(2,1)} %bitcast.4), calls=%async_computation | async-start | bytes 720896 | tf_op jit(solution)/shard_map/all_to_all | solution.py:653
  49.4 1.3 %collective-permute-start.4 = (bf16[96,128]{1,0:T(8,128)(2,1)S(1)}, bf16[96,128]{1,0:T(8,128)(2,1)S(1)}, u32[]{:S(2)}, u32[]{:S(2)}) collective-permute-start(bf16[96,128]{1,0:T(8,128)(2,1)S(1)} %get-tuple-element.74), channel_id=1, source_target_pairs={{0,16},{16,0},{1,17},{17,1},{2,18},{18,2},{3,19},{19,3},{4,20},{20... | collective-permute-start | bytes 73736 | tf_op jit(solution)/shard_map/ppermute | solution.py:670
  50.7 17.3 %copy-start = (f32[1,1152,128]{2,1,0:T(8,128)S(1)}, f32[1,1152,128]{2,1,0:T(8,128)}, u32[]{:S(2)}) copy-start(f32[1,1152,128]{2,1,0:T(8,128)} %refs_12_.1) | copy-start | bytes 1769476
  50.7 17.2 %copy-start.1 = (f32[1,1152,128]{2,1,0:T(8,128)S(1)}, f32[1,1152,128]{2,1,0:T(8,128)}, u32[]{:S(2)}) copy-start(f32[1,1152,128]{2,1,0:T(8,128)} %refs_13_.1) | copy-start | bytes 1769476
  50.7 17.2 %copy-start.2 = (f32[1,1152,128]{2,1,0:T(8,128)S(1)}, f32[1,1152,128]{2,1,0:T(8,128)}, u32[]{:S(2)}) copy-start(f32[1,1152,128]{2,1,0:T(8,128)} %refs_14_.1) | copy-start | bytes 1769476
  50.7 17.2 %copy-start.3 = (f32[1,512,64]{1,2,0:T(8,128)S(1)}, f32[1,512,64]{1,2,0:T(8,128)}, u32[]{:S(2)}) copy-start(f32[1,512,64]{1,2,0:T(8,128)} %param.21) | copy-start | bytes 393220
  50.7 17.2 %copy-start.5 = (f32[1,128,64]{1,2,0:T(8,128)S(1)}, f32[1,128,64]{1,2,0:T(8,128)}, u32[]{:S(2)}) copy-start(f32[1,128,64]{1,2,0:T(8,128)} %param.25) | copy-start | bytes 98308
  50.7 17.2 %copy-start.6 = (f32[1,27,128]{2,0,1:T(1,128)S(1)}, f32[1,27,128]{2,0,1:T(1,128)}, u32[]{:S(2)}) copy-start(f32[1,27,128]{2,0,1:T(1,128)} %param.22) | copy-start | bytes 41476
  50.8 17.2 %copy-start.7 = (f32[1,128,64]{1,2,0:T(8,128)S(1)}, f32[1,128,64]{1,2,0:T(8,128)}, u32[]{:S(2)}) copy-start(f32[1,128,64]{1,2,0:T(8,128)} %param.26) | copy-start | bytes 98308
  50.8 17.2 %copy-start.8 = (f32[1,128,64]{1,2,0:T(8,128)S(1)}, f32[1,128,64]{1,2,0:T(8,128)}, u32[]{:S(2)}) copy-start(f32[1,128,64]{1,2,0:T(8,128)} %param.27) | copy-start | bytes 98308
  50.8 17.2 %copy-start.9 = (f32[1,27,128]{2,0,1:T(1,128)S(1)}, f32[1,27,128]{2,0,1:T(1,128)}, u32[]{:S(2)}) copy-start(f32[1,27,128]{2,0,1:T(1,128)} %param.23) | copy-start | bytes 41476
  50.8 17.2 %copy-start.10 = (f32[1,27,128]{2,0,1:T(1,128)S(1)}, f32[1,27,128]{2,0,1:T(1,128)}, u32[]{:S(2)}) copy-start(f32[1,27,128]{2,0,1:T(1,128)} %param.24) | copy-start | bytes 41476
  50.8 17.2 %copy-start.11 = (f32[1,512]{1,0:T(1,128)S(1)}, f32[1,512]{1,0:T(1,128)}, u32[]{:S(2)}) copy-start(f32[1,512]{1,0:T(1,128)} %refs_4_.1) | copy-start | bytes 6148
  50.8 17.2 %copy-start.12 = (f32[1,128,3]{1,0,2:T(1,128)S(1)}, f32[1,128,3]{1,0,2:T(1,128)}, u32[]{:S(2)}) copy-start(f32[1,128,3]{1,0,2:T(1,128)} %param.31) | copy-start | bytes 4612
  50.8 17.2 %copy-start.13 = (f32[1,128,3]{1,0,2:T(1,128)S(1)}, f32[1,128,3]{1,0,2:T(1,128)}, u32[]{:S(2)}) copy-start(f32[1,128,3]{1,0,2:T(1,128)} %param.32) | copy-start | bytes 4612
  50.8 17.2 %copy-start.14 = (f32[1,128,3]{1,0,2:T(1,128)S(1)}, f32[1,128,3]{1,0,2:T(1,128)}, u32[]{:S(2)}) copy-start(f32[1,128,3]{1,0,2:T(1,128)} %param.33) | copy-start | bytes 4612
  52.2 6.0 %collective-permute-start.5 = (bf16[216,128]{1,0:T(8,128)(2,1)S(1)}, bf16[216,128]{1,0:T(8,128)(2,1)S(1)}, u32[]{:S(2)}, u32[]{:S(2)}) collective-permute-start(bf16[216,128]{1,0:T(8,128)(2,1)S(1)} %pad_maximum_fusion), channel_id=1, source_target_pairs={{0,12},{1,13},{2,14},{3,15},{4,8},{5,9},{6,10},{7,11},{8,4},{9,5},... | collective-permute-start | bytes 165896 | tf_op jit(solution)/shard_map/ppermute | solution.py:690
  54.7 5.1 %collective-permute-start.6 = (bf16[216,128]{1,0:T(8,128)(2,1)S(1)}, bf16[216,128]{1,0:T(8,128)(2,1)S(1)}, u32[]{:S(2)}, u32[]{:S(2)}) collective-permute-start(bf16[216,128]{1,0:T(8,128)(2,1)S(1)} %pad_maximum_fusion), channel_id=1, source_target_pairs={{0,8},{1,9},{2,10},{3,11},{4,12},{5,13},{6,14},{7,15},{8,0},{9,1},... | collective-permute-start | bytes 165896 | tf_op jit(solution)/shard_map/ppermute | solution.py:690
  54.8 5.0 %collective-permute-start.7 = (bf16[216,128]{1,0:T(8,128)(2,1)S(1)}, bf16[216,128]{1,0:T(8,128)(2,1)S(1)}, u32[]{:S(2)}, u32[]{:S(2)}) collective-permute-start(bf16[216,128]{1,0:T(8,128)(2,1)S(1)} %pad_maximum_fusion), channel_id=1, source_target_pairs={{0,4},{1,5},{2,6},{3,7},{4,0},{5,1},{6,2},{7,3},{8,12},{9,13},{10,... | collective-permute-start | bytes 165896 | tf_op jit(solution)/shard_map/ppermute | solution.py:690
  60.1 5.8 %collective-permute-start.10 = (bf16[480,128]{1,0:T(8,128)(2,1)S(1)}, bf16[480,128]{1,0:T(8,128)(2,1)S(1)}, u32[]{:S(2)}, u32[]{:S(2)}) collective-permute-start(bf16[480,128]{1,0:T(8,128)(2,1)S(1)} %concatenate.15.refs_0_), channel_id=1, source_target_pairs={{0,3},{1,2},{2,1},{3,0},{4,7},{5,6},{6,5},{7,4},{8,11},{9,10},{10,... | collective-permute-start | bytes 368648 | tf_op jit(solution)/shard_map/ppermute | solution.py:690
  62.5 4.9 %collective-permute-start.8 = (bf16[480,128]{1,0:T(8,128)(2,1)S(1)}, bf16[480,128]{1,0:T(8,128)(2,1)S(1)}, u32[]{:S(2)}, u32[]{:S(2)}) collective-permute-start(bf16[480,128]{1,0:T(8,128)(2,1)S(1)} %concatenate.15.refs_0_), channel_id=1, source_target_pairs={{0,1},{1,0},{2,3},{3,2},{4,5},{5,4},{6,7},{7,6},{8,9},{9,8},{10,11... | collective-permute-start | bytes 368648 | tf_op jit(solution)/shard_map/ppermute | solution.py:690
  63.1 4.9 %collective-permute-start.9 = (bf16[480,128]{1,0:T(8,128)(2,1)S(1)}, bf16[480,128]{1,0:T(8,128)(2,1)S(1)}, u32[]{:S(2)}, u32[]{:S(2)}) collective-permute-start(bf16[480,128]{1,0:T(8,128)(2,1)S(1)} %concatenate.15.refs_0_), channel_id=1, source_target_pairs={{0,2},{1,3},{2,0},{3,1},{4,6},{5,7},{6,4},{7,5},{8,10},{9,11},{10,... | collective-permute-start | bytes 368648 | tf_op jit(solution)/shard_map/ppermute | solution.py:690

commit v5 on v4

--- a/solution.py
+++ b/solution.py
@@ -14,7 +14,7 @@
 F32 = jnp.float32
 BF = jnp.bfloat16
 W = 128
-STEP_MIB, BACK_MIB = 56, 56
+EARLY_MIB, STEP_MIB, BACK_MIB = 36, 36, 56
 NOBODY = 300.0
 
 TAPS = 9 * 128
@@ -137,9 +137,9 @@
     return onehots, highs
 
 
-def quantized(here, bt):
+def quantized(onehots, highs, bt):
     quants = []
-    for onehot, high, book in zip(*one_hots(here), bt):
+    for onehot, high, book in zip(onehots, highs, bt):
         both = dot(book, onehot)
         quants.append(jnp.where(high, both[64:128], both[0:64]))
     return jnp.concatenate(quants, 0)
@@ -150,14 +150,85 @@
     return jnp.where(bottom, a, b), jnp.where(bottom, b, a)
 
 
-def lookup_kernel(tile, mine, theirs, u_c, *, batches, rows):
+def either(mine, theirs, bottom, start, size):
+    a, b = mine[start : start + size], theirs[start : start + size]
+    return jnp.where(bottom, a, b), jnp.where(bottom, b, a)
+
+
+def encoder_weights(mine, theirs, bottom, et, zt):
+    one, zero = either(mine, theirs, bottom, R_ET, 128)
+    et[0:128] = (0.5 * one.astype(F32)).astype(BF)
+    et[128:256] = (0.5 * zero.astype(F32)).astype(BF)
+    one, zero = either(mine, theirs, bottom, R_ZT, 64)
+    blank = jnp.zeros((64, 128), BF)
+    zt[0:64] = jnp.concatenate([one, blank], 1)
+    zt[64:128] = jnp.concatenate([blank, zero], 1)
+
+
+def encoded(x, u, k, onehots, highs, et, zt, g_s):
+    h, slope = silu_parts(dot(et[:, 0:PATCH], x))
+    h = h.astype(BF)
+    z = dot(zt[...], h)
+    gap = z - u
+    kept = k * gap
+    z = k * z.astype(BF).astype(F32)
+    row = lax.broadcasted_iota(jnp.int32, (16, z.shape[1]), 0)
+    for v in range(2):
+        part_z = z[v * 64 : v * 64 + 64]
+        high = highs[v]
+        low_k = jnp.where(high, 0.0, k)
+        high_k = jnp.where(high, k, 0.0)
+        left = jnp.concatenate(
+            [
+                jnp.where(high, 0.0, part_z),
+                jnp.where(high, part_z, 0.0),
+                jnp.where(row == 0, low_k, jnp.where(row == 1, high_k, 0.0)),
+            ],
+            0,
+        ).astype(BF)
+        g_s[v] += dot(left, onehots[v], NT)
+    return h, slope, 0.5 * kept, kept * gap
+
+
+def early_kernel(
+    tile, mine, theirs,
+    u_s, h_s, slope_s, gap_s, x_s, g_s, l_s, et, zt,
+    *, batches, rows,
+):
     level = lax.axis_index("level")
-    bt = books(mine, theirs, level == 1)
+    bottom = level == 1
+    edge = level * (rows - 1)
+    bt = books(mine, theirs, bottom)
+    encoder_weights(mine, theirs, bottom, et, zt)
+    for ref in (g_s, l_s):
+        ref[...] = jnp.zeros_like(ref)
 
     def batch(b, _):
-        first = b * 2 * rows + level * (rows - 2)
-        runs = [tile[pl.ds(pl.multiple_of((first + i) * 8, 8), 8), :] for i in range(rows + 2)]
-        u_c[:, at(b * (rows + 2), rows + 2)] = quantized(jnp.concatenate(runs, 1), bt).astype(BF)
+        def row(i):
+            return tile[pl.ds(pl.multiple_of((b * 2 * rows + i) * 8, 8), 8), :]
+
+        run = [row(jnp.clip(level * rows + r, 0, 2 * rows - 1)) for r in range(-1, rows + 2)]
+        value = jnp.concatenate([jnp.concatenate(run[i : i + 2], 0) for i in range(rows + 2)], 1)
+        for dc, view in enumerate(sides(value)):
+            x_s[dc, :, at(b * (rows + 2), rows + 2)] = view.astype(BF)
+        own = run[1 : rows + 1]
+        beyond = [row(rows - 2 * level + i) for i in range(2)]
+        onehots, highs = one_hots(jnp.concatenate(own + beyond, 1))
+        u = quantized(onehots, highs, bt)
+        inner = slice(0, rows * W)
+        for k, view in enumerate(sides(u)):
+            view = view.astype(BF)
+            u_s[k, :, at(b * (rows + 4) + 2, rows)] = view[:, inner]
+            u_s[k, :, at(b * (rows + 4) + (rows + 2) * (1 - level), 2)] = view[:, rows * W :]
+        k = jnp.concatenate([jnp.where(edge == i, 0.0, own[i][3:4]) for i in range(rows)], 1)
+        h, slope, gap, error = encoded(
+            patches(x_s, b * (rows + 2), rows), u[:, inner], k,
+            [item[:, inner] for item in onehots], [item[:, inner] for item in highs], et, zt, g_s,
+        )
+        h_s[b] = h
+        slope_s[b] = slope
+        gap_s[b] = gap
+        l_s[0:128] += fold(error, 256)
         return 0
 
     lax.fori_loop(0, batches, batch, 0)
@@ -194,11 +265,12 @@
 
 
 def step_kernel(
-    tile, near, mine, theirs, u_c,
-    keep_big, keep_small, send, h_out, slope_out, gap_out, da_out, x_out, dn_out, zn_out,
-    t_s, dt, et, zt, ot, on, u_s, h_s, slope_s, gap_s, da_s, x_s, dn, zn, g_d, g_o, g_s, l_s, sems, fixed_sems,
-    *, batches, rows,
+    tile, near, mine, theirs, *refs,
+    batches, rows,
 ):
+    (keep_big, keep_small, send, h_out, slope_out, gap_out, da_out, x_out, dn_out, zn_out,
+     u_s, h_s, slope_s, gap_s, x_s, g_s, l_s,
+     t_s, dt, et, zt, ot, on, da_s, dn, zn, g_d, g_o, sems, fixed_sems) = refs[7:]
     level, me, devices = lax.axis_index("level"), lax.axis_index("dp"), lax.axis_size("dp")
     band, ext = 2 * rows, rows + 4
     above, below = (me + 1) * band, (me + 2) * band
@@ -208,8 +280,7 @@
     bottom = level == 1
 
     def pair(start, size):
-        a, b = mine[start : start + size], theirs[start : start + size]
-        return jnp.where(bottom, a, b), jnp.where(bottom, b, a)
+        return either(mine, theirs, bottom, start, size)
 
     for t in range(9):
         one, zero = pair(t * 128, 128)
@@ -219,16 +290,10 @@
         dn[dc * 128 : (dc + 1) * 128, dr * 256 + 128 : (dr + 1) * 256] = zero
         dt[0:128, t * 128 : (t + 1) * 128] = (0.5 * one.astype(F32)).T.astype(BF)
         dt[128:256, t * 128 : (t + 1) * 128] = (0.5 * zero.astype(F32)).T.astype(BF)
-    one, zero = pair(R_ET, 128)
-    et[0:128] = (0.5 * one.astype(F32)).astype(BF)
-    et[128:256] = (0.5 * zero.astype(F32)).astype(BF)
+    encoder_weights(mine, theirs, bottom, et, zt)
     one, zero = pair(R_ZN, 128)
     zn[0:128] = (0.5 * one.astype(F32)).astype(BF)
     zn[128:256] = pltpu.roll(0.5 * zero.astype(F32), 64, 1).astype(BF)
-    one, zero = pair(R_ZT, 64)
-    blank = jnp.zeros((64, 128), BF)
-    zt[0:64] = jnp.concatenate([one, blank], 1)
-    zt[64:128] = jnp.concatenate([blank, zero], 1)
     one, zero = pair(R_OT, 16)
     blank = jnp.zeros((8, 128), F32)
     out_t = jnp.concatenate(
@@ -251,77 +316,58 @@
     sub = lax.broadcasted_iota(jnp.int32, (8, W), 0)
     nothing = jnp.where((sub == 4) | (sub == 5), NOBODY, 0.0)
 
-    def inner(i, _):
-        b, e = i // (rows + 2), i % (rows + 2)
-        row = b * band + level * (rows - 2) + e
-        t_s[b, e + jnp.where(bottom, 0, 2)] = tile[pl.ds(pl.multiple_of(row * 8, 8), 8), :]
-        return 0
-
-    lax.fori_loop(0, batches * (rows + 2), inner, 0, unroll=6)
+    outside = []
     for b in range(batches):
         both = near[b * 16 : (b + 1) * 16].astype(F32)
         for r in range(2):
-            shown = jnp.where(valid > 0, both[r * 8 : (r + 1) * 8], nothing)
-            t_s[b, jnp.where(bottom, rows + 2 + r, r)] = shown
-
-    for ref in (g_d, g_o, g_s, l_s):
+            outside.append(jnp.where(valid > 0, both[r * 8 : (r + 1) * 8], nothing))
+    for i, shown in enumerate(outside):
+        t_s[i] = shown
+
+    def row(b, r):
+        return tile[pl.ds(pl.multiple_of((b * band + r) * 8, 8), 8), :]
+
+    for ref in (g_d, g_o):
         ref[...] = jnp.zeros_like(ref)
 
     def spread_rows(u, b, e, n):
         for k, view in enumerate(sides(u)):
             u_s[k, :, at(b * ext + e, n)] = view.astype(BF)
 
-    outer = jnp.where(bottom, rows + 2, 0)
-    here = jnp.concatenate([t_s[b, outer + r] for b in range(batches) for r in range(2)], 1)
-    u = quantized(here, bt)
+    first = level * rows
+    runs = []
+    for b in range(batches):
+        low, high = outside[2 * b], outside[2 * b + 1]
+        runs.append(jnp.concatenate([jnp.where(bottom, row(b, band - 1), high), jnp.where(bottom, low, row(b, 0))], 0))
+        runs.append(jnp.concatenate([jnp.where(bottom, low, row(b, 0)), jnp.where(bottom, high, row(b, 1))], 0))
+    for dc, view in enumerate(sides(jnp.concatenate(runs, 1))):
+        view = view.astype(BF)
+        for b in range(batches):
+            x_s[dc, :, at(b * (rows + 2) + first, 2)] = view[:, b * 2 * W : (b + 1) * 2 * W]
+    outer, edge = jnp.where(bottom, rows + 2, 0), level * (rows - 1)
+    u = quantized(*one_hots(jnp.concatenate(outside, 1)), bt)
     for b in range(batches):
         spread_rows(u[:, b * 2 * W : (b + 1) * 2 * W], b, outer, 2)
+    here = jnp.concatenate([row(b, level * (band - 1)) for b in range(batches)], 1)
+    u = jnp.concatenate([u_s[1, :, at(b * ext + 2 + edge, 1)] for b in range(batches)], 1).astype(F32)
+    x = jnp.concatenate([patches(x_s, b * (rows + 2) + edge, 1) for b in range(batches)], 1)
+    h, slope, gap, error = encoded(x, u, here[3:4], *one_hots(here), et, zt, g_s)
+    l_s[0:128, 0:W] += fold(error, W)
+    for b in range(batches):
+        cols = slice(b * W, (b + 1) * W)
+        h_s[b, :, at(edge, 1)] = h[:, cols]
+        slope_s[b, :, at(edge, 1)] = slope[:, cols]
+        gap_s[b, :, at(edge, 1)] = gap[:, cols]
 
     pairs = ((h_s, h_out), (slope_s, slope_out), (gap_s, gap_out), (da_s, da_out))
 
     def leave(b, which=range(4)):
         return [pltpu.make_async_copy(pairs[n][0].at[b], pairs[n][1].at[b], sems.at[n, b]) for n in which]
 
-    def encode(b, _):
-        runs = [jnp.concatenate([t_s[b, e], t_s[b, e + 1]], 0) for e in range(1, rows + 3)]
-        for dc, view in enumerate(sides(jnp.concatenate(runs, 1))):
-            x_s[dc, :, at(b * (rows + 2), rows + 2)] = view.astype(BF)
-        spread_rows(u_c[:, at(b * (rows + 2), rows + 2)].astype(F32), b, jnp.where(bottom, 0, 2), rows + 2)
-        u = u_c[:, at(b * (rows + 2) + 2 * level, rows)].astype(F32)
-        here = jnp.concatenate([t_s[b, 2 + i] for i in range(rows)], 1)
-        onehots, highs = one_hots(here)
-        h, slope = silu_parts(dot(et[:, 0:PATCH], patches(x_s, b * (rows + 2), rows)))
-        slope_s[b] = slope
-        h = h.astype(BF)
-        h_s[b] = h
-        z = dot(zt[...], h)
-        k = here[3:4]
-        gap = z - u
-        kept = k * gap
-        l_s[0:128] += fold(kept * gap, 256)
-        gap_s[b] = 0.5 * kept
-        z = k * z.astype(BF).astype(F32)
-        row = lax.broadcasted_iota(jnp.int32, (16, rows * W), 0)
-        for v in range(2):
-            part_z = z[v * 64 : v * 64 + 64]
-            high = highs[v]
-            low_k = jnp.where(high, 0.0, k)
-            high_k = jnp.where(high, k, 0.0)
-            left = jnp.concatenate(
-                [
-                    jnp.where(high, 0.0, part_z),
-                    jnp.where(high, part_z, 0.0),
-                    jnp.where(row == 0, low_k, jnp.where(row == 1, high_k, 0.0)),
-                ],
-                0,
-            ).astype(BF)
-            g_s[v] += dot(left, onehots[v], NT)
+    fixed[0].start()
+    for b in range(batches):
         for copy in leave(b, range(3)):
             copy.start()
-        return 0
-
-    lax.fori_loop(0, batches, encode, 0)
-    fixed[0].start()
 
     def decode(b, _):
         u = jnp.concatenate(
@@ -331,7 +377,10 @@
         g, slope = silu_parts(dot(dt[...], u))
         g = g.astype(BF)
         y = dot(ot[...], g)
-        here = jnp.concatenate([t_s[b, e] for e in range(1, rows + 3)], 1)
+        shown = [row(b, jnp.clip(level * rows + r, 0, band - 1)) for r in range(-1, rows + 1)]
+        shown[0] = jnp.where(bottom, shown[0], t_s[2 * b + 1])
+        shown[-1] = jnp.where(bottom, t_s[2 * b], shown[-1])
+        here = jnp.concatenate(shown, 1)
         k = here[3:4]
         x = jnp.where(lax.broadcasted_iota(jnp.int32, here.shape, 0) < 3, here, 0.0)
         diff = y - jnp.concatenate([x, x], 0)
@@ -592,14 +641,7 @@
     near = lax.ppermute(near, both, pairs)
     theirs = lax.ppermute(pack, "level", swap)
 
-    u_c = pl.pallas_call(
-        functools.partial(lookup_kernel, batches=batches, rows=rows),
-        out_shape=pltpu.VMEM((128, batches * (rows + 2) * W), BF),
-        in_specs=[VMEM] * 3,
-        out_specs=VMEM,
-        compiler_params=limit(40),
-        cost_estimate=pl.CostEstimate(flops=3 << 30, bytes_accessed=1 << 20, transcendentals=0),
-    )(*[inside_vmem(item) for item in (tile, pack, theirs)])
+    ext = rows + 4
     ext = rows + 4
     pixels = batches * rows * W
     framed = batches * (rows + 2) * W
@@ -613,34 +655,52 @@
     size = -(-BIG // (8 * devices)) * 8
     padded = size * devices
     shape = jax.ShapeDtypeStruct
-    keep, early, send, *kept = pl.pallas_call(
+    staged = [
+        pltpu.VMEM((3, 128, batches * ext * W), BF),
+        *[pltpu.VMEM(*item) for item in held[:3]],
+        pltpu.VMEM(*fixed[0]),
+        pltpu.VMEM((2, 144, 256), F32),
+        pltpu.VMEM((144, 256), F32),
+    ]
+    stages_early = pl.pallas_call(
+        functools.partial(early_kernel, batches=batches, rows=rows),
+        out_shape=staged,
+        in_specs=[VMEM] * 3,
+        out_specs=[VMEM] * 7,
+        scratch_shapes=[pltpu.VMEM((256, 128), BF), pltpu.VMEM((128, 256), BF)],
+        compiler_params=limit(EARLY_MIB),
+        cost_estimate=pl.CostEstimate(flops=3 << 30, bytes_accessed=1 << 20, transcendentals=0),
+    )(*[inside_vmem(item) for item in (tile, pack, theirs)])
+    results = pl.pallas_call(
         functools.partial(step_kernel, batches=batches, rows=rows),
         out_shape=[
             pltpu.VMEM((padded, W), F32),
             pltpu.VMEM((SMALL - LATE, W), BF),
             pltpu.VMEM((padded + SMALL - LATE, W), BF),
             *[shape(*item) for item in held + fixed],
+            *staged,
         ],
-        in_specs=[VMEM] * 5,
-        out_specs=[VMEM] * 3 + [AWAY] * 7,
+        in_specs=[VMEM] * 11,
+        out_specs=[VMEM] * 3 + [AWAY] * 7 + [VMEM] * 7,
+        input_output_aliases={4 + i: 10 + i for i in range(7)},
         scratch_shapes=[
-            pltpu.VMEM((batches, ext, 8, W), F32),
+            pltpu.VMEM((2 * batches, 8, W), F32),
             pltpu.VMEM((256, TAPS), BF),
             pltpu.VMEM((256, 128), BF),
             pltpu.VMEM((128, 256), BF),
             pltpu.VMEM((16, 256), BF),
             pltpu.VMEM((256, 16), BF),
-            pltpu.VMEM((3, 128, batches * ext * W), BF),
-            *[pltpu.VMEM(*item) for item in held + fixed],
+            pltpu.VMEM(*held[3]),
+            *[pltpu.VMEM(*item) for item in fixed[1:]],
             pltpu.VMEM((TAPS, 256), F32),
             pltpu.VMEM((256, 16), F32),
-            pltpu.VMEM((2, 144, 256), F32),
-            pltpu.VMEM((144, 256), F32),
             pltpu.SemaphoreType.DMA((4, batches)),
             pltpu.SemaphoreType.DMA((3,)),
         ],
         compiler_params=limit(STEP_MIB),
-    )(*[inside_vmem(item) for item in (tile, near, pack, theirs, u_c)])
+    )(*[inside_vmem(item) for item in (tile, near, pack, theirs, *stages_early)])
+    keep, early, send = results[:3]
+    kept = results[3:10]
 
     got = lax.ppermute(send, "level", swap)
     big, early = pl.pallas_call(

time: 70.6 us -> 69.5 us (0.984)
  starting transfers between devices: 20.7 us -> 19.2 us
    pallas_call x1, Pallas kernels: 1.51 us -> 7.45 us  [local(): pl.pallas_call(functools.partial(early_kernel, batches=batches, rows=rows...]
    pallas_call x1, Pallas kernels: 19.6 us -> 14.1 us  [local(): pl.pallas_call(functools.partial(step_kernel, batches=batches, rows=rows)...]
    all_to_all x1, starting transfers between devices: 7.49 us -> 5.94 us  [local(): big = lax.all_to_all(big.reshape(devices, size, W), 'dp', 0, 0)]
  transfers between devices with their start and end apart: 12 -> 12, of which waited for: 8 -> 8; matrix products, arithmetic and copies ran while one was open for 0% -> 0% of each run, Pallas kernels for 19% -> 28%
where the time goes in v5:
time: 69.5 us; the launch traced here: 69.2 us
  Pallas kernels  36.4 us (52%)
  starting transfers between devices  19.2 us (28%)
  waiting for transfers between devices  11.5 us (17%)
  between operations  1.21 us (2%)
  local copies, waits for them, and re-layouts  0.82 us (1%)
    pallas_call x1, Pallas kernels, local(): pl.pallas_call(functools.partial(step_kernel, batches=batches, rows=rows)...  14.1 us
    pallas_call x1, Pallas kernels, local(): pl.pallas_call(functools.partial(back_kernel, batches=batches, rows=rows)...  9.5 us
    ppermute x6, starting transfers between devices, local(): lax.ppermute(payload, both, xor_pairs(devices, k << start, k << other))  7.99 us
    pallas_call x1, Pallas kernels, local(): pl.pallas_call(functools.partial(early_kernel, batches=batches, rows=rows...  7.45 us
    ppermute x6, waiting for transfers between devices, local(): lax.ppermute(payload, both, xor_pairs(devices, k << start, k << other))  7.4 us
    all_to_all x1, starting transfers between devices, local(): big = lax.all_to_all(big.reshape(devices, size, W), 'dp', 0, 0)  5.94 us
    ppermute x1, starting transfers between devices, local(): near = lax.ppermute(near, both, pairs)  4.48 us
    ppermute x2, waiting for transfers between devices, local(): got = lax.ppermute(send, 'level', swap)  2.83 us
  transfers between devices with their start and end apart: 12, of which 8 were waited for; matrix products, arithmetic and copies ran while one was open for 0% of the time, Pallas kernels for 28%

profile of v5, /device:TPU:0, one launch (start us, length us, event | category | flops | bytes accessed | tf_op | source)
XLA Modules:
  0.0 69.2 jit_solution(9196016509070506004)
XLA Ops:
  0.7 0.5 collective-permute-start
  1.2 1.3 %shard_map.320.mine = bf16[1744,128]{1,0:T(8,128)(2,1)S(1)} custom-call(f32[1,512]{1,0:T(1,128)} %refs_4_.1, f32[1,64,512]{2,1,0:T(8,128)} %bitcast.40, f32[27,1,128]{2,1,0:T(1,128)} %bitcast.44, f32[1,64,128]{2,1,0:T(8,128)} %bitcast.42, f32[1,1152,128]{2,1,0:T(8,128)} %refs_12_.1, f32[3,1,128]{2,1,0:T(1,128)} %bitcast.50), custom_call_target="tpu_custom_call" | custom-call | tf_op jit(solution)/shard_map/pallas_call | solution.py:621
  2.5 0.0 collective-permute-done.others
  2.5 0.0 copy-start.15
  2.5 0.1 collective-permute-start.2
  2.7 0.5 copy-done.15
  3.1 1.0 %shard_map.321 = (f32[768,128]{1,0:T(8,128)S(1)}, bf16[48,128]{1,0:T(8,128)(2,1)S(1)}) custom-call(bf16[3,3,32,128]{3,2,1,0:T(8,128)(2,1)} %image.1, s32[3,32,128]{2,1,0:T(8,128)} %mask.1, s32[1,3,32,128]{3,2,1,0:T(8,128)} %codes.1, s32[1,3,32,128]{3,2,1,0:T(8,128)} %copy-done.15), custom_call_target="tpu_custom_call" | custom-call | tf_op jit(solution)/shard_map/pallas_call | solution.py:630
  4.1 4.5 %collective-permute-start.1 = (bf16[48,128]{1,0:T(8,128)(2,1)S(1)}, bf16[48,128]{1,0:T(8,128)(2,1)S(1)}, u32[]{:S(2)}, u32[]{:S(2)}) collective-permute-start(bf16[48,128]{1,0:T(8,128)(2,1)S(1)} %get-tuple-element.67), channel_id=1, source_target_pairs={{0,1},{1,2},{3,4},{4,5},{5,6},{7,8},{8,9},{9,10},{11,12},{12,13},{... | collective-permute-start | bytes 36872 | tf_op jit(solution)/shard_map/ppermute | solution.py:641
  8.6 0.0 collective-permute-done.2.theirs
  8.6 7.5 %shard_map.322 = (bf16[3,128,7680]{2,1,0:T(8,128)(2,1)S(1)}, bf16[3,256,2048]{2,1,0:T(8,128)(2,1)S(1)}, f32[3,256,2048]{2,1,0:T(8,128)S(1)}, f32[3,128,2048]{2,1...) custom-call(f32[768,128]{1,0:T(8,128)S(1)} %get-tuple-element.66.tile, ...), custom_call_target="tpu_custom_call" | custom-call | flops 3221225472 | bytes 1048576 | tf_op jit(solution)/shard_map/pallas_call | solution.py:665
  16.1 14.1 %shard_map.323 = (f32[1408,128]{1,0:T(8,128)S(1)}, bf16[32,128]{1,0:T(8,128)(2,1)S(1)}, bf16[1440,128]{1,0:T(8,128)(2,1)S(1)}, bf16[3,256,2048]{2,1,0:T(8,128)(2...) custom-call(f32[768,128]{1,0:T(8,128)S(1)} %get-tuple-element.66.til, ...), custom_call_target="tpu_custom_call", output_to_operand_aliasing={{10}: (4, {}), {11}: (5, {}), {12}: (6, {}), {13}: (7, {}),... | custom-call | tf_op jit(solution)/shard_map/pallas_call | solution.py:674
  30.2 0.1 collective-permute-start.3
  30.3 1.7 %collective-permute-done.3.got._ = bf16[1440,128]{1,0:T(8,128)(2,1)S(1)} collective-permute-done((bf16[1440,128]{1,0:T(8,128)(2,1)S(1)}, bf16[1440,128]{1,0:T(8,128)(2,1)S(1)}, u32[]{:S(2)}, u32[]{:S(2)}) %collective-permute-start.3) | collective-permute-done | bytes 368672 | tf_op jit(solution)/shard_map/ppermute | solution.py:705
  32.0 0.9 %shard_map.324 = (bf16[1408,128]{1,0:T(8,128)(2,1)}, bf16[32,128]{1,0:T(8,128)(2,1)S(1)}) custom-call(f32[1408,128]{1,0:T(8,128)S(1)} %get-tuple-element.76.keep, bf16[32,128]{1,0:T(8,128)(2,1)S(1)} %get-tuple-element.77.early, bf16[1440,128]{1,0:T(8,128)(2,1)S(1)} %collective-permute-done.3.got._), custom_call_target="tpu_custom_call" | custom-call | tf_op jit(solution)/shard_map/pallas_call | solution.py:706
  32.8 5.9 %all-to-all-start = ((bf16[16,88,128]{2,1,0:T(8,128)(2,1)}), bf16[16,88,128]{2,1,0:T(8,128)(2,1)S(1)}, u32[]{:S(2)}, u32[]{:S(2)}) async-start(bf16[16,88,128]{2,1,0:T(8,128)(2,1)} %bitcast.4), calls=%async_computation | async-start | bytes 720896 | tf_op jit(solution)/shard_map/all_to_all | solution.py:713
  38.8 9.5 %shard_map.326 = (bf16[96,128]{1,0:T(8,128)(2,1)S(1)}, bf16[96,128]{1,0:T(8,128)(2,1)S(1)}) custom-call(bf16[3,256,2048]{2,1,0:T(8,128)(2,1)} %get-tuple-element.80.h_in, f32[3,256,2048]{2,1,0:T(8,128)} %get-tuple-element.81.slope_in, f32[3,128,2048]{2,1,0:T(8,128)} %get-tuple-element.82.gap_in, bf16[3,256,2304]{2,1,0:T(8,128)(2,1)} %get-tuple-element.83.da_in, ...), custom_call_target="tpu_custom_call" | custom-call | flops 4831838208 | bytes 1048576 | tf_op jit(solution)/shard_map/pallas_call | solution.py:715
  48.3 0.1 collective-permute-start.4
  48.4 1.2 %collective-permute-done.4 = bf16[96,128]{1,0:T(8,128)(2,1)S(1)} collective-permute-done((bf16[96,128]{1,0:T(8,128)(2,1)S(1)}, bf16[96,128]{1,0:T(8,128)(2,1)S(1)}, u32[]{:S(2)}, u32[]{:S(2)}) %collective-permute-start.4) | collective-permute-done | bytes 24608 | tf_op jit(solution)/shard_map/ppermute | solution.py:730
  49.6 0.0 copy-start
  49.6 0.0 copy-start.1
  49.6 0.0 copy-start.2
  49.6 0.0 copy-start.3
  49.6 0.0 copy-start.5
  49.6 0.0 copy-start.6
  49.6 0.0 copy-start.7
  49.7 0.0 copy-start.8
  49.7 0.0 copy-start.9
  49.7 0.0 copy-start.10
  49.7 0.0 copy-start.11
  49.7 0.0 copy-start.12
  49.7 0.0 copy-start.13
  49.7 0.0 copy-start.14
  49.7 1.3 %all-to-all-done.parts = bf16[16,88,128]{2,1,0:T(8,128)(2,1)S(1)} async-done(((bf16[16,88,128]{2,1,0:T(8,128)(2,1)}), bf16[16,88,128]{2,1,0:T(8,128)(2,1)S(1)}, u32[]{:S(2)}, u32[]{:S(2)}) %all-to-all-start) | async-done | bytes 360480 | tf_op jit(solution)/shard_map/all_to_all | solution.py:713
  51.0 0.1 shard_map.325
  51.1 2.5 %collective-permute-start.5 = (bf16[216,128]{1,0:T(8,128)(2,1)S(1)}, bf16[216,128]{1,0:T(8,128)(2,1)S(1)}, u32[]{:S(2)}, u32[]{:S(2)}) collective-permute-start(bf16[216,128]{1,0:T(8,128)(2,1)S(1)} %pad_maximum_fusion), channel_id=1, source_target_pairs={{0,12},{1,13},{2,14},{3,15},{4,8},{5,9},{6,10},{7,11},{8,4},{9,5},... | collective-permute-start | bytes 165896 | tf_op jit(solution)/shard_map/ppermute | solution.py:750
  53.6 0.1 collective-permute-start.6
  53.7 1.9 %collective-permute-start.7 = (bf16[216,128]{1,0:T(8,128)(2,1)S(1)}, bf16[216,128]{1,0:T(8,128)(2,1)S(1)}, u32[]{:S(2)}, u32[]{:S(2)}) collective-permute-start(bf16[216,128]{1,0:T(8,128)(2,1)S(1)} %pad_maximum_fusion), channel_id=1, source_target_pairs={{0,4},{1,5},{2,6},{3,7},{4,0},{5,1},{6,2},{7,3},{8,12},{9,13},{10,... | collective-permute-start | bytes 165896 | tf_op jit(solution)/shard_map/ppermute | solution.py:750
  55.6 1.5 %collective-permute-done.5 = bf16[216,128]{1,0:T(8,128)(2,1)S(1)} collective-permute-done((bf16[216,128]{1,0:T(8,128)(2,1)S(1)}, bf16[216,128]{1,0:T(8,128)(2,1)S(1)}, u32[]{:S(2)}, u32[]{:S(2)}) %collective-permute-start.5) | collective-permute-done | bytes 55328 | tf_op jit(solution)/shard_map/ppermute | solution.py:750
  57.1 1.6 %collective-permute-done.6 = bf16[216,128]{1,0:T(8,128)(2,1)S(1)} collective-permute-done((bf16[216,128]{1,0:T(8,128)(2,1)S(1)}, bf16[216,128]{1,0:T(8,128)(2,1)S(1)}, u32[]{:S(2)}, u32[]{:S(2)}) %collective-permute-start.6) | collective-permute-done | bytes 55328 | tf_op jit(solution)/shard_map/ppermute | solution.py:750
  58.7 0.0 collective-permute-done.7
  58.8 0.2 concatenate.15.refs_0_
  59.0 2.4 %collective-permute-start.10 = (bf16[480,128]{1,0:T(8,128)(2,1)S(1)}, bf16[480,128]{1,0:T(8,128)(2,1)S(1)}, u32[]{:S(2)}, u32[]{:S(2)}) collective-permute-start(bf16[480,128]{1,0:T(8,128)(2,1)S(1)} %concatenate.15.refs_0_), channel_id=1, source_target_pairs={{0,3},{1,2},{2,1},{3,0},{4,7},{5,6},{6,5},{7,4},{8,11},{9,10},{10,... | collective-permute-start | bytes 368648 | tf_op jit(solution)/shard_map/ppermute | solution.py:750
  61.4 0.6 collective-permute-start.8
  61.9 0.6 collective-permute-start.9
  62.5 2.3 %collective-permute-done.10.refs_3_ = bf16[480,128]{1,0:T(8,128)(2,1)S(1)} collective-permute-done((bf16[480,128]{1,0:T(8,128)(2,1)S(1)}, bf16[480,128]{1,0:T(8,128)(2,1)S(1)}, u32[]{:S(2)}, u32[]{:S(2)}) %collective-permute-start.10) | collective-permute-done | bytes 122912 | tf_op jit(solution)/shard_map/ppermute | solution.py:750
  64.8 1.5 %collective-permute-done.8.refs_1_ = bf16[480,128]{1,0:T(8,128)(2,1)S(1)} collective-permute-done((bf16[480,128]{1,0:T(8,128)(2,1)S(1)}, bf16[480,128]{1,0:T(8,128)(2,1)S(1)}, u32[]{:S(2)}, u32[]{:S(2)}) %collective-permute-start.8) | collective-permute-done | bytes 122912 | tf_op jit(solution)/shard_map/ppermute | solution.py:750
  66.3 0.6 collective-permute-done.9.refs_2_
  66.9 2.1 %shard_map.327 = (f32[1,1]{1,0:T(1,128)}, f32[1,1]{1,0:T(1,128)}, f32[1,512]{1,0:T(1,128)}, f32[1,64,512]{2,1,0:T(8,128)}, f32[27,1,128]{2,1,0:T(1,128)}, /*inde...) custom-call(bf16[480,128]{1,0:T(8,128)(2,1)S(1)} %concatenate.15.ref, ...), custom_call_target="tpu_custom_call" | custom-call | tf_op jit(solution)/shard_map/pallas_call | solution.py:773
  (29 shorter events, 0.2 us)
Async XLA Ops:
  0.7 1.9 %collective-permute-start = (s32[1,3,32,128]{3,2,1,0:T(8,128)}, s32[1,3,32,128]{3,2,1,0:T(8,128)S(1)}, u32[]{:S(2)}, u32[]{:S(2)}) collective-permute-start(s32[1,3,32,128]{3,2,1,0:T(8,128)} %codes.1), channel_id=1, source_target_pairs={{0,16},{16,0},{1,17},{17,1},{2,18},{18,2},{3,19},{19,3},{4,20},{20... | collective-permute-start | bytes 147464 | tf_op jit(solution)/shard_map/ppermute | solution.py:619
  2.5 0.6 copy-start.15
  2.5 6.1 %collective-permute-start.2 = (bf16[1744,128]{1,0:T(8,128)(2,1)S(1)}, bf16[1744,128]{1,0:T(8,128)(2,1)S(1)}, u32[]{:S(2)}, u32[]{:S(2)}) collective-permute-start(bf16[1744,128]{1,0:T(8,128)(2,1)S(1)} %shard_map.320.mine), channel_id=1, source_target_pairs={{0,16},{16,0},{1,17},{17,1},{2,18},{18,2},{3,19},{19,3},{4,20},{20... | collective-permute-start | bytes 1339400 | tf_op jit(solution)/shard_map/ppermute | solution.py:642
  4.1 12.0 %collective-permute-start.1 = (bf16[48,128]{1,0:T(8,128)(2,1)S(1)}, bf16[48,128]{1,0:T(8,128)(2,1)S(1)}, u32[]{:S(2)}, u32[]{:S(2)}) collective-permute-start(bf16[48,128]{1,0:T(8,128)(2,1)S(1)} %get-tuple-element.67), channel_id=1, source_target_pairs={{0,1},{1,2},{3,4},{4,5},{5,6},{7,8},{8,9},{9,10},{11,12},{12,13},{... | collective-permute-start | bytes 36872 | tf_op jit(solution)/shard_map/ppermute | solution.py:641
  30.2 1.8 %collective-permute-start.3 = (bf16[1440,128]{1,0:T(8,128)(2,1)S(1)}, bf16[1440,128]{1,0:T(8,128)(2,1)S(1)}, u32[]{:S(2)}, u32[]{:S(2)}) collective-permute-start(bf16[1440,128]{1,0:T(8,128)(2,1)S(1)} %get-tuple-element.78), channel_id=1, source_target_pairs={{0,16},{16,0},{1,17},{17,1},{2,18},{18,2},{3,19},{19,3},{4,20},{20... | collective-permute-start | bytes 1105928 | tf_op jit(solution)/shard_map/ppermute | solution.py:705
  32.0 6.8 %copy-start.4 = (bf16[1440,128]{1,0:T(8,128)(2,1)}, bf16[1440,128]{1,0:T(8,128)(2,1)S(1)}, u32[]{:S(2)}) copy-start(bf16[1440,128]{1,0:T(8,128)(2,1)S(1)} %collective-permute-done.3.got._) | copy-start | bytes 1105924
  32.8 18.2 %all-to-all-start = ((bf16[16,88,128]{2,1,0:T(8,128)(2,1)}), bf16[16,88,128]{2,1,0:T(8,128)(2,1)S(1)}, u32[]{:S(2)}, u32[]{:S(2)}) async-start(bf16[16,88,128]{2,1,0:T(8,128)(2,1)} %bitcast.4), calls=%async_computation | async-start | bytes 720896 | tf_op jit(solution)/shard_map/all_to_all | solution.py:713
  48.3 1.3 %collective-permute-start.4 = (bf16[96,128]{1,0:T(8,128)(2,1)S(1)}, bf16[96,128]{1,0:T(8,128)(2,1)S(1)}, u32[]{:S(2)}, u32[]{:S(2)}) collective-permute-start(bf16[96,128]{1,0:T(8,128)(2,1)S(1)} %get-tuple-element.88), channel_id=1, source_target_pairs={{0,16},{16,0},{1,17},{17,1},{2,18},{18,2},{3,19},{19,3},{4,20},{20... | collective-permute-start | bytes 73736 | tf_op jit(solution)/shard_map/ppermute | solution.py:730
  49.6 17.3 %copy-start = (f32[1,1152,128]{2,1,0:T(8,128)S(1)}, f32[1,1152,128]{2,1,0:T(8,128)}, u32[]{:S(2)}) copy-start(f32[1,1152,128]{2,1,0:T(8,128)} %refs_12_.1) | copy-start | bytes 1769476
  49.6 17.2 %copy-start.1 = (f32[1,1152,128]{2,1,0:T(8,128)S(1)}, f32[1,1152,128]{2,1,0:T(8,128)}, u32[]{:S(2)}) copy-start(f32[1,1152,128]{2,1,0:T(8,128)} %refs_13_.1) | copy-start | bytes 1769476
  49.6 17.2 %copy-start.2 = (f32[1,1152,128]{2,1,0:T(8,128)S(1)}, f32[1,1152,128]{2,1,0:T(8,128)}, u32[]{:S(2)}) copy-start(f32[1,1152,128]{2,1,0:T(8,128)} %refs_14_.1) | copy-start | bytes 1769476
  49.6 17.2 %copy-start.3 = (f32[1,512,64]{1,2,0:T(8,128)S(1)}, f32[1,512,64]{1,2,0:T(8,128)}, u32[]{:S(2)}) copy-start(f32[1,512,64]{1,2,0:T(8,128)} %param.21) | copy-start | bytes 393220
  49.6 17.2 %copy-start.5 = (f32[1,128,64]{1,2,0:T(8,128)S(1)}, f32[1,128,64]{1,2,0:T(8,128)}, u32[]{:S(2)}) copy-start(f32[1,128,64]{1,2,0:T(8,128)} %param.25) | copy-start | bytes 98308
  49.6 17.2 %copy-start.6 = (f32[1,27,128]{2,0,1:T(1,128)S(1)}, f32[1,27,128]{2,0,1:T(1,128)}, u32[]{:S(2)}) copy-start(f32[1,27,128]{2,0,1:T(1,128)} %param.22) | copy-start | bytes 41476
  49.6 17.2 %copy-start.7 = (f32[1,128,64]{1,2,0:T(8,128)S(1)}, f32[1,128,64]{1,2,0:T(8,128)}, u32[]{:S(2)}) copy-start(f32[1,128,64]{1,2,0:T(8,128)} %param.26) | copy-start | bytes 98308
  49.7 17.2 %copy-start.8 = (f32[1,128,64]{1,2,0:T(8,128)S(1)}, f32[1,128,64]{1,2,0:T(8,128)}, u32[]{:S(2)}) copy-start(f32[1,128,64]{1,2,0:T(8,128)} %param.27) | copy-start | bytes 98308
  49.7 17.2 %copy-start.9 = (f32[1,27,128]{2,0,1:T(1,128)S(1)}, f32[1,27,128]{2,0,1:T(1,128)}, u32[]{:S(2)}) copy-start(f32[1,27,128]{2,0,1:T(1,128)} %param.23) | copy-start | bytes 41476
  49.7 17.2 %copy-start.10 = (f32[1,27,128]{2,0,1:T(1,128)S(1)}, f32[1,27,128]{2,0,1:T(1,128)}, u32[]{:S(2)}) copy-start(f32[1,27,128]{2,0,1:T(1,128)} %param.24) | copy-start | bytes 41476
  49.7 17.2 %copy-start.11 = (f32[1,512]{1,0:T(1,128)S(1)}, f32[1,512]{1,0:T(1,128)}, u32[]{:S(2)}) copy-start(f32[1,512]{1,0:T(1,128)} %refs_4_.1) | copy-start | bytes 6148
  49.7 17.2 %copy-start.12 = (f32[1,128,3]{1,0,2:T(1,128)S(1)}, f32[1,128,3]{1,0,2:T(1,128)}, u32[]{:S(2)}) copy-start(f32[1,128,3]{1,0,2:T(1,128)} %param.31) | copy-start | bytes 4612
  49.7 17.2 %copy-start.13 = (f32[1,128,3]{1,0,2:T(1,128)S(1)}, f32[1,128,3]{1,0,2:T(1,128)}, u32[]{:S(2)}) copy-start(f32[1,128,3]{1,0,2:T(1,128)} %param.32) | copy-start | bytes 4612
  49.7 17.2 %copy-start.14 = (f32[1,128,3]{1,0,2:T(1,128)S(1)}, f32[1,128,3]{1,0,2:T(1,128)}, u32[]{:S(2)}) copy-start(f32[1,128,3]{1,0,2:T(1,128)} %param.33) | copy-start | bytes 4612
  51.1 6.0 %collective-permute-start.5 = (bf16[216,128]{1,0:T(8,128)(2,1)S(1)}, bf16[216,128]{1,0:T(8,128)(2,1)S(1)}, u32[]{:S(2)}, u32[]{:S(2)}) collective-permute-start(bf16[216,128]{1,0:T(8,128)(2,1)S(1)} %pad_maximum_fusion), channel_id=1, source_target_pairs={{0,12},{1,13},{2,14},{3,15},{4,8},{5,9},{6,10},{7,11},{8,4},{9,5},... | collective-permute-start | bytes 165896 | tf_op jit(solution)/shard_map/ppermute | solution.py:750
  53.6 5.1 %collective-permute-start.6 = (bf16[216,128]{1,0:T(8,128)(2,1)S(1)}, bf16[216,128]{1,0:T(8,128)(2,1)S(1)}, u32[]{:S(2)}, u32[]{:S(2)}) collective-permute-start(bf16[216,128]{1,0:T(8,128)(2,1)S(1)} %pad_maximum_fusion), channel_id=1, source_target_pairs={{0,8},{1,9},{2,10},{3,11},{4,12},{5,13},{6,14},{7,15},{8,0},{9,1},... | collective-permute-start | bytes 165896 | tf_op jit(solution)/shard_map/ppermute | solution.py:750
  53.7 5.0 %collective-permute-start.7 = (bf16[216,128]{1,0:T(8,128)(2,1)S(1)}, bf16[216,128]{1,0:T(8,128)(2,1)S(1)}, u32[]{:S(2)}, u32[]{:S(2)}) collective-permute-start(bf16[216,128]{1,0:T(8,128)(2,1)S(1)} %pad_maximum_fusion), channel_id=1, source_target_pairs={{0,4},{1,5},{2,6},{3,7},{4,0},{5,1},{6,2},{7,3},{8,12},{9,13},{10,... | collective-permute-start | bytes 165896 | tf_op jit(solution)/shard_map/ppermute | solution.py:750
  59.0 5.8 %collective-permute-start.10 = (bf16[480,128]{1,0:T(8,128)(2,1)S(1)}, bf16[480,128]{1,0:T(8,128)(2,1)S(1)}, u32[]{:S(2)}, u32[]{:S(2)}) collective-permute-start(bf16[480,128]{1,0:T(8,128)(2,1)S(1)} %concatenate.15.refs_0_), channel_id=1, source_target_pairs={{0,3},{1,2},{2,1},{3,0},{4,7},{5,6},{6,5},{7,4},{8,11},{9,10},{10,... | collective-permute-start | bytes 368648 | tf_op jit(solution)/shard_map/ppermute | solution.py:750
  61.4 4.9 %collective-permute-start.8 = (bf16[480,128]{1,0:T(8,128)(2,1)S(1)}, bf16[480,128]{1,0:T(8,128)(2,1)S(1)}, u32[]{:S(2)}, u32[]{:S(2)}) collective-permute-start(bf16[480,128]{1,0:T(8,128)(2,1)S(1)} %concatenate.15.refs_0_), channel_id=1, source_target_pairs={{0,1},{1,0},{2,3},{3,2},{4,5},{5,4},{6,7},{7,6},{8,9},{9,8},{10,11... | collective-permute-start | bytes 368648 | tf_op jit(solution)/shard_map/ppermute | solution.py:750
  61.9 4.9 %collective-permute-start.9 = (bf16[480,128]{1,0:T(8,128)(2,1)S(1)}, bf16[480,128]{1,0:T(8,128)(2,1)S(1)}, u32[]{:S(2)}, u32[]{:S(2)}) collective-permute-start(bf16[480,128]{1,0:T(8,128)(2,1)S(1)} %concatenate.15.refs_0_), channel_id=1, source_target_pairs={{0,2},{1,3},{2,0},{3,1},{4,6},{5,7},{6,4},{7,5},{8,10},{9,11},{10,... | collective-permute-start | bytes 368648 | tf_op jit(solution)/shard_map/ppermute | solution.py:750

commit v6 on v5

--- a/solution.py
+++ b/solution.py
@@ -55,31 +55,31 @@
     return ((dr // 2) * 3 + dc) * 16 + (dr % 2) * 8
 
 
-def rows_kernel(image, mask, codes, others, tile, near):
+def fitted(code):
+    return jnp.where(code < 256, code, code - 512).astype(F32)
+
+
+def rows_kernel(_, others, tile, near):
     level = lax.axis_index("level")
-    batches, _, band, _ = image.shape
-
-    def fitted(code):
-        return jnp.where(code < 256, code, code - 512).astype(F32)
-
+    _, batches, band, _ = others.shape
     for b in range(batches):
-        base = b * band * 8
-        shown = image[b].astype(F32)
-        for c in range(3):
-            tile[pl.ds(base + c, band, stride=8), :] = shown[c]
-        tile[pl.ds(base + 3, band, stride=8), :] = mask[b].astype(F32)
-        mine, theirs = fitted(codes[0, b]), fitted(others[0, b])
-        tile[pl.ds(base + 4, band, stride=8), :] = jnp.where(level == 1, mine, theirs)
-        tile[pl.ds(base + 5, band, stride=8), :] = jnp.where(level == 1, theirs, mine)
-        for c in range(6, 8):
-            tile[pl.ds(base + c, band, stride=8), :] = jnp.zeros((band, W), F32)
+        bottom_rows, top_rows = (pl.ds(b * band * 8 + c, band, stride=8) for c in (4, 5))
+        mine, theirs = tile[bottom_rows, :], fitted(others[0, b])
+        tile[bottom_rows, :] = jnp.where(level == 1, mine, theirs)
+        tile[top_rows, :] = jnp.where(level == 1, theirs, mine)
     for b in range(batches):
         row = jnp.where(level == 0, band - 2, 0)
         start = pl.multiple_of((b * band + row) * 8, 8)
         near[b * 16 : (b + 1) * 16] = tile[pl.ds(start, 16), :].astype(BF)
 
 
-def pack_kernel(count, total, enc, lat, dec, read, pack, flat):
+def pack_kernel(image, mask, codes, count, total, enc, lat, dec, read, pack, tile, flat):
+    batches, _, band, _ = image.shape
+    for b in range(batches):
+        planes = [image[b, c].astype(F32) for c in range(3)] + [mask[b].astype(F32), fitted(codes[0, b])]
+        planes += [jnp.zeros((band, W), F32)] * 3
+        for c, plane in enumerate(planes):
+            tile[pl.ds(b * band * 8 + c, band, stride=8), :] = plane
     pack[0:TAPS] = dec[0].astype(BF)
     flat[...] = jnp.zeros_like(flat)
     for t in range(9):
@@ -617,23 +617,28 @@
 
     swap = [(0, 1), (1, 0)]
     others = lax.ppermute(codes, "level", swap)
-    weights = outside(ema_count, ema_sum, encoder_weight, latent_weight, decoder_weight, readout_weight)
-    pack = pl.pallas_call(
+    tiled = pltpu.VMEM((batches * band * 8, W), F32)
+    pack, tile = pl.pallas_call(
         pack_kernel,
-        out_shape=pltpu.VMEM((PACKED, W), BF),
-        in_specs=[VMEM] * 6,
-        out_specs=VMEM,
+        out_shape=[pltpu.VMEM((PACKED, W), BF), tiled],
+        in_specs=[VMEM] * 9,
+        out_specs=[VMEM] * 2,
         scratch_shapes=[pltpu.VMEM((128, 128), F32)],
         compiler_params=limit(56),
-    )(*weights)
-    others, pack = lax.optimization_barrier((others, pack))
+    )(
+        *outside(
+            image, mask, codes, ema_count, ema_sum, encoder_weight, latent_weight, decoder_weight, readout_weight
+        )
+    )
+    others, pack, tile = lax.optimization_barrier((others, pack, tile))
     tile, near = pl.pallas_call(
         rows_kernel,
-        out_shape=[pltpu.VMEM((batches * band * 8, W), F32), pltpu.VMEM((batches * 16, W), BF)],
-        in_specs=[VMEM] * 4,
+        out_shape=[tiled, pltpu.VMEM((batches * 16, W), BF)],
+        in_specs=[VMEM] * 2,
         out_specs=[VMEM] * 2,
-        compiler_params=limit(56),
-    )(*outside(image, mask, codes), others)
+        input_output_aliases={0: 0},
+        compiler_params=limit(32),
+    )(inside_vmem(tile), inside_vmem(others))
 
     both = ("level", "dp")
     inside = [d for d in range(1, devices) if (d + 1) * band % CROP != 0]

time: 69.5 us -> 68.4 us (0.984)
  Pallas kernels: 36.4 us -> 35.5 us
    pallas_call x2, Pallas kernels: 2.33 us -> 1.42 us  [the longest x1 1.39 us: local(): pl.pallas_call(pack_kernel, out_shape=[pltpu.VMEM((PACKED, W), BF), tiled...]
  transfers between devices with their start and end apart: 12 -> 12, of which waited for: 8 -> 8; matrix products, arithmetic and copies ran while one was open for 0% -> 0% of each run, Pallas kernels for 28% -> 27%
where the time goes in v6:
time: 68.4 us; the launch traced here: 68.2 us
  Pallas kernels  35.5 us (52%)
  starting transfers between devices  19.5 us (29%)
  waiting for transfers between devices  11.5 us (17%)
  between operations  1.2 us (2%)
    pallas_call x1, Pallas kernels, local(): pl.pallas_call(functools.partial(step_kernel, batches=batches, rows=rows)...  14.1 us
    pallas_call x1, Pallas kernels, local(): pl.pallas_call(functools.partial(back_kernel, batches=batches, rows=rows)...  9.5 us
    ppermute x6, starting transfers between devices, local(): lax.ppermute(payload, both, xor_pairs(devices, k << start, k << other))  7.99 us
    pallas_call x1, Pallas kernels, local(): pl.pallas_call(functools.partial(early_kernel, batches=batches, rows=rows...  7.46 us
    ppermute x6, waiting for transfers between devices, local(): lax.ppermute(payload, both, xor_pairs(devices, k << start, k << other))  7.4 us
    all_to_all x1, starting transfers between devices, local(): big = lax.all_to_all(big.reshape(devices, size, W), 'dp', 0, 0)  5.92 us
    ppermute x1, starting transfers between devices, local(): near = lax.ppermute(near, both, pairs)  4.84 us
    ppermute x2, waiting for transfers between devices, local(): got = lax.ppermute(send, 'level', swap)  2.83 us
  transfers between devices with their start and end apart: 12, of which 8 were waited for; matrix products, arithmetic and copies ran while one was open for 0% of the time, Pallas kernels for 27%

profile of v6, /device:TPU:0, one launch (start us, length us, event | category | flops | bytes accessed | tf_op | source)
XLA Modules:
  0.0 68.2 jit_solution(12573615975534301286)
XLA Ops:
  0.7 0.5 collective-permute-start
  1.2 1.4 %shard_map.320 = (bf16[1744,128]{1,0:T(8,128)(2,1)S(1)}, f32[768,128]{1,0:T(8,128)S(1)}) custom-call(bf16[3,3,32,128]{3,2,1,0:T(8,128)(2,1)} %image.1, s32[3,32,128]{2,1,0:T(8,128)} %mask.1, s32[1,3,32,128]{3,2,1,0:T(8,128)} %codes.1, f32[1,512]{1,0:T(1,128)} %refs_4_.1, f32[1,64,512]{2,1,0:T(8,128)} %bitcast.40, f32[27,1,128]{2,1,0:T(1,128)} %bitcast.44, ...), custom_call_target="tpu_custom_call" | custom-call | tf_op jit(solution)/shard_map/pallas_call | solution.py:621
  2.6 0.0 collective-permute-done.others
  2.6 0.1 collective-permute-start.2
  2.7 4.8 %collective-permute-start.1 = (bf16[48,128]{1,0:T(8,128)(2,1)S(1)}, bf16[48,128]{1,0:T(8,128)(2,1)S(1)}, u32[]{:S(2)}, u32[]{:S(2)}) collective-permute-start(bf16[48,128]{1,0:T(8,128)(2,1)S(1)} %get-tuple-element.73), channel_id=1, source_target_pairs={{0,1},{1,2},{3,4},{4,5},{5,6},{7,8},{8,9},{9,10},{11,12},{12,13},{... | collective-permute-start | bytes 36872 | tf_op jit(solution)/shard_map/ppermute | solution.py:646
  7.6 0.0 collective-permute-done.2.theirs
  7.6 7.5 %shard_map.322 = (bf16[3,128,7680]{2,1,0:T(8,128)(2,1)S(1)}, bf16[3,256,2048]{2,1,0:T(8,128)(2,1)S(1)}, f32[3,256,2048]{2,1,0:T(8,128)S(1)}, f32[3,128,2048]{2,1...) custom-call(f32[768,128]{1,0:T(8,128)S(1)} %get-tuple-element.72.tile, ...), custom_call_target="tpu_custom_call" | custom-call | flops 3221225472 | bytes 1048576 | tf_op jit(solution)/shard_map/pallas_call | solution.py:670
  15.1 0.0 collective-permute-done.1.near
  15.1 14.1 %shard_map.323 = (f32[1408,128]{1,0:T(8,128)S(1)}, bf16[32,128]{1,0:T(8,128)(2,1)S(1)}, bf16[1440,128]{1,0:T(8,128)(2,1)S(1)}, bf16[3,256,2048]{2,1,0:T(8,128)(2...) custom-call(f32[768,128]{1,0:T(8,128)S(1)} %get-tuple-element.72.til, ...), custom_call_target="tpu_custom_call", output_to_operand_aliasing={{10}: (4, {}), {11}: (5, {}), {12}: (6, {}), {13}: (7, {}),... | custom-call | tf_op jit(solution)/shard_map/pallas_call | solution.py:679
  29.2 0.1 collective-permute-start.3
  29.3 1.7 %collective-permute-done.3.got._ = bf16[1440,128]{1,0:T(8,128)(2,1)S(1)} collective-permute-done((bf16[1440,128]{1,0:T(8,128)(2,1)S(1)}, bf16[1440,128]{1,0:T(8,128)(2,1)S(1)}, u32[]{:S(2)}, u32[]{:S(2)}) %collective-permute-start.3) | collective-permute-done | bytes 368672 | tf_op jit(solution)/shard_map/ppermute | solution.py:710
  31.0 0.9 %shard_map.324 = (bf16[1408,128]{1,0:T(8,128)(2,1)}, bf16[32,128]{1,0:T(8,128)(2,1)S(1)}) custom-call(f32[1408,128]{1,0:T(8,128)S(1)} %get-tuple-element.82.keep, bf16[32,128]{1,0:T(8,128)(2,1)S(1)} %get-tuple-element.83.early, bf16[1440,128]{1,0:T(8,128)(2,1)S(1)} %collective-permute-done.3.got._), custom_call_target="tpu_custom_call" | custom-call | tf_op jit(solution)/shard_map/pallas_call | solution.py:711
  31.8 5.9 %all-to-all-start = ((bf16[16,88,128]{2,1,0:T(8,128)(2,1)}), bf16[16,88,128]{2,1,0:T(8,128)(2,1)S(1)}, u32[]{:S(2)}, u32[]{:S(2)}) async-start(bf16[16,88,128]{2,1,0:T(8,128)(2,1)} %bitcast.4), calls=%async_computation | async-start | bytes 720896 | tf_op jit(solution)/shard_map/all_to_all | solution.py:718
  37.7 0.0 copy-done.4
  37.7 9.5 %shard_map.326 = (bf16[96,128]{1,0:T(8,128)(2,1)S(1)}, bf16[96,128]{1,0:T(8,128)(2,1)S(1)}) custom-call(bf16[3,256,2048]{2,1,0:T(8,128)(2,1)} %get-tuple-element.86.h_in, f32[3,256,2048]{2,1,0:T(8,128)} %get-tuple-element.87.slope_in, f32[3,128,2048]{2,1,0:T(8,128)} %get-tuple-element.88.gap_in, bf16[3,256,2304]{2,1,0:T(8,128)(2,1)} %get-tuple-element.89.da_in, ...), custom_call_target="tpu_custom_call" | custom-call | flops 4831838208 | bytes 1048576 | tf_op jit(solution)/shard_map/pallas_call | solution.py:720
  47.3 0.1 collective-permute-start.4
  47.4 1.2 %collective-permute-done.4 = bf16[96,128]{1,0:T(8,128)(2,1)S(1)} collective-permute-done((bf16[96,128]{1,0:T(8,128)(2,1)S(1)}, bf16[96,128]{1,0:T(8,128)(2,1)S(1)}, u32[]{:S(2)}, u32[]{:S(2)}) %collective-permute-start.4) | collective-permute-done | bytes 24608 | tf_op jit(solution)/shard_map/ppermute | solution.py:735
  48.5 0.0 copy-start
  48.5 0.0 copy-start.1
  48.6 0.0 copy-start.2
  48.6 0.0 copy-start.3
  48.6 0.0 copy-start.5
  48.6 0.0 copy-start.6
  48.6 0.0 copy-start.7
  48.6 0.0 copy-start.8
  48.6 0.0 copy-start.9
  48.6 0.0 copy-start.10
  48.7 0.0 copy-start.11
  48.7 0.0 copy-start.12
  48.7 0.0 copy-start.13
  48.7 0.0 copy-start.14
  48.7 1.3 %all-to-all-done.parts = bf16[16,88,128]{2,1,0:T(8,128)(2,1)S(1)} async-done(((bf16[16,88,128]{2,1,0:T(8,128)(2,1)}), bf16[16,88,128]{2,1,0:T(8,128)(2,1)S(1)}, u32[]{:S(2)}, u32[]{:S(2)}) %all-to-all-start) | async-done | bytes 360480 | tf_op jit(solution)/shard_map/all_to_all | solution.py:718
  50.0 0.1 shard_map.325
  50.1 2.5 %collective-permute-start.5 = (bf16[216,128]{1,0:T(8,128)(2,1)S(1)}, bf16[216,128]{1,0:T(8,128)(2,1)S(1)}, u32[]{:S(2)}, u32[]{:S(2)}) collective-permute-start(bf16[216,128]{1,0:T(8,128)(2,1)S(1)} %pad_maximum_fusion), channel_id=1, source_target_pairs={{0,12},{1,13},{2,14},{3,15},{4,8},{5,9},{6,10},{7,11},{8,4},{9,5},... | collective-permute-start | bytes 165896 | tf_op jit(solution)/shard_map/ppermute | solution.py:755
  52.6 0.1 collective-permute-start.6
  52.6 1.9 %collective-permute-start.7 = (bf16[216,128]{1,0:T(8,128)(2,1)S(1)}, bf16[216,128]{1,0:T(8,128)(2,1)S(1)}, u32[]{:S(2)}, u32[]{:S(2)}) collective-permute-start(bf16[216,128]{1,0:T(8,128)(2,1)S(1)} %pad_maximum_fusion), channel_id=1, source_target_pairs={{0,4},{1,5},{2,6},{3,7},{4,0},{5,1},{6,2},{7,3},{8,12},{9,13},{10,... | collective-permute-start | bytes 165896 | tf_op jit(solution)/shard_map/ppermute | solution.py:755
  54.5 1.5 %collective-permute-done.5 = bf16[216,128]{1,0:T(8,128)(2,1)S(1)} collective-permute-done((bf16[216,128]{1,0:T(8,128)(2,1)S(1)}, bf16[216,128]{1,0:T(8,128)(2,1)S(1)}, u32[]{:S(2)}, u32[]{:S(2)}) %collective-permute-start.5) | collective-permute-done | bytes 55328 | tf_op jit(solution)/shard_map/ppermute | solution.py:755
  56.1 1.5 %collective-permute-done.6 = bf16[216,128]{1,0:T(8,128)(2,1)S(1)} collective-permute-done((bf16[216,128]{1,0:T(8,128)(2,1)S(1)}, bf16[216,128]{1,0:T(8,128)(2,1)S(1)}, u32[]{:S(2)}, u32[]{:S(2)}) %collective-permute-start.6) | collective-permute-done | bytes 55328 | tf_op jit(solution)/shard_map/ppermute | solution.py:755
  57.6 0.0 collective-permute-done.7
  57.8 0.2 concatenate.15.refs_0_
  57.9 2.4 %collective-permute-start.10 = (bf16[480,128]{1,0:T(8,128)(2,1)S(1)}, bf16[480,128]{1,0:T(8,128)(2,1)S(1)}, u32[]{:S(2)}, u32[]{:S(2)}) collective-permute-start(bf16[480,128]{1,0:T(8,128)(2,1)S(1)} %concatenate.15.refs_0_), channel_id=1, source_target_pairs={{0,3},{1,2},{2,1},{3,0},{4,7},{5,6},{6,5},{7,4},{8,11},{9,10},{10,... | collective-permute-start | bytes 368648 | tf_op jit(solution)/shard_map/ppermute | solution.py:755
  60.3 0.6 collective-permute-start.8
  60.9 0.6 collective-permute-start.9
  61.5 2.3 %collective-permute-done.10.refs_3_ = bf16[480,128]{1,0:T(8,128)(2,1)S(1)} collective-permute-done((bf16[480,128]{1,0:T(8,128)(2,1)S(1)}, bf16[480,128]{1,0:T(8,128)(2,1)S(1)}, u32[]{:S(2)}, u32[]{:S(2)}) %collective-permute-start.10) | collective-permute-done | bytes 122912 | tf_op jit(solution)/shard_map/ppermute | solution.py:755
  63.8 1.5 %collective-permute-done.8.refs_1_ = bf16[480,128]{1,0:T(8,128)(2,1)S(1)} collective-permute-done((bf16[480,128]{1,0:T(8,128)(2,1)S(1)}, bf16[480,128]{1,0:T(8,128)(2,1)S(1)}, u32[]{:S(2)}, u32[]{:S(2)}) %collective-permute-start.8) | collective-permute-done | bytes 122912 | tf_op jit(solution)/shard_map/ppermute | solution.py:755
  65.2 0.6 collective-permute-done.9.refs_2_
  65.8 0.0 copy-done.3
  65.9 2.1 %shard_map.327 = (f32[1,1]{1,0:T(1,128)}, f32[1,1]{1,0:T(1,128)}, f32[1,512]{1,0:T(1,128)}, f32[1,64,512]{2,1,0:T(8,128)}, f32[27,1,128]{2,1,0:T(1,128)}, /*inde...) custom-call(bf16[480,128]{1,0:T(8,128)(2,1)S(1)} %concatenate.15.ref, ...), custom_call_target="tpu_custom_call" | custom-call | tf_op jit(solution)/shard_map/pallas_call | solution.py:778
  (27 shorter events, 0.2 us)
Async XLA Ops:
  0.7 1.9 %collective-permute-start = (s32[1,3,32,128]{3,2,1,0:T(8,128)}, s32[1,3,32,128]{3,2,1,0:T(8,128)S(1)}, u32[]{:S(2)}, u32[]{:S(2)}) collective-permute-start(s32[1,3,32,128]{3,2,1,0:T(8,128)} %codes.1), channel_id=1, source_target_pairs={{0,16},{16,0},{1,17},{17,1},{2,18},{18,2},{3,19},{19,3},{4,20},{20... | collective-permute-start | bytes 147464 | tf_op jit(solution)/shard_map/ppermute | solution.py:619
  2.6 5.0 %collective-permute-start.2 = (bf16[1744,128]{1,0:T(8,128)(2,1)S(1)}, bf16[1744,128]{1,0:T(8,128)(2,1)S(1)}, u32[]{:S(2)}, u32[]{:S(2)}) collective-permute-start(bf16[1744,128]{1,0:T(8,128)(2,1)S(1)} %get-tuple-element.74.mine), channel_id=1, source_target_pairs={{0,16},{16,0},{1,17},{17,1},{2,18},{18,2},{3,19},{19,3},{4,20},{20... | collective-permute-start | bytes 1339400 | tf_op jit(solution)/shard_map/ppermute | solution.py:647
  2.7 12.3 %collective-permute-start.1 = (bf16[48,128]{1,0:T(8,128)(2,1)S(1)}, bf16[48,128]{1,0:T(8,128)(2,1)S(1)}, u32[]{:S(2)}, u32[]{:S(2)}) collective-permute-start(bf16[48,128]{1,0:T(8,128)(2,1)S(1)} %get-tuple-element.73), channel_id=1, source_target_pairs={{0,1},{1,2},{3,4},{4,5},{5,6},{7,8},{8,9},{9,10},{11,12},{12,13},{... | collective-permute-start | bytes 36872 | tf_op jit(solution)/shard_map/ppermute | solution.py:646
  29.2 1.8 %collective-permute-start.3 = (bf16[1440,128]{1,0:T(8,128)(2,1)S(1)}, bf16[1440,128]{1,0:T(8,128)(2,1)S(1)}, u32[]{:S(2)}, u32[]{:S(2)}) collective-permute-start(bf16[1440,128]{1,0:T(8,128)(2,1)S(1)} %get-tuple-element.84), channel_id=1, source_target_pairs={{0,16},{16,0},{1,17},{17,1},{2,18},{18,2},{3,19},{19,3},{4,20},{20... | collective-permute-start | bytes 1105928 | tf_op jit(solution)/shard_map/ppermute | solution.py:710
  31.0 6.8 %copy-start.4 = (bf16[1440,128]{1,0:T(8,128)(2,1)}, bf16[1440,128]{1,0:T(8,128)(2,1)S(1)}, u32[]{:S(2)}) copy-start(bf16[1440,128]{1,0:T(8,128)(2,1)S(1)} %collective-permute-done.3.got._) | copy-start | bytes 1105924
  31.8 18.2 %all-to-all-start = ((bf16[16,88,128]{2,1,0:T(8,128)(2,1)}), bf16[16,88,128]{2,1,0:T(8,128)(2,1)S(1)}, u32[]{:S(2)}, u32[]{:S(2)}) async-start(bf16[16,88,128]{2,1,0:T(8,128)(2,1)} %bitcast.4), calls=%async_computation | async-start | bytes 720896 | tf_op jit(solution)/shard_map/all_to_all | solution.py:718
  47.3 1.3 %collective-permute-start.4 = (bf16[96,128]{1,0:T(8,128)(2,1)S(1)}, bf16[96,128]{1,0:T(8,128)(2,1)S(1)}, u32[]{:S(2)}, u32[]{:S(2)}) collective-permute-start(bf16[96,128]{1,0:T(8,128)(2,1)S(1)} %get-tuple-element.94), channel_id=1, source_target_pairs={{0,16},{16,0},{1,17},{17,1},{2,18},{18,2},{3,19},{19,3},{4,20},{20... | collective-permute-start | bytes 73736 | tf_op jit(solution)/shard_map/ppermute | solution.py:735
  48.5 17.3 %copy-start = (f32[1,1152,128]{2,1,0:T(8,128)S(1)}, f32[1,1152,128]{2,1,0:T(8,128)}, u32[]{:S(2)}) copy-start(f32[1,1152,128]{2,1,0:T(8,128)} %refs_12_.1) | copy-start | bytes 1769476
  48.5 17.2 %copy-start.1 = (f32[1,1152,128]{2,1,0:T(8,128)S(1)}, f32[1,1152,128]{2,1,0:T(8,128)}, u32[]{:S(2)}) copy-start(f32[1,1152,128]{2,1,0:T(8,128)} %refs_13_.1) | copy-start | bytes 1769476
  48.6 17.2 %copy-start.2 = (f32[1,1152,128]{2,1,0:T(8,128)S(1)}, f32[1,1152,128]{2,1,0:T(8,128)}, u32[]{:S(2)}) copy-start(f32[1,1152,128]{2,1,0:T(8,128)} %refs_14_.1) | copy-start | bytes 1769476
  48.6 17.2 %copy-start.3 = (f32[1,512,64]{1,2,0:T(8,128)S(1)}, f32[1,512,64]{1,2,0:T(8,128)}, u32[]{:S(2)}) copy-start(f32[1,512,64]{1,2,0:T(8,128)} %param.21) | copy-start | bytes 393220
  48.6 17.2 %copy-start.5 = (f32[1,128,64]{1,2,0:T(8,128)S(1)}, f32[1,128,64]{1,2,0:T(8,128)}, u32[]{:S(2)}) copy-start(f32[1,128,64]{1,2,0:T(8,128)} %param.25) | copy-start | bytes 98308
  48.6 17.2 %copy-start.6 = (f32[1,27,128]{2,0,1:T(1,128)S(1)}, f32[1,27,128]{2,0,1:T(1,128)}, u32[]{:S(2)}) copy-start(f32[1,27,128]{2,0,1:T(1,128)} %param.22) | copy-start | bytes 41476
  48.6 17.2 %copy-start.7 = (f32[1,128,64]{1,2,0:T(8,128)S(1)}, f32[1,128,64]{1,2,0:T(8,128)}, u32[]{:S(2)}) copy-start(f32[1,128,64]{1,2,0:T(8,128)} %param.26) | copy-start | bytes 98308
  48.6 17.2 %copy-start.8 = (f32[1,128,64]{1,2,0:T(8,128)S(1)}, f32[1,128,64]{1,2,0:T(8,128)}, u32[]{:S(2)}) copy-start(f32[1,128,64]{1,2,0:T(8,128)} %param.27) | copy-start | bytes 98308
  48.6 17.2 %copy-start.9 = (f32[1,27,128]{2,0,1:T(1,128)S(1)}, f32[1,27,128]{2,0,1:T(1,128)}, u32[]{:S(2)}) copy-start(f32[1,27,128]{2,0,1:T(1,128)} %param.23) | copy-start | bytes 41476
  48.6 17.2 %copy-start.10 = (f32[1,27,128]{2,0,1:T(1,128)S(1)}, f32[1,27,128]{2,0,1:T(1,128)}, u32[]{:S(2)}) copy-start(f32[1,27,128]{2,0,1:T(1,128)} %param.24) | copy-start | bytes 41476
  48.7 17.2 %copy-start.11 = (f32[1,512]{1,0:T(1,128)S(1)}, f32[1,512]{1,0:T(1,128)}, u32[]{:S(2)}) copy-start(f32[1,512]{1,0:T(1,128)} %refs_4_.1) | copy-start | bytes 6148
  48.7 17.2 %copy-start.12 = (f32[1,128,3]{1,0,2:T(1,128)S(1)}, f32[1,128,3]{1,0,2:T(1,128)}, u32[]{:S(2)}) copy-start(f32[1,128,3]{1,0,2:T(1,128)} %param.31) | copy-start | bytes 4612
  48.7 17.2 %copy-start.13 = (f32[1,128,3]{1,0,2:T(1,128)S(1)}, f32[1,128,3]{1,0,2:T(1,128)}, u32[]{:S(2)}) copy-start(f32[1,128,3]{1,0,2:T(1,128)} %param.32) | copy-start | bytes 4612
  48.7 17.2 %copy-start.14 = (f32[1,128,3]{1,0,2:T(1,128)S(1)}, f32[1,128,3]{1,0,2:T(1,128)}, u32[]{:S(2)}) copy-start(f32[1,128,3]{1,0,2:T(1,128)} %param.33) | copy-start | bytes 4612
  50.1 6.0 %collective-permute-start.5 = (bf16[216,128]{1,0:T(8,128)(2,1)S(1)}, bf16[216,128]{1,0:T(8,128)(2,1)S(1)}, u32[]{:S(2)}, u32[]{:S(2)}) collective-permute-start(bf16[216,128]{1,0:T(8,128)(2,1)S(1)} %pad_maximum_fusion), channel_id=1, source_target_pairs={{0,12},{1,13},{2,14},{3,15},{4,8},{5,9},{6,10},{7,11},{8,4},{9,5},... | collective-permute-start | bytes 165896 | tf_op jit(solution)/shard_map/ppermute | solution.py:755
  52.6 5.1 %collective-permute-start.6 = (bf16[216,128]{1,0:T(8,128)(2,1)S(1)}, bf16[216,128]{1,0:T(8,128)(2,1)S(1)}, u32[]{:S(2)}, u32[]{:S(2)}) collective-permute-start(bf16[216,128]{1,0:T(8,128)(2,1)S(1)} %pad_maximum_fusion), channel_id=1, source_target_pairs={{0,8},{1,9},{2,10},{3,11},{4,12},{5,13},{6,14},{7,15},{8,0},{9,1},... | collective-permute-start | bytes 165896 | tf_op jit(solution)/shard_map/ppermute | solution.py:755
  52.6 5.0 %collective-permute-start.7 = (bf16[216,128]{1,0:T(8,128)(2,1)S(1)}, bf16[216,128]{1,0:T(8,128)(2,1)S(1)}, u32[]{:S(2)}, u32[]{:S(2)}) collective-permute-start(bf16[216,128]{1,0:T(8,128)(2,1)S(1)} %pad_maximum_fusion), channel_id=1, source_target_pairs={{0,4},{1,5},{2,6},{3,7},{4,0},{5,1},{6,2},{7,3},{8,12},{9,13},{10,... | collective-permute-start | bytes 165896 | tf_op jit(solution)/shard_map/ppermute | solution.py:755
  57.9 5.8 %collective-permute-start.10 = (bf16[480,128]{1,0:T(8,128)(2,1)S(1)}, bf16[480,128]{1,0:T(8,128)(2,1)S(1)}, u32[]{:S(2)}, u32[]{:S(2)}) collective-permute-start(bf16[480,128]{1,0:T(8,128)(2,1)S(1)} %concatenate.15.refs_0_), channel_id=1, source_target_pairs={{0,3},{1,2},{2,1},{3,0},{4,7},{5,6},{6,5},{7,4},{8,11},{9,10},{10,... | collective-permute-start | bytes 368648 | tf_op jit(solution)/shard_map/ppermute | solution.py:755
  60.3 4.9 %collective-permute-start.8 = (bf16[480,128]{1,0:T(8,128)(2,1)S(1)}, bf16[480,128]{1,0:T(8,128)(2,1)S(1)}, u32[]{:S(2)}, u32[]{:S(2)}) collective-permute-start(bf16[480,128]{1,0:T(8,128)(2,1)S(1)} %concatenate.15.refs_0_), channel_id=1, source_target_pairs={{0,1},{1,0},{2,3},{3,2},{4,5},{5,4},{6,7},{7,6},{8,9},{9,8},{10,11... | collective-permute-start | bytes 368648 | tf_op jit(solution)/shard_map/ppermute | solution.py:755
  60.9 4.9 %collective-permute-start.9 = (bf16[480,128]{1,0:T(8,128)(2,1)S(1)}, bf16[480,128]{1,0:T(8,128)(2,1)S(1)}, u32[]{:S(2)}, u32[]{:S(2)}) collective-permute-start(bf16[480,128]{1,0:T(8,128)(2,1)S(1)} %concatenate.15.refs_0_), channel_id=1, source_target_pairs={{0,2},{1,3},{2,0},{3,1},{4,6},{5,7},{6,4},{7,5},{8,10},{9,11},{10,... | collective-permute-start | bytes 368648 | tf_op jit(solution)/shard_map/ppermute | solution.py:755

commit v7 on v6

--- a/solution.py
+++ b/solution.py
@@ -226,12 +226,12 @@
             [item[:, inner] for item in onehots], [item[:, inner] for item in highs], et, zt, g_s,
         )
         h_s[b] = h
-        slope_s[b] = slope
+        slope_s[b] = slope.astype(BF)
         gap_s[b] = gap
         l_s[0:128] += fold(error, 256)
         return 0
 
-    lax.fori_loop(0, batches, batch, 0)
+    lax.fori_loop(0, batches, batch, 0, unroll=True)
 
 
 def patches(x_s, row, n):
@@ -356,7 +356,7 @@
     for b in range(batches):
         cols = slice(b * W, (b + 1) * W)
         h_s[b, :, at(edge, 1)] = h[:, cols]
-        slope_s[b, :, at(edge, 1)] = slope[:, cols]
+        slope_s[b, :, at(edge, 1)] = slope[:, cols].astype(BF)
         gap_s[b, :, at(edge, 1)] = gap[:, cols]
 
     pairs = ((h_s, h_out), (slope_s, slope_out), (gap_s, gap_out), (da_s, da_out))
@@ -652,7 +652,7 @@
     framed = batches * (rows + 2) * W
     held = [
         ((batches, 256, rows * W), BF),
-        ((batches, 256, rows * W), F32),
+        ((batches, 256, rows * W), BF),
         ((batches, 128, rows * W), F32),
         ((batches, 256, (rows + 2) * W), BF),
     ]

time: 68.4 us -> 67.4 us (0.985)
  Pallas kernels: 35.5 us -> 34.5 us
    pallas_call x1, Pallas kernels: 7.46 us -> 6.71 us  [local(): pl.pallas_call(functools.partial(early_kernel, batches=batches, rows=rows...]
  transfers between devices with their start and end apart: 12 -> 12, of which waited for: 8 -> 8; matrix products, arithmetic and copies ran while one was open for 0% -> 0% of each run, Pallas kernels for 27% -> 26%
where the time goes in v7:
time: 67.4 us; the launch traced here: 67.2 us
  Pallas kernels  34.5 us (51%)
  starting transfers between devices  19.5 us (29%)
  waiting for transfers between devices  11.5 us (17%)
  between operations  1.21 us (2%)
    pallas_call x1, Pallas kernels, local(): pl.pallas_call(functools.partial(step_kernel, batches=batches, rows=rows)...  14.1 us
    pallas_call x1, Pallas kernels, local(): pl.pallas_call(functools.partial(back_kernel, batches=batches, rows=rows)...  9.24 us
    ppermute x6, starting transfers between devices, local(): lax.ppermute(payload, both, xor_pairs(devices, k << start, k << other))  7.99 us
    ppermute x6, waiting for transfers between devices, local(): lax.ppermute(payload, both, xor_pairs(devices, k << start, k << other))  7.12 us
    pallas_call x1, Pallas kernels, local(): pl.pallas_call(functools.partial(early_kernel, batches=batches, rows=rows...  6.71 us
    all_to_all x1, starting transfers between devices, local(): big = lax.all_to_all(big.reshape(devices, size, W), 'dp', 0, 0)  5.93 us
    ppermute x1, starting transfers between devices, local(): near = lax.ppermute(near, both, pairs)  4.84 us
    ppermute x2, waiting for transfers between devices, local(): got = lax.ppermute(send, 'level', swap)  2.83 us
  transfers between devices with their start and end apart: 12, of which 8 were waited for; matrix products, arithmetic and copies ran while one was open for 0% of the time, Pallas kernels for 26%

profile of v7, /device:TPU:0, one launch (start us, length us, event | category | flops | bytes accessed | tf_op | source)
XLA Modules:
  0.0 67.2 jit_solution(8864459158247706447)
XLA Ops:
  0.7 0.5 collective-permute-start
  1.2 1.4 %shard_map.320 = (bf16[1744,128]{1,0:T(8,128)(2,1)S(1)}, f32[768,128]{1,0:T(8,128)S(1)}) custom-call(bf16[3,3,32,128]{3,2,1,0:T(8,128)(2,1)} %image.1, s32[3,32,128]{2,1,0:T(8,128)} %mask.1, s32[1,3,32,128]{3,2,1,0:T(8,128)} %codes.1, f32[1,512]{1,0:T(1,128)} %refs_4_.1, f32[1,64,512]{2,1,0:T(8,128)} %bitcast.40, f32[27,1,128]{2,1,0:T(1,128)} %bitcast.44, ...), custom_call_target="tpu_custom_call" | custom-call | tf_op jit(solution)/shard_map/pallas_call | solution.py:621
  2.6 0.0 collective-permute-done.others
  2.6 0.1 collective-permute-start.2
  2.7 4.8 %collective-permute-start.1 = (bf16[48,128]{1,0:T(8,128)(2,1)S(1)}, bf16[48,128]{1,0:T(8,128)(2,1)S(1)}, u32[]{:S(2)}, u32[]{:S(2)}) collective-permute-start(bf16[48,128]{1,0:T(8,128)(2,1)S(1)} %get-tuple-element.73), channel_id=1, source_target_pairs={{0,1},{1,2},{3,4},{4,5},{5,6},{7,8},{8,9},{9,10},{11,12},{12,13},{... | collective-permute-start | bytes 36872 | tf_op jit(solution)/shard_map/ppermute | solution.py:646
  7.6 0.0 collective-permute-done.2.theirs
  7.6 6.7 %shard_map.322 = (bf16[3,128,7680]{2,1,0:T(8,128)(2,1)S(1)}, bf16[3,256,2048]{2,1,0:T(8,128)(2,1)S(1)}, bf16[3,256,2048]{2,1,0:T(8,128)(2,1)S(1)}, f32[3,128,204...) custom-call(f32[768,128]{1,0:T(8,128)S(1)} %get-tuple-element.72.tile, ...), custom_call_target="tpu_custom_call" | custom-call | flops 3221225472 | bytes 1048576 | tf_op jit(solution)/shard_map/pallas_call | solution.py:670
  14.3 0.0 collective-permute-done.1.near
  14.3 14.1 %shard_map.323 = (f32[1408,128]{1,0:T(8,128)S(1)}, bf16[32,128]{1,0:T(8,128)(2,1)S(1)}, bf16[1440,128]{1,0:T(8,128)(2,1)S(1)}, bf16[3,256,2048]{2,1,0:T(8,128)(2...) custom-call(f32[768,128]{1,0:T(8,128)S(1)} %get-tuple-element.72.til, ...), custom_call_target="tpu_custom_call", output_to_operand_aliasing={{10}: (4, {}), {11}: (5, {}), {12}: (6, {}), {13}: (7, {}),... | custom-call | tf_op jit(solution)/shard_map/pallas_call | solution.py:679
  28.5 0.1 collective-permute-start.3
  28.5 1.7 %collective-permute-done.3.got._ = bf16[1440,128]{1,0:T(8,128)(2,1)S(1)} collective-permute-done((bf16[1440,128]{1,0:T(8,128)(2,1)S(1)}, bf16[1440,128]{1,0:T(8,128)(2,1)S(1)}, u32[]{:S(2)}, u32[]{:S(2)}) %collective-permute-start.3) | collective-permute-done | bytes 368672 | tf_op jit(solution)/shard_map/ppermute | solution.py:710
  30.2 0.9 %shard_map.324 = (bf16[1408,128]{1,0:T(8,128)(2,1)}, bf16[32,128]{1,0:T(8,128)(2,1)S(1)}) custom-call(f32[1408,128]{1,0:T(8,128)S(1)} %get-tuple-element.82.keep, bf16[32,128]{1,0:T(8,128)(2,1)S(1)} %get-tuple-element.83.early, bf16[1440,128]{1,0:T(8,128)(2,1)S(1)} %collective-permute-done.3.got._), custom_call_target="tpu_custom_call" | custom-call | tf_op jit(solution)/shard_map/pallas_call | solution.py:711
  31.1 5.9 %all-to-all-start = ((bf16[16,88,128]{2,1,0:T(8,128)(2,1)}), bf16[16,88,128]{2,1,0:T(8,128)(2,1)S(1)}, u32[]{:S(2)}, u32[]{:S(2)}) async-start(bf16[16,88,128]{2,1,0:T(8,128)(2,1)} %bitcast.4), calls=%async_computation | async-start | bytes 720896 | tf_op jit(solution)/shard_map/all_to_all | solution.py:718
  37.0 0.0 copy-done.4
  37.0 9.2 %shard_map.326 = (bf16[96,128]{1,0:T(8,128)(2,1)S(1)}, bf16[96,128]{1,0:T(8,128)(2,1)S(1)}) custom-call(bf16[3,256,2048]{2,1,0:T(8,128)(2,1)} %get-tuple-element.86.h_in, bf16[3,256,2048]{2,1,0:T(8,128)(2,1)} %get-tuple-element.87.slope_in, f32[3,128,2048]{2,1,0:T(8,128)} %get-tuple-element.88.gap_in, bf16[3,256,2304]{2,1,0:T(8,128)(2,1)} %get-tuple-element.89.da_in, ...), custom_call_target="tpu_custom_call" | custom-call | flops 4831838208 | bytes 1048576 | tf_op jit(solution)/shard_map/pallas_call | solution.py:720
  46.3 0.1 collective-permute-start.4
  46.4 1.2 %collective-permute-done.4 = bf16[96,128]{1,0:T(8,128)(2,1)S(1)} collective-permute-done((bf16[96,128]{1,0:T(8,128)(2,1)S(1)}, bf16[96,128]{1,0:T(8,128)(2,1)S(1)}, u32[]{:S(2)}, u32[]{:S(2)}) %collective-permute-start.4) | collective-permute-done | bytes 24608 | tf_op jit(solution)/shard_map/ppermute | solution.py:735
  47.5 0.0 copy-start
  47.5 0.0 copy-start.1
  47.6 0.0 copy-start.2
  47.6 0.0 copy-start.3
  47.6 0.0 copy-start.5
  47.6 0.0 copy-start.6
  47.6 0.0 copy-start.7
  47.6 0.0 copy-start.8
  47.6 0.0 copy-start.9
  47.6 0.0 copy-start.10
  47.7 0.0 copy-start.11
  47.7 0.0 copy-start.12
  47.7 0.0 copy-start.13
  47.7 0.0 copy-start.14
  47.7 1.5 %all-to-all-done.parts = bf16[16,88,128]{2,1,0:T(8,128)(2,1)S(1)} async-done(((bf16[16,88,128]{2,1,0:T(8,128)(2,1)}), bf16[16,88,128]{2,1,0:T(8,128)(2,1)S(1)}, u32[]{:S(2)}, u32[]{:S(2)}) %all-to-all-start) | async-done | bytes 360480 | tf_op jit(solution)/shard_map/all_to_all | solution.py:718
  49.3 0.1 shard_map.325
  49.3 2.2 %collective-permute-start.5 = (bf16[216,128]{1,0:T(8,128)(2,1)S(1)}, bf16[216,128]{1,0:T(8,128)(2,1)S(1)}, u32[]{:S(2)}, u32[]{:S(2)}) collective-permute-start(bf16[216,128]{1,0:T(8,128)(2,1)S(1)} %pad_maximum_fusion), channel_id=1, source_target_pairs={{0,12},{1,13},{2,14},{3,15},{4,8},{5,9},{6,10},{7,11},{8,4},{9,5},... | collective-permute-start | bytes 165896 | tf_op jit(solution)/shard_map/ppermute | solution.py:755
  51.6 0.3 collective-permute-start.6
  51.9 1.9 %collective-permute-start.7 = (bf16[216,128]{1,0:T(8,128)(2,1)S(1)}, bf16[216,128]{1,0:T(8,128)(2,1)S(1)}, u32[]{:S(2)}, u32[]{:S(2)}) collective-permute-start(bf16[216,128]{1,0:T(8,128)(2,1)S(1)} %pad_maximum_fusion), channel_id=1, source_target_pairs={{0,4},{1,5},{2,6},{3,7},{4,0},{5,1},{6,2},{7,3},{8,12},{9,13},{10,... | collective-permute-start | bytes 165896 | tf_op jit(solution)/shard_map/ppermute | solution.py:755
  53.8 1.5 %collective-permute-done.5 = bf16[216,128]{1,0:T(8,128)(2,1)S(1)} collective-permute-done((bf16[216,128]{1,0:T(8,128)(2,1)S(1)}, bf16[216,128]{1,0:T(8,128)(2,1)S(1)}, u32[]{:S(2)}, u32[]{:S(2)}) %collective-permute-start.5) | collective-permute-done | bytes 55328 | tf_op jit(solution)/shard_map/ppermute | solution.py:755
  55.3 1.3 %collective-permute-done.6 = bf16[216,128]{1,0:T(8,128)(2,1)S(1)} collective-permute-done((bf16[216,128]{1,0:T(8,128)(2,1)S(1)}, bf16[216,128]{1,0:T(8,128)(2,1)S(1)}, u32[]{:S(2)}, u32[]{:S(2)}) %collective-permute-start.6) | collective-permute-done | bytes 55328 | tf_op jit(solution)/shard_map/ppermute | solution.py:755
  56.6 0.0 collective-permute-done.7
  56.8 0.2 concatenate.15.refs_0_
  56.9 2.4 %collective-permute-start.10 = (bf16[480,128]{1,0:T(8,128)(2,1)S(1)}, bf16[480,128]{1,0:T(8,128)(2,1)S(1)}, u32[]{:S(2)}, u32[]{:S(2)}) collective-permute-start(bf16[480,128]{1,0:T(8,128)(2,1)S(1)} %concatenate.15.refs_0_), channel_id=1, source_target_pairs={{0,3},{1,2},{2,1},{3,0},{4,7},{5,6},{6,5},{7,4},{8,11},{9,10},{10,... | collective-permute-start | bytes 368648 | tf_op jit(solution)/shard_map/ppermute | solution.py:755
  59.3 0.6 collective-permute-start.8
  59.9 0.6 collective-permute-start.9
  60.5 2.3 %collective-permute-done.10.refs_3_ = bf16[480,128]{1,0:T(8,128)(2,1)S(1)} collective-permute-done((bf16[480,128]{1,0:T(8,128)(2,1)S(1)}, bf16[480,128]{1,0:T(8,128)(2,1)S(1)}, u32[]{:S(2)}, u32[]{:S(2)}) %collective-permute-start.10) | collective-permute-done | bytes 122912 | tf_op jit(solution)/shard_map/ppermute | solution.py:755
  62.8 1.4 %collective-permute-done.8.refs_1_ = bf16[480,128]{1,0:T(8,128)(2,1)S(1)} collective-permute-done((bf16[480,128]{1,0:T(8,128)(2,1)S(1)}, bf16[480,128]{1,0:T(8,128)(2,1)S(1)}, u32[]{:S(2)}, u32[]{:S(2)}) %collective-permute-start.8) | collective-permute-done | bytes 122912 | tf_op jit(solution)/shard_map/ppermute | solution.py:755
  64.2 0.6 collective-permute-done.9.refs_2_
  64.8 0.0 copy-done
  64.9 2.1 %shard_map.327 = (f32[1,1]{1,0:T(1,128)}, f32[1,1]{1,0:T(1,128)}, f32[1,512]{1,0:T(1,128)}, f32[1,64,512]{2,1,0:T(8,128)}, f32[27,1,128]{2,1,0:T(1,128)}, /*inde...) custom-call(bf16[480,128]{1,0:T(8,128)(2,1)S(1)} %concatenate.15.ref, ...), custom_call_target="tpu_custom_call" | custom-call | tf_op jit(solution)/shard_map/pallas_call | solution.py:778
  (27 shorter events, 0.2 us)
Async XLA Ops:
  0.7 1.9 %collective-permute-start = (s32[1,3,32,128]{3,2,1,0:T(8,128)}, s32[1,3,32,128]{3,2,1,0:T(8,128)S(1)}, u32[]{:S(2)}, u32[]{:S(2)}) collective-permute-start(s32[1,3,32,128]{3,2,1,0:T(8,128)} %codes.1), channel_id=1, source_target_pairs={{0,16},{16,0},{1,17},{17,1},{2,18},{18,2},{3,19},{19,3},{4,20},{20... | collective-permute-start | bytes 147464 | tf_op jit(solution)/shard_map/ppermute | solution.py:619
  2.6 5.0 %collective-permute-start.2 = (bf16[1744,128]{1,0:T(8,128)(2,1)S(1)}, bf16[1744,128]{1,0:T(8,128)(2,1)S(1)}, u32[]{:S(2)}, u32[]{:S(2)}) collective-permute-start(bf16[1744,128]{1,0:T(8,128)(2,1)S(1)} %get-tuple-element.74.mine), channel_id=1, source_target_pairs={{0,16},{16,0},{1,17},{17,1},{2,18},{18,2},{3,19},{19,3},{4,20},{20... | collective-permute-start | bytes 1339400 | tf_op jit(solution)/shard_map/ppermute | solution.py:647
  2.7 11.6 %collective-permute-start.1 = (bf16[48,128]{1,0:T(8,128)(2,1)S(1)}, bf16[48,128]{1,0:T(8,128)(2,1)S(1)}, u32[]{:S(2)}, u32[]{:S(2)}) collective-permute-start(bf16[48,128]{1,0:T(8,128)(2,1)S(1)} %get-tuple-element.73), channel_id=1, source_target_pairs={{0,1},{1,2},{3,4},{4,5},{5,6},{7,8},{8,9},{9,10},{11,12},{12,13},{... | collective-permute-start | bytes 36872 | tf_op jit(solution)/shard_map/ppermute | solution.py:646
  28.5 1.8 %collective-permute-start.3 = (bf16[1440,128]{1,0:T(8,128)(2,1)S(1)}, bf16[1440,128]{1,0:T(8,128)(2,1)S(1)}, u32[]{:S(2)}, u32[]{:S(2)}) collective-permute-start(bf16[1440,128]{1,0:T(8,128)(2,1)S(1)} %get-tuple-element.84), channel_id=1, source_target_pairs={{0,16},{16,0},{1,17},{17,1},{2,18},{18,2},{3,19},{19,3},{4,20},{20... | collective-permute-start | bytes 1105928 | tf_op jit(solution)/shard_map/ppermute | solution.py:710
  30.2 6.8 %copy-start.4 = (bf16[1440,128]{1,0:T(8,128)(2,1)}, bf16[1440,128]{1,0:T(8,128)(2,1)S(1)}, u32[]{:S(2)}) copy-start(bf16[1440,128]{1,0:T(8,128)(2,1)S(1)} %collective-permute-done.3.got._) | copy-start | bytes 1105924
  31.1 18.2 %all-to-all-start = ((bf16[16,88,128]{2,1,0:T(8,128)(2,1)}), bf16[16,88,128]{2,1,0:T(8,128)(2,1)S(1)}, u32[]{:S(2)}, u32[]{:S(2)}) async-start(bf16[16,88,128]{2,1,0:T(8,128)(2,1)} %bitcast.4), calls=%async_computation | async-start | bytes 720896 | tf_op jit(solution)/shard_map/all_to_all | solution.py:718
  46.3 1.3 %collective-permute-start.4 = (bf16[96,128]{1,0:T(8,128)(2,1)S(1)}, bf16[96,128]{1,0:T(8,128)(2,1)S(1)}, u32[]{:S(2)}, u32[]{:S(2)}) collective-permute-start(bf16[96,128]{1,0:T(8,128)(2,1)S(1)} %get-tuple-element.94), channel_id=1, source_target_pairs={{0,16},{16,0},{1,17},{17,1},{2,18},{18,2},{3,19},{19,3},{4,20},{20... | collective-permute-start | bytes 73736 | tf_op jit(solution)/shard_map/ppermute | solution.py:735
  47.5 17.2 %copy-start = (f32[1,1152,128]{2,1,0:T(8,128)S(1)}, f32[1,1152,128]{2,1,0:T(8,128)}, u32[]{:S(2)}) copy-start(f32[1,1152,128]{2,1,0:T(8,128)} %refs_12_.1) | copy-start | bytes 1769476
  47.5 17.2 %copy-start.1 = (f32[1,1152,128]{2,1,0:T(8,128)S(1)}, f32[1,1152,128]{2,1,0:T(8,128)}, u32[]{:S(2)}) copy-start(f32[1,1152,128]{2,1,0:T(8,128)} %refs_13_.1) | copy-start | bytes 1769476
  47.6 17.2 %copy-start.2 = (f32[1,1152,128]{2,1,0:T(8,128)S(1)}, f32[1,1152,128]{2,1,0:T(8,128)}, u32[]{:S(2)}) copy-start(f32[1,1152,128]{2,1,0:T(8,128)} %refs_14_.1) | copy-start | bytes 1769476
  47.6 17.2 %copy-start.3 = (f32[1,512,64]{1,2,0:T(8,128)S(1)}, f32[1,512,64]{1,2,0:T(8,128)}, u32[]{:S(2)}) copy-start(f32[1,512,64]{1,2,0:T(8,128)} %param.21) | copy-start | bytes 393220
  47.6 17.2 %copy-start.5 = (f32[1,128,64]{1,2,0:T(8,128)S(1)}, f32[1,128,64]{1,2,0:T(8,128)}, u32[]{:S(2)}) copy-start(f32[1,128,64]{1,2,0:T(8,128)} %param.25) | copy-start | bytes 98308
  47.6 17.2 %copy-start.6 = (f32[1,27,128]{2,0,1:T(1,128)S(1)}, f32[1,27,128]{2,0,1:T(1,128)}, u32[]{:S(2)}) copy-start(f32[1,27,128]{2,0,1:T(1,128)} %param.22) | copy-start | bytes 41476
  47.6 17.2 %copy-start.7 = (f32[1,128,64]{1,2,0:T(8,128)S(1)}, f32[1,128,64]{1,2,0:T(8,128)}, u32[]{:S(2)}) copy-start(f32[1,128,64]{1,2,0:T(8,128)} %param.26) | copy-start | bytes 98308
  47.6 17.2 %copy-start.8 = (f32[1,128,64]{1,2,0:T(8,128)S(1)}, f32[1,128,64]{1,2,0:T(8,128)}, u32[]{:S(2)}) copy-start(f32[1,128,64]{1,2,0:T(8,128)} %param.27) | copy-start | bytes 98308
  47.6 17.2 %copy-start.9 = (f32[1,27,128]{2,0,1:T(1,128)S(1)}, f32[1,27,128]{2,0,1:T(1,128)}, u32[]{:S(2)}) copy-start(f32[1,27,128]{2,0,1:T(1,128)} %param.23) | copy-start | bytes 41476
  47.6 17.2 %copy-start.10 = (f32[1,27,128]{2,0,1:T(1,128)S(1)}, f32[1,27,128]{2,0,1:T(1,128)}, u32[]{:S(2)}) copy-start(f32[1,27,128]{2,0,1:T(1,128)} %param.24) | copy-start | bytes 41476
  47.7 17.2 %copy-start.11 = (f32[1,512]{1,0:T(1,128)S(1)}, f32[1,512]{1,0:T(1,128)}, u32[]{:S(2)}) copy-start(f32[1,512]{1,0:T(1,128)} %refs_4_.1) | copy-start | bytes 6148
  47.7 17.2 %copy-start.12 = (f32[1,128,3]{1,0,2:T(1,128)S(1)}, f32[1,128,3]{1,0,2:T(1,128)}, u32[]{:S(2)}) copy-start(f32[1,128,3]{1,0,2:T(1,128)} %param.31) | copy-start | bytes 4612
  47.7 17.2 %copy-start.13 = (f32[1,128,3]{1,0,2:T(1,128)S(1)}, f32[1,128,3]{1,0,2:T(1,128)}, u32[]{:S(2)}) copy-start(f32[1,128,3]{1,0,2:T(1,128)} %param.32) | copy-start | bytes 4612
  47.7 17.2 %copy-start.14 = (f32[1,128,3]{1,0,2:T(1,128)S(1)}, f32[1,128,3]{1,0,2:T(1,128)}, u32[]{:S(2)}) copy-start(f32[1,128,3]{1,0,2:T(1,128)} %param.33) | copy-start | bytes 4612
  49.3 6.0 %collective-permute-start.5 = (bf16[216,128]{1,0:T(8,128)(2,1)S(1)}, bf16[216,128]{1,0:T(8,128)(2,1)S(1)}, u32[]{:S(2)}, u32[]{:S(2)}) collective-permute-start(bf16[216,128]{1,0:T(8,128)(2,1)S(1)} %pad_maximum_fusion), channel_id=1, source_target_pairs={{0,12},{1,13},{2,14},{3,15},{4,8},{5,9},{6,10},{7,11},{8,4},{9,5},... | collective-permute-start | bytes 165896 | tf_op jit(solution)/shard_map/ppermute | solution.py:755
  51.6 5.1 %collective-permute-start.6 = (bf16[216,128]{1,0:T(8,128)(2,1)S(1)}, bf16[216,128]{1,0:T(8,128)(2,1)S(1)}, u32[]{:S(2)}, u32[]{:S(2)}) collective-permute-start(bf16[216,128]{1,0:T(8,128)(2,1)S(1)} %pad_maximum_fusion), channel_id=1, source_target_pairs={{0,8},{1,9},{2,10},{3,11},{4,12},{5,13},{6,14},{7,15},{8,0},{9,1},... | collective-permute-start | bytes 165896 | tf_op jit(solution)/shard_map/ppermute | solution.py:755
  51.9 4.8 %collective-permute-start.7 = (bf16[216,128]{1,0:T(8,128)(2,1)S(1)}, bf16[216,128]{1,0:T(8,128)(2,1)S(1)}, u32[]{:S(2)}, u32[]{:S(2)}) collective-permute-start(bf16[216,128]{1,0:T(8,128)(2,1)S(1)} %pad_maximum_fusion), channel_id=1, source_target_pairs={{0,4},{1,5},{2,6},{3,7},{4,0},{5,1},{6,2},{7,3},{8,12},{9,13},{10,... | collective-permute-start | bytes 165896 | tf_op jit(solution)/shard_map/ppermute | solution.py:755
  56.9 5.8 %collective-permute-start.10 = (bf16[480,128]{1,0:T(8,128)(2,1)S(1)}, bf16[480,128]{1,0:T(8,128)(2,1)S(1)}, u32[]{:S(2)}, u32[]{:S(2)}) collective-permute-start(bf16[480,128]{1,0:T(8,128)(2,1)S(1)} %concatenate.15.refs_0_), channel_id=1, source_target_pairs={{0,3},{1,2},{2,1},{3,0},{4,7},{5,6},{6,5},{7,4},{8,11},{9,10},{10,... | collective-permute-start | bytes 368648 | tf_op jit(solution)/shard_map/ppermute | solution.py:755
  59.3 4.9 %collective-permute-start.8 = (bf16[480,128]{1,0:T(8,128)(2,1)S(1)}, bf16[480,128]{1,0:T(8,128)(2,1)S(1)}, u32[]{:S(2)}, u32[]{:S(2)}) collective-permute-start(bf16[480,128]{1,0:T(8,128)(2,1)S(1)} %concatenate.15.refs_0_), channel_id=1, source_target_pairs={{0,1},{1,0},{2,3},{3,2},{4,5},{5,4},{6,7},{7,6},{8,9},{9,8},{10,11... | collective-permute-start | bytes 368648 | tf_op jit(solution)/shard_map/ppermute | solution.py:755
  59.9 4.9 %collective-permute-start.9 = (bf16[480,128]{1,0:T(8,128)(2,1)S(1)}, bf16[480,128]{1,0:T(8,128)(2,1)S(1)}, u32[]{:S(2)}, u32[]{:S(2)}) collective-permute-start(bf16[480,128]{1,0:T(8,128)(2,1)S(1)} %concatenate.15.refs_0_), channel_id=1, source_target_pairs={{0,2},{1,3},{2,0},{3,1},{4,6},{5,7},{6,4},{7,5},{8,10},{9,11},{10,... | collective-permute-start | bytes 368648 | tf_op jit(solution)/shard_map/ppermute | solution.py:755

commit v8 on v7

--- a/solution.py
+++ b/solution.py
@@ -390,8 +390,8 @@
         da_s[b] = da
         leave(b, [3])[0].start()
         l_s[128:144] += fold((kept * diff)[:, inner], 256)
+        g_d[...] += dot(u[:, inner], da[:, inner], NT)
         g_o[...] += dot(g[:, inner], dy[:, inner], NT)
-        g_d[...] += dot(u[:, inner], da[:, inner], NT)
         return 0
 
     lax.fori_loop(0, batches, decode, 0)

time: 67.4 us -> 67.2 us (level)
  no operation moved by 1% of the time
where the time goes in v8:
time: 67.2 us; the launch traced here: 66.9 us
  Pallas kernels  34.2 us (51%)
  starting transfers between devices  19.5 us (29%)
  waiting for transfers between devices  11.5 us (17%)
  between operations  1.21 us (2%)
    pallas_call x1, Pallas kernels, local(): pl.pallas_call(functools.partial(step_kernel, batches=batches, rows=rows)...  13.8 us
    pallas_call x1, Pallas kernels, local(): pl.pallas_call(functools.partial(back_kernel, batches=batches, rows=rows)...  9.23 us
    ppermute x6, starting transfers between devices, local(): lax.ppermute(payload, both, xor_pairs(devices, k << start, k << other))  7.99 us
    ppermute x6, waiting for transfers between devices, local(): lax.ppermute(payload, both, xor_pairs(devices, k << start, k << other))  7.13 us
    pallas_call x1, Pallas kernels, local(): pl.pallas_call(functools.partial(early_kernel, batches=batches, rows=rows...  6.71 us
    all_to_all x1, starting transfers between devices, local(): big = lax.all_to_all(big.reshape(devices, size, W), 'dp', 0, 0)  5.93 us
    ppermute x1, starting transfers between devices, local(): near = lax.ppermute(near, both, pairs)  4.84 us
    ppermute x2, waiting for transfers between devices, local(): got = lax.ppermute(send, 'level', swap)  2.83 us
  transfers between devices with their start and end apart: 12, of which 8 were waited for; matrix products, arithmetic and copies ran while one was open for 0% of the time, Pallas kernels for 26%

profile of v8, /device:TPU:0, one launch (start us, length us, event | category | flops | bytes accessed | tf_op | source)
XLA Modules:
  0.0 66.9 jit_solution(18007762648029878902)
XLA Ops:
  0.7 0.5 collective-permute-start
  1.2 1.4 %shard_map.320 = (bf16[1744,128]{1,0:T(8,128)(2,1)S(1)}, f32[768,128]{1,0:T(8,128)S(1)}) custom-call(bf16[3,3,32,128]{3,2,1,0:T(8,128)(2,1)} %image.1, s32[3,32,128]{2,1,0:T(8,128)} %mask.1, s32[1,3,32,128]{3,2,1,0:T(8,128)} %codes.1, f32[1,512]{1,0:T(1,128)} %refs_4_.1, f32[1,64,512]{2,1,0:T(8,128)} %bitcast.40, f32[27,1,128]{2,1,0:T(1,128)} %bitcast.44, ...), custom_call_target="tpu_custom_call" | custom-call | tf_op jit(solution)/shard_map/pallas_call | solution.py:621
  2.6 0.0 collective-permute-done.others
  2.6 0.1 collective-permute-start.2
  2.7 4.8 %collective-permute-start.1 = (bf16[48,128]{1,0:T(8,128)(2,1)S(1)}, bf16[48,128]{1,0:T(8,128)(2,1)S(1)}, u32[]{:S(2)}, u32[]{:S(2)}) collective-permute-start(bf16[48,128]{1,0:T(8,128)(2,1)S(1)} %get-tuple-element.73), channel_id=1, source_target_pairs={{0,1},{1,2},{3,4},{4,5},{5,6},{7,8},{8,9},{9,10},{11,12},{12,13},{... | collective-permute-start | bytes 36872 | tf_op jit(solution)/shard_map/ppermute | solution.py:646
  7.6 0.0 collective-permute-done.2.theirs
  7.6 6.7 %shard_map.322 = (bf16[3,128,7680]{2,1,0:T(8,128)(2,1)S(1)}, bf16[3,256,2048]{2,1,0:T(8,128)(2,1)S(1)}, bf16[3,256,2048]{2,1,0:T(8,128)(2,1)S(1)}, f32[3,128,204...) custom-call(f32[768,128]{1,0:T(8,128)S(1)} %get-tuple-element.72.tile, ...), custom_call_target="tpu_custom_call" | custom-call | flops 3221225472 | bytes 1048576 | tf_op jit(solution)/shard_map/pallas_call | solution.py:670
  14.3 0.0 collective-permute-done.1.near
  14.3 13.8 %shard_map.323 = (f32[1408,128]{1,0:T(8,128)S(1)}, bf16[32,128]{1,0:T(8,128)(2,1)S(1)}, bf16[1440,128]{1,0:T(8,128)(2,1)S(1)}, bf16[3,256,2048]{2,1,0:T(8,128)(2...) custom-call(f32[768,128]{1,0:T(8,128)S(1)} %get-tuple-element.72.til, ...), custom_call_target="tpu_custom_call", output_to_operand_aliasing={{10}: (4, {}), {11}: (5, {}), {12}: (6, {}), {13}: (7, {}),... | custom-call | tf_op jit(solution)/shard_map/pallas_call | solution.py:679
  28.2 0.1 collective-permute-start.3
  28.3 1.7 %collective-permute-done.3.got._ = bf16[1440,128]{1,0:T(8,128)(2,1)S(1)} collective-permute-done((bf16[1440,128]{1,0:T(8,128)(2,1)S(1)}, bf16[1440,128]{1,0:T(8,128)(2,1)S(1)}, u32[]{:S(2)}, u32[]{:S(2)}) %collective-permute-start.3) | collective-permute-done | bytes 368672 | tf_op jit(solution)/shard_map/ppermute | solution.py:710
  29.9 0.9 %shard_map.324 = (bf16[1408,128]{1,0:T(8,128)(2,1)}, bf16[32,128]{1,0:T(8,128)(2,1)S(1)}) custom-call(f32[1408,128]{1,0:T(8,128)S(1)} %get-tuple-element.82.keep, bf16[32,128]{1,0:T(8,128)(2,1)S(1)} %get-tuple-element.83.early, bf16[1440,128]{1,0:T(8,128)(2,1)S(1)} %collective-permute-done.3.got._), custom_call_target="tpu_custom_call" | custom-call | tf_op jit(solution)/shard_map/pallas_call | solution.py:711
  30.8 5.9 %all-to-all-start = ((bf16[16,88,128]{2,1,0:T(8,128)(2,1)}), bf16[16,88,128]{2,1,0:T(8,128)(2,1)S(1)}, u32[]{:S(2)}, u32[]{:S(2)}) async-start(bf16[16,88,128]{2,1,0:T(8,128)(2,1)} %bitcast.4), calls=%async_computation | async-start | bytes 720896 | tf_op jit(solution)/shard_map/all_to_all | solution.py:718
  36.7 0.0 copy-done.4
  36.7 9.2 %shard_map.326 = (bf16[96,128]{1,0:T(8,128)(2,1)S(1)}, bf16[96,128]{1,0:T(8,128)(2,1)S(1)}) custom-call(bf16[3,256,2048]{2,1,0:T(8,128)(2,1)} %get-tuple-element.86.h_in, bf16[3,256,2048]{2,1,0:T(8,128)(2,1)} %get-tuple-element.87.slope_in, f32[3,128,2048]{2,1,0:T(8,128)} %get-tuple-element.88.gap_in, bf16[3,256,2304]{2,1,0:T(8,128)(2,1)} %get-tuple-element.89.da_in, ...), custom_call_target="tpu_custom_call" | custom-call | flops 4831838208 | bytes 1048576 | tf_op jit(solution)/shard_map/pallas_call | solution.py:720
  46.0 0.1 collective-permute-start.4
  46.1 1.2 %collective-permute-done.4 = bf16[96,128]{1,0:T(8,128)(2,1)S(1)} collective-permute-done((bf16[96,128]{1,0:T(8,128)(2,1)S(1)}, bf16[96,128]{1,0:T(8,128)(2,1)S(1)}, u32[]{:S(2)}, u32[]{:S(2)}) %collective-permute-start.4) | collective-permute-done | bytes 24608 | tf_op jit(solution)/shard_map/ppermute | solution.py:735
  47.3 0.0 copy-start
  47.3 0.0 copy-start.1
  47.3 0.0 copy-start.2
  47.3 0.0 copy-start.3
  47.3 0.0 copy-start.5
  47.3 0.0 copy-start.6
  47.3 0.0 copy-start.7
  47.3 0.0 copy-start.8
  47.4 0.0 copy-start.9
  47.4 0.0 copy-start.10
  47.4 0.0 copy-start.11
  47.4 0.0 copy-start.12
  47.4 0.0 copy-start.13
  47.4 0.0 copy-start.14
  47.4 1.6 %all-to-all-done.parts = bf16[16,88,128]{2,1,0:T(8,128)(2,1)S(1)} async-done(((bf16[16,88,128]{2,1,0:T(8,128)(2,1)}), bf16[16,88,128]{2,1,0:T(8,128)(2,1)S(1)}, u32[]{:S(2)}, u32[]{:S(2)}) %all-to-all-start) | async-done | bytes 360480 | tf_op jit(solution)/shard_map/all_to_all | solution.py:718
  49.0 0.1 shard_map.325
  49.1 2.2 %collective-permute-start.5 = (bf16[216,128]{1,0:T(8,128)(2,1)S(1)}, bf16[216,128]{1,0:T(8,128)(2,1)S(1)}, u32[]{:S(2)}, u32[]{:S(2)}) collective-permute-start(bf16[216,128]{1,0:T(8,128)(2,1)S(1)} %pad_maximum_fusion), channel_id=1, source_target_pairs={{0,12},{1,13},{2,14},{3,15},{4,8},{5,9},{6,10},{7,11},{8,4},{9,5},... | collective-permute-start | bytes 165896 | tf_op jit(solution)/shard_map/ppermute | solution.py:755
  51.3 0.3 collective-permute-start.6
  51.6 1.9 %collective-permute-start.7 = (bf16[216,128]{1,0:T(8,128)(2,1)S(1)}, bf16[216,128]{1,0:T(8,128)(2,1)S(1)}, u32[]{:S(2)}, u32[]{:S(2)}) collective-permute-start(bf16[216,128]{1,0:T(8,128)(2,1)S(1)} %pad_maximum_fusion), channel_id=1, source_target_pairs={{0,4},{1,5},{2,6},{3,7},{4,0},{5,1},{6,2},{7,3},{8,12},{9,13},{10,... | collective-permute-start | bytes 165896 | tf_op jit(solution)/shard_map/ppermute | solution.py:755
  53.5 1.5 %collective-permute-done.5 = bf16[216,128]{1,0:T(8,128)(2,1)S(1)} collective-permute-done((bf16[216,128]{1,0:T(8,128)(2,1)S(1)}, bf16[216,128]{1,0:T(8,128)(2,1)S(1)}, u32[]{:S(2)}, u32[]{:S(2)}) %collective-permute-start.5) | collective-permute-done | bytes 55328 | tf_op jit(solution)/shard_map/ppermute | solution.py:755
  55.1 1.3 %collective-permute-done.6 = bf16[216,128]{1,0:T(8,128)(2,1)S(1)} collective-permute-done((bf16[216,128]{1,0:T(8,128)(2,1)S(1)}, bf16[216,128]{1,0:T(8,128)(2,1)S(1)}, u32[]{:S(2)}, u32[]{:S(2)}) %collective-permute-start.6) | collective-permute-done | bytes 55328 | tf_op jit(solution)/shard_map/ppermute | solution.py:755
  56.4 0.0 collective-permute-done.7
  56.5 0.2 concatenate.15.refs_0_
  56.7 2.4 %collective-permute-start.10 = (bf16[480,128]{1,0:T(8,128)(2,1)S(1)}, bf16[480,128]{1,0:T(8,128)(2,1)S(1)}, u32[]{:S(2)}, u32[]{:S(2)}) collective-permute-start(bf16[480,128]{1,0:T(8,128)(2,1)S(1)} %concatenate.15.refs_0_), channel_id=1, source_target_pairs={{0,3},{1,2},{2,1},{3,0},{4,7},{5,6},{6,5},{7,4},{8,11},{9,10},{10,... | collective-permute-start | bytes 368648 | tf_op jit(solution)/shard_map/ppermute | solution.py:755
  59.1 0.6 collective-permute-start.8
  59.6 0.6 collective-permute-start.9
  60.2 2.3 %collective-permute-done.10.refs_3_ = bf16[480,128]{1,0:T(8,128)(2,1)S(1)} collective-permute-done((bf16[480,128]{1,0:T(8,128)(2,1)S(1)}, bf16[480,128]{1,0:T(8,128)(2,1)S(1)}, u32[]{:S(2)}, u32[]{:S(2)}) %collective-permute-start.10) | collective-permute-done | bytes 122912 | tf_op jit(solution)/shard_map/ppermute | solution.py:755
  62.5 1.4 %collective-permute-done.8.refs_1_ = bf16[480,128]{1,0:T(8,128)(2,1)S(1)} collective-permute-done((bf16[480,128]{1,0:T(8,128)(2,1)S(1)}, bf16[480,128]{1,0:T(8,128)(2,1)S(1)}, u32[]{:S(2)}, u32[]{:S(2)}) %collective-permute-start.8) | collective-permute-done | bytes 122912 | tf_op jit(solution)/shard_map/ppermute | solution.py:755
  64.0 0.6 collective-permute-done.9.refs_2_
  64.5 0.0 copy-done
  64.6 2.1 %shard_map.327 = (f32[1,1]{1,0:T(1,128)}, f32[1,1]{1,0:T(1,128)}, f32[1,512]{1,0:T(1,128)}, f32[1,64,512]{2,1,0:T(8,128)}, f32[27,1,128]{2,1,0:T(1,128)}, /*inde...) custom-call(bf16[480,128]{1,0:T(8,128)(2,1)S(1)} %concatenate.15.ref, ...), custom_call_target="tpu_custom_call" | custom-call | tf_op jit(solution)/shard_map/pallas_call | solution.py:778
  (27 shorter events, 0.2 us)
Async XLA Ops:
  0.7 1.9 %collective-permute-start = (s32[1,3,32,128]{3,2,1,0:T(8,128)}, s32[1,3,32,128]{3,2,1,0:T(8,128)S(1)}, u32[]{:S(2)}, u32[]{:S(2)}) collective-permute-start(s32[1,3,32,128]{3,2,1,0:T(8,128)} %codes.1), channel_id=1, source_target_pairs={{0,16},{16,0},{1,17},{17,1},{2,18},{18,2},{3,19},{19,3},{4,20},{20... | collective-permute-start | bytes 147464 | tf_op jit(solution)/shard_map/ppermute | solution.py:619
  2.6 5.0 %collective-permute-start.2 = (bf16[1744,128]{1,0:T(8,128)(2,1)S(1)}, bf16[1744,128]{1,0:T(8,128)(2,1)S(1)}, u32[]{:S(2)}, u32[]{:S(2)}) collective-permute-start(bf16[1744,128]{1,0:T(8,128)(2,1)S(1)} %get-tuple-element.74.mine), channel_id=1, source_target_pairs={{0,16},{16,0},{1,17},{17,1},{2,18},{18,2},{3,19},{19,3},{4,20},{20... | collective-permute-start | bytes 1339400 | tf_op jit(solution)/shard_map/ppermute | solution.py:647
  2.7 11.6 %collective-permute-start.1 = (bf16[48,128]{1,0:T(8,128)(2,1)S(1)}, bf16[48,128]{1,0:T(8,128)(2,1)S(1)}, u32[]{:S(2)}, u32[]{:S(2)}) collective-permute-start(bf16[48,128]{1,0:T(8,128)(2,1)S(1)} %get-tuple-element.73), channel_id=1, source_target_pairs={{0,1},{1,2},{3,4},{4,5},{5,6},{7,8},{8,9},{9,10},{11,12},{12,13},{... | collective-permute-start | bytes 36872 | tf_op jit(solution)/shard_map/ppermute | solution.py:646
  28.2 1.8 %collective-permute-start.3 = (bf16[1440,128]{1,0:T(8,128)(2,1)S(1)}, bf16[1440,128]{1,0:T(8,128)(2,1)S(1)}, u32[]{:S(2)}, u32[]{:S(2)}) collective-permute-start(bf16[1440,128]{1,0:T(8,128)(2,1)S(1)} %get-tuple-element.84), channel_id=1, source_target_pairs={{0,16},{16,0},{1,17},{17,1},{2,18},{18,2},{3,19},{19,3},{4,20},{20... | collective-permute-start | bytes 1105928 | tf_op jit(solution)/shard_map/ppermute | solution.py:710
  29.9 6.8 %copy-start.4 = (bf16[1440,128]{1,0:T(8,128)(2,1)}, bf16[1440,128]{1,0:T(8,128)(2,1)S(1)}, u32[]{:S(2)}) copy-start(bf16[1440,128]{1,0:T(8,128)(2,1)S(1)} %collective-permute-done.3.got._) | copy-start | bytes 1105924
  30.8 18.2 %all-to-all-start = ((bf16[16,88,128]{2,1,0:T(8,128)(2,1)}), bf16[16,88,128]{2,1,0:T(8,128)(2,1)S(1)}, u32[]{:S(2)}, u32[]{:S(2)}) async-start(bf16[16,88,128]{2,1,0:T(8,128)(2,1)} %bitcast.4), calls=%async_computation | async-start | bytes 720896 | tf_op jit(solution)/shard_map/all_to_all | solution.py:718
  46.0 1.3 %collective-permute-start.4 = (bf16[96,128]{1,0:T(8,128)(2,1)S(1)}, bf16[96,128]{1,0:T(8,128)(2,1)S(1)}, u32[]{:S(2)}, u32[]{:S(2)}) collective-permute-start(bf16[96,128]{1,0:T(8,128)(2,1)S(1)} %get-tuple-element.94), channel_id=1, source_target_pairs={{0,16},{16,0},{1,17},{17,1},{2,18},{18,2},{3,19},{19,3},{4,20},{20... | collective-permute-start | bytes 73736 | tf_op jit(solution)/shard_map/ppermute | solution.py:735
  47.3 17.3 %copy-start = (f32[1,1152,128]{2,1,0:T(8,128)S(1)}, f32[1,1152,128]{2,1,0:T(8,128)}, u32[]{:S(2)}) copy-start(f32[1,1152,128]{2,1,0:T(8,128)} %refs_12_.1) | copy-start | bytes 1769476
  47.3 17.2 %copy-start.1 = (f32[1,1152,128]{2,1,0:T(8,128)S(1)}, f32[1,1152,128]{2,1,0:T(8,128)}, u32[]{:S(2)}) copy-start(f32[1,1152,128]{2,1,0:T(8,128)} %refs_13_.1) | copy-start | bytes 1769476
  47.3 17.2 %copy-start.2 = (f32[1,1152,128]{2,1,0:T(8,128)S(1)}, f32[1,1152,128]{2,1,0:T(8,128)}, u32[]{:S(2)}) copy-start(f32[1,1152,128]{2,1,0:T(8,128)} %refs_14_.1) | copy-start | bytes 1769476
  47.3 17.2 %copy-start.3 = (f32[1,512,64]{1,2,0:T(8,128)S(1)}, f32[1,512,64]{1,2,0:T(8,128)}, u32[]{:S(2)}) copy-start(f32[1,512,64]{1,2,0:T(8,128)} %param.21) | copy-start | bytes 393220
  47.3 17.2 %copy-start.5 = (f32[1,128,64]{1,2,0:T(8,128)S(1)}, f32[1,128,64]{1,2,0:T(8,128)}, u32[]{:S(2)}) copy-start(f32[1,128,64]{1,2,0:T(8,128)} %param.25) | copy-start | bytes 98308
  47.3 17.2 %copy-start.6 = (f32[1,27,128]{2,0,1:T(1,128)S(1)}, f32[1,27,128]{2,0,1:T(1,128)}, u32[]{:S(2)}) copy-start(f32[1,27,128]{2,0,1:T(1,128)} %param.22) | copy-start | bytes 41476
  47.3 17.2 %copy-start.7 = (f32[1,128,64]{1,2,0:T(8,128)S(1)}, f32[1,128,64]{1,2,0:T(8,128)}, u32[]{:S(2)}) copy-start(f32[1,128,64]{1,2,0:T(8,128)} %param.26) | copy-start | bytes 98308
  47.3 17.2 %copy-start.8 = (f32[1,128,64]{1,2,0:T(8,128)S(1)}, f32[1,128,64]{1,2,0:T(8,128)}, u32[]{:S(2)}) copy-start(f32[1,128,64]{1,2,0:T(8,128)} %param.27) | copy-start | bytes 98308
  47.4 17.2 %copy-start.9 = (f32[1,27,128]{2,0,1:T(1,128)S(1)}, f32[1,27,128]{2,0,1:T(1,128)}, u32[]{:S(2)}) copy-start(f32[1,27,128]{2,0,1:T(1,128)} %param.23) | copy-start | bytes 41476
  47.4 17.2 %copy-start.10 = (f32[1,27,128]{2,0,1:T(1,128)S(1)}, f32[1,27,128]{2,0,1:T(1,128)}, u32[]{:S(2)}) copy-start(f32[1,27,128]{2,0,1:T(1,128)} %param.24) | copy-start | bytes 41476
  47.4 17.2 %copy-start.11 = (f32[1,512]{1,0:T(1,128)S(1)}, f32[1,512]{1,0:T(1,128)}, u32[]{:S(2)}) copy-start(f32[1,512]{1,0:T(1,128)} %refs_4_.1) | copy-start | bytes 6148
  47.4 17.2 %copy-start.12 = (f32[1,128,3]{1,0,2:T(1,128)S(1)}, f32[1,128,3]{1,0,2:T(1,128)}, u32[]{:S(2)}) copy-start(f32[1,128,3]{1,0,2:T(1,128)} %param.31) | copy-start | bytes 4612
  47.4 17.2 %copy-start.13 = (f32[1,128,3]{1,0,2:T(1,128)S(1)}, f32[1,128,3]{1,0,2:T(1,128)}, u32[]{:S(2)}) copy-start(f32[1,128,3]{1,0,2:T(1,128)} %param.32) | copy-start | bytes 4612
  47.4 17.2 %copy-start.14 = (f32[1,128,3]{1,0,2:T(1,128)S(1)}, f32[1,128,3]{1,0,2:T(1,128)}, u32[]{:S(2)}) copy-start(f32[1,128,3]{1,0,2:T(1,128)} %param.33) | copy-start | bytes 4612
  49.1 6.0 %collective-permute-start.5 = (bf16[216,128]{1,0:T(8,128)(2,1)S(1)}, bf16[216,128]{1,0:T(8,128)(2,1)S(1)}, u32[]{:S(2)}, u32[]{:S(2)}) collective-permute-start(bf16[216,128]{1,0:T(8,128)(2,1)S(1)} %pad_maximum_fusion), channel_id=1, source_target_pairs={{0,12},{1,13},{2,14},{3,15},{4,8},{5,9},{6,10},{7,11},{8,4},{9,5},... | collective-permute-start | bytes 165896 | tf_op jit(solution)/shard_map/ppermute | solution.py:755
  51.3 5.1 %collective-permute-start.6 = (bf16[216,128]{1,0:T(8,128)(2,1)S(1)}, bf16[216,128]{1,0:T(8,128)(2,1)S(1)}, u32[]{:S(2)}, u32[]{:S(2)}) collective-permute-start(bf16[216,128]{1,0:T(8,128)(2,1)S(1)} %pad_maximum_fusion), channel_id=1, source_target_pairs={{0,8},{1,9},{2,10},{3,11},{4,12},{5,13},{6,14},{7,15},{8,0},{9,1},... | collective-permute-start | bytes 165896 | tf_op jit(solution)/shard_map/ppermute | solution.py:755
  51.6 4.8 %collective-permute-start.7 = (bf16[216,128]{1,0:T(8,128)(2,1)S(1)}, bf16[216,128]{1,0:T(8,128)(2,1)S(1)}, u32[]{:S(2)}, u32[]{:S(2)}) collective-permute-start(bf16[216,128]{1,0:T(8,128)(2,1)S(1)} %pad_maximum_fusion), channel_id=1, source_target_pairs={{0,4},{1,5},{2,6},{3,7},{4,0},{5,1},{6,2},{7,3},{8,12},{9,13},{10,... | collective-permute-start | bytes 165896 | tf_op jit(solution)/shard_map/ppermute | solution.py:755
  56.7 5.8 %collective-permute-start.10 = (bf16[480,128]{1,0:T(8,128)(2,1)S(1)}, bf16[480,128]{1,0:T(8,128)(2,1)S(1)}, u32[]{:S(2)}, u32[]{:S(2)}) collective-permute-start(bf16[480,128]{1,0:T(8,128)(2,1)S(1)} %concatenate.15.refs_0_), channel_id=1, source_target_pairs={{0,3},{1,2},{2,1},{3,0},{4,7},{5,6},{6,5},{7,4},{8,11},{9,10},{10,... | collective-permute-start | bytes 368648 | tf_op jit(solution)/shard_map/ppermute | solution.py:755
  59.1 4.9 %collective-permute-start.8 = (bf16[480,128]{1,0:T(8,128)(2,1)S(1)}, bf16[480,128]{1,0:T(8,128)(2,1)S(1)}, u32[]{:S(2)}, u32[]{:S(2)}) collective-permute-start(bf16[480,128]{1,0:T(8,128)(2,1)S(1)} %concatenate.15.refs_0_), channel_id=1, source_target_pairs={{0,1},{1,0},{2,3},{3,2},{4,5},{5,4},{6,7},{7,6},{8,9},{9,8},{10,11... | collective-permute-start | bytes 368648 | tf_op jit(solution)/shard_map/ppermute | solution.py:755
  59.6 4.9 %collective-permute-start.9 = (bf16[480,128]{1,0:T(8,128)(2,1)S(1)}, bf16[480,128]{1,0:T(8,128)(2,1)S(1)}, u32[]{:S(2)}, u32[]{:S(2)}) collective-permute-start(bf16[480,128]{1,0:T(8,128)(2,1)S(1)} %concatenate.15.refs_0_), channel_id=1, source_target_pairs={{0,2},{1,3},{2,0},{3,1},{4,6},{5,7},{6,4},{7,5},{8,10},{9,11},{10,... | collective-permute-start | bytes 368648 | tf_op jit(solution)/shard_map/ppermute | solution.py:755

commit v9 on v8

--- a/solution.py
+++ b/solution.py
@@ -259,9 +259,9 @@
 
 def encoder_back(du, gap, h, slope, x, zn, g_z, g_e):
     dz = (du + gap).astype(BF)
-    g_z[...] += dot(dz, h, NT)
     dpre = (dot(zn[...], dz) * slope).astype(BF)
     g_e[...] += dot(x, dpre, NT)
+    g_z[...] += dot(dz, h, NT)
 
 
 def step_kernel(

time: 67.2 us -> 67.1 us (level)
  no operation moved by 1% of the time
where the time goes in v9:
time: 67.1 us; the launch traced here: 66.8 us
  Pallas kernels  34.1 us (51%)
  starting transfers between devices  19.5 us (29%)
  waiting for transfers between devices  11.5 us (17%)
  between operations  1.21 us (2%)
    pallas_call x1, Pallas kernels, local(): pl.pallas_call(functools.partial(step_kernel, batches=batches, rows=rows)...  13.8 us
    pallas_call x1, Pallas kernels, local(): pl.pallas_call(functools.partial(back_kernel, batches=batches, rows=rows)...  9.11 us
    ppermute x6, starting transfers between devices, local(): lax.ppermute(payload, both, xor_pairs(devices, k << start, k << other))  7.99 us
    ppermute x6, waiting for transfers between devices, local(): lax.ppermute(payload, both, xor_pairs(devices, k << start, k << other))  7.01 us
    pallas_call x1, Pallas kernels, local(): pl.pallas_call(functools.partial(early_kernel, batches=batches, rows=rows...  6.71 us
    all_to_all x1, starting transfers between devices, local(): big = lax.all_to_all(big.reshape(devices, size, W), 'dp', 0, 0)  5.93 us
    ppermute x1, starting transfers between devices, local(): near = lax.ppermute(near, both, pairs)  4.84 us
    ppermute x2, waiting for transfers between devices, local(): got = lax.ppermute(send, 'level', swap)  2.83 us
  transfers between devices with their start and end apart: 12, of which 8 were waited for; matrix products, arithmetic and copies ran while one was open for 0% of the time, Pallas kernels for 26%

profile of v9, /device:TPU:0, one launch (start us, length us, event | category | flops | bytes accessed | tf_op | source)
XLA Modules:
  0.0 66.8 jit_solution(10640725706180741156)
XLA Ops:
  0.7 0.5 collective-permute-start
  1.2 1.4 %shard_map.320 = (bf16[1744,128]{1,0:T(8,128)(2,1)S(1)}, f32[768,128]{1,0:T(8,128)S(1)}) custom-call(bf16[3,3,32,128]{3,2,1,0:T(8,128)(2,1)} %image.1, s32[3,32,128]{2,1,0:T(8,128)} %mask.1, s32[1,3,32,128]{3,2,1,0:T(8,128)} %codes.1, f32[1,512]{1,0:T(1,128)} %refs_4_.1, f32[1,64,512]{2,1,0:T(8,128)} %bitcast.40, f32[27,1,128]{2,1,0:T(1,128)} %bitcast.44, ...), custom_call_target="tpu_custom_call" | custom-call | tf_op jit(solution)/shard_map/pallas_call | solution.py:621
  2.6 0.0 collective-permute-done.others
  2.6 0.1 collective-permute-start.2
  2.7 4.8 %collective-permute-start.1 = (bf16[48,128]{1,0:T(8,128)(2,1)S(1)}, bf16[48,128]{1,0:T(8,128)(2,1)S(1)}, u32[]{:S(2)}, u32[]{:S(2)}) collective-permute-start(bf16[48,128]{1,0:T(8,128)(2,1)S(1)} %get-tuple-element.73), channel_id=1, source_target_pairs={{0,1},{1,2},{3,4},{4,5},{5,6},{7,8},{8,9},{9,10},{11,12},{12,13},{... | collective-permute-start | bytes 36872 | tf_op jit(solution)/shard_map/ppermute | solution.py:646
  7.6 0.0 collective-permute-done.2.theirs
  7.6 6.7 %shard_map.322 = (bf16[3,128,7680]{2,1,0:T(8,128)(2,1)S(1)}, bf16[3,256,2048]{2,1,0:T(8,128)(2,1)S(1)}, bf16[3,256,2048]{2,1,0:T(8,128)(2,1)S(1)}, f32[3,128,204...) custom-call(f32[768,128]{1,0:T(8,128)S(1)} %get-tuple-element.72.tile, ...), custom_call_target="tpu_custom_call" | custom-call | flops 3221225472 | bytes 1048576 | tf_op jit(solution)/shard_map/pallas_call | solution.py:670
  14.3 0.0 collective-permute-done.1.near
  14.3 13.8 %shard_map.323 = (f32[1408,128]{1,0:T(8,128)S(1)}, bf16[32,128]{1,0:T(8,128)(2,1)S(1)}, bf16[1440,128]{1,0:T(8,128)(2,1)S(1)}, bf16[3,256,2048]{2,1,0:T(8,128)(2...) custom-call(f32[768,128]{1,0:T(8,128)S(1)} %get-tuple-element.72.til, ...), custom_call_target="tpu_custom_call", output_to_operand_aliasing={{10}: (4, {}), {11}: (5, {}), {12}: (6, {}), {13}: (7, {}),... | custom-call | tf_op jit(solution)/shard_map/pallas_call | solution.py:679
  28.2 0.1 collective-permute-start.3
  28.3 1.7 %collective-permute-done.3.got._ = bf16[1440,128]{1,0:T(8,128)(2,1)S(1)} collective-permute-done((bf16[1440,128]{1,0:T(8,128)(2,1)S(1)}, bf16[1440,128]{1,0:T(8,128)(2,1)S(1)}, u32[]{:S(2)}, u32[]{:S(2)}) %collective-permute-start.3) | collective-permute-done | bytes 368672 | tf_op jit(solution)/shard_map/ppermute | solution.py:710
  29.9 0.9 %shard_map.324 = (bf16[1408,128]{1,0:T(8,128)(2,1)}, bf16[32,128]{1,0:T(8,128)(2,1)S(1)}) custom-call(f32[1408,128]{1,0:T(8,128)S(1)} %get-tuple-element.82.keep, bf16[32,128]{1,0:T(8,128)(2,1)S(1)} %get-tuple-element.83.early, bf16[1440,128]{1,0:T(8,128)(2,1)S(1)} %collective-permute-done.3.got._), custom_call_target="tpu_custom_call" | custom-call | tf_op jit(solution)/shard_map/pallas_call | solution.py:711
  30.8 5.9 %all-to-all-start = ((bf16[16,88,128]{2,1,0:T(8,128)(2,1)}), bf16[16,88,128]{2,1,0:T(8,128)(2,1)S(1)}, u32[]{:S(2)}, u32[]{:S(2)}) async-start(bf16[16,88,128]{2,1,0:T(8,128)(2,1)} %bitcast.4), calls=%async_computation | async-start | bytes 720896 | tf_op jit(solution)/shard_map/all_to_all | solution.py:718
  36.7 9.1 %shard_map.326 = (bf16[96,128]{1,0:T(8,128)(2,1)S(1)}, bf16[96,128]{1,0:T(8,128)(2,1)S(1)}) custom-call(bf16[3,256,2048]{2,1,0:T(8,128)(2,1)} %get-tuple-element.86.h_in, bf16[3,256,2048]{2,1,0:T(8,128)(2,1)} %get-tuple-element.87.slope_in, f32[3,128,2048]{2,1,0:T(8,128)} %get-tuple-element.88.gap_in, bf16[3,256,2304]{2,1,0:T(8,128)(2,1)} %get-tuple-element.89.da_in, ...), custom_call_target="tpu_custom_call" | custom-call | flops 4831838208 | bytes 1048576 | tf_op jit(solution)/shard_map/pallas_call | solution.py:720
  45.9 0.1 collective-permute-start.4
  46.0 1.2 %collective-permute-done.4 = bf16[96,128]{1,0:T(8,128)(2,1)S(1)} collective-permute-done((bf16[96,128]{1,0:T(8,128)(2,1)S(1)}, bf16[96,128]{1,0:T(8,128)(2,1)S(1)}, u32[]{:S(2)}, u32[]{:S(2)}) %collective-permute-start.4) | collective-permute-done | bytes 24608 | tf_op jit(solution)/shard_map/ppermute | solution.py:735
  47.1 0.0 copy-start
  47.1 0.0 copy-start.1
  47.2 0.0 copy-start.2
  47.2 0.0 copy-start.3
  47.2 0.0 copy-start.5
  47.2 0.0 copy-start.6
  47.2 0.0 copy-start.7
  47.2 0.0 copy-start.8
  47.2 0.0 copy-start.9
  47.2 0.0 copy-start.10
  47.3 0.0 copy-start.11
  47.3 0.0 copy-start.12
  47.3 0.0 copy-start.13
  47.3 0.0 copy-start.14
  47.3 1.7 %all-to-all-done.parts = bf16[16,88,128]{2,1,0:T(8,128)(2,1)S(1)} async-done(((bf16[16,88,128]{2,1,0:T(8,128)(2,1)}), bf16[16,88,128]{2,1,0:T(8,128)(2,1)S(1)}, u32[]{:S(2)}, u32[]{:S(2)}) %all-to-all-start) | async-done | bytes 360480 | tf_op jit(solution)/shard_map/all_to_all | solution.py:718
  49.0 0.1 shard_map.325
  49.1 2.1 %collective-permute-start.5 = (bf16[216,128]{1,0:T(8,128)(2,1)S(1)}, bf16[216,128]{1,0:T(8,128)(2,1)S(1)}, u32[]{:S(2)}, u32[]{:S(2)}) collective-permute-start(bf16[216,128]{1,0:T(8,128)(2,1)S(1)} %pad_maximum_fusion), channel_id=1, source_target_pairs={{0,12},{1,13},{2,14},{3,15},{4,8},{5,9},{6,10},{7,11},{8,4},{9,5},... | collective-permute-start | bytes 165896 | tf_op jit(solution)/shard_map/ppermute | solution.py:755
  51.2 0.5 collective-permute-start.6
  51.6 1.9 %collective-permute-start.7 = (bf16[216,128]{1,0:T(8,128)(2,1)S(1)}, bf16[216,128]{1,0:T(8,128)(2,1)S(1)}, u32[]{:S(2)}, u32[]{:S(2)}) collective-permute-start(bf16[216,128]{1,0:T(8,128)(2,1)S(1)} %pad_maximum_fusion), channel_id=1, source_target_pairs={{0,4},{1,5},{2,6},{3,7},{4,0},{5,1},{6,2},{7,3},{8,12},{9,13},{10,... | collective-permute-start | bytes 165896 | tf_op jit(solution)/shard_map/ppermute | solution.py:755
  53.5 1.5 %collective-permute-done.5 = bf16[216,128]{1,0:T(8,128)(2,1)S(1)} collective-permute-done((bf16[216,128]{1,0:T(8,128)(2,1)S(1)}, bf16[216,128]{1,0:T(8,128)(2,1)S(1)}, u32[]{:S(2)}, u32[]{:S(2)}) %collective-permute-start.5) | collective-permute-done | bytes 55328 | tf_op jit(solution)/shard_map/ppermute | solution.py:755
  55.1 1.3 %collective-permute-done.6 = bf16[216,128]{1,0:T(8,128)(2,1)S(1)} collective-permute-done((bf16[216,128]{1,0:T(8,128)(2,1)S(1)}, bf16[216,128]{1,0:T(8,128)(2,1)S(1)}, u32[]{:S(2)}, u32[]{:S(2)}) %collective-permute-start.6) | collective-permute-done | bytes 55328 | tf_op jit(solution)/shard_map/ppermute | solution.py:755
  56.4 0.0 collective-permute-done.7
  56.5 0.2 concatenate.15.refs_0_
  56.7 2.3 %collective-permute-start.10 = (bf16[480,128]{1,0:T(8,128)(2,1)S(1)}, bf16[480,128]{1,0:T(8,128)(2,1)S(1)}, u32[]{:S(2)}, u32[]{:S(2)}) collective-permute-start(bf16[480,128]{1,0:T(8,128)(2,1)S(1)} %concatenate.15.refs_0_), channel_id=1, source_target_pairs={{0,3},{1,2},{2,1},{3,0},{4,7},{5,6},{6,5},{7,4},{8,11},{9,10},{10,... | collective-permute-start | bytes 368648 | tf_op jit(solution)/shard_map/ppermute | solution.py:755
  59.0 0.6 collective-permute-start.8
  59.5 0.7 %collective-permute-start.9 = (bf16[480,128]{1,0:T(8,128)(2,1)S(1)}, bf16[480,128]{1,0:T(8,128)(2,1)S(1)}, u32[]{:S(2)}, u32[]{:S(2)}) collective-permute-start(bf16[480,128]{1,0:T(8,128)(2,1)S(1)} %concatenate.15.refs_0_), channel_id=1, source_target_pairs={{0,2},{1,3},{2,0},{3,1},{4,6},{5,7},{6,4},{7,5},{8,10},{9,11},{10,... | collective-permute-start | bytes 368648 | tf_op jit(solution)/shard_map/ppermute | solution.py:755
  60.2 2.3 %collective-permute-done.10.refs_3_ = bf16[480,128]{1,0:T(8,128)(2,1)S(1)} collective-permute-done((bf16[480,128]{1,0:T(8,128)(2,1)S(1)}, bf16[480,128]{1,0:T(8,128)(2,1)S(1)}, u32[]{:S(2)}, u32[]{:S(2)}) %collective-permute-start.10) | collective-permute-done | bytes 122912 | tf_op jit(solution)/shard_map/ppermute | solution.py:755
  62.5 1.3 %collective-permute-done.8.refs_1_ = bf16[480,128]{1,0:T(8,128)(2,1)S(1)} collective-permute-done((bf16[480,128]{1,0:T(8,128)(2,1)S(1)}, bf16[480,128]{1,0:T(8,128)(2,1)S(1)}, u32[]{:S(2)}, u32[]{:S(2)}) %collective-permute-start.8) | collective-permute-done | bytes 122912 | tf_op jit(solution)/shard_map/ppermute | solution.py:755
  63.8 0.6 collective-permute-done.9.refs_2_
  64.4 0.0 copy-done.3
  64.4 0.0 copy-done.5
  64.5 2.1 %shard_map.327 = (f32[1,1]{1,0:T(1,128)}, f32[1,1]{1,0:T(1,128)}, f32[1,512]{1,0:T(1,128)}, f32[1,64,512]{2,1,0:T(8,128)}, f32[27,1,128]{2,1,0:T(1,128)}, /*inde...) custom-call(bf16[480,128]{1,0:T(8,128)(2,1)S(1)} %concatenate.15.ref, ...), custom_call_target="tpu_custom_call" | custom-call | tf_op jit(solution)/shard_map/pallas_call | solution.py:778
  (27 shorter events, 0.2 us)
Async XLA Ops:
  0.7 1.9 %collective-permute-start = (s32[1,3,32,128]{3,2,1,0:T(8,128)}, s32[1,3,32,128]{3,2,1,0:T(8,128)S(1)}, u32[]{:S(2)}, u32[]{:S(2)}) collective-permute-start(s32[1,3,32,128]{3,2,1,0:T(8,128)} %codes.1), channel_id=1, source_target_pairs={{0,16},{16,0},{1,17},{17,1},{2,18},{18,2},{3,19},{19,3},{4,20},{20... | collective-permute-start | bytes 147464 | tf_op jit(solution)/shard_map/ppermute | solution.py:619
  2.6 5.0 %collective-permute-start.2 = (bf16[1744,128]{1,0:T(8,128)(2,1)S(1)}, bf16[1744,128]{1,0:T(8,128)(2,1)S(1)}, u32[]{:S(2)}, u32[]{:S(2)}) collective-permute-start(bf16[1744,128]{1,0:T(8,128)(2,1)S(1)} %get-tuple-element.74.mine), channel_id=1, source_target_pairs={{0,16},{16,0},{1,17},{17,1},{2,18},{18,2},{3,19},{19,3},{4,20},{20... | collective-permute-start | bytes 1339400 | tf_op jit(solution)/shard_map/ppermute | solution.py:647
  2.7 11.6 %collective-permute-start.1 = (bf16[48,128]{1,0:T(8,128)(2,1)S(1)}, bf16[48,128]{1,0:T(8,128)(2,1)S(1)}, u32[]{:S(2)}, u32[]{:S(2)}) collective-permute-start(bf16[48,128]{1,0:T(8,128)(2,1)S(1)} %get-tuple-element.73), channel_id=1, source_target_pairs={{0,1},{1,2},{3,4},{4,5},{5,6},{7,8},{8,9},{9,10},{11,12},{12,13},{... | collective-permute-start | bytes 36872 | tf_op jit(solution)/shard_map/ppermute | solution.py:646
  28.2 1.8 %collective-permute-start.3 = (bf16[1440,128]{1,0:T(8,128)(2,1)S(1)}, bf16[1440,128]{1,0:T(8,128)(2,1)S(1)}, u32[]{:S(2)}, u32[]{:S(2)}) collective-permute-start(bf16[1440,128]{1,0:T(8,128)(2,1)S(1)} %get-tuple-element.84), channel_id=1, source_target_pairs={{0,16},{16,0},{1,17},{17,1},{2,18},{18,2},{3,19},{19,3},{4,20},{20... | collective-permute-start | bytes 1105928 | tf_op jit(solution)/shard_map/ppermute | solution.py:710
  29.9 6.8 %copy-start.4 = (bf16[1440,128]{1,0:T(8,128)(2,1)}, bf16[1440,128]{1,0:T(8,128)(2,1)S(1)}, u32[]{:S(2)}) copy-start(bf16[1440,128]{1,0:T(8,128)(2,1)S(1)} %collective-permute-done.3.got._) | copy-start | bytes 1105924
  30.8 18.2 %all-to-all-start = ((bf16[16,88,128]{2,1,0:T(8,128)(2,1)}), bf16[16,88,128]{2,1,0:T(8,128)(2,1)S(1)}, u32[]{:S(2)}, u32[]{:S(2)}) async-start(bf16[16,88,128]{2,1,0:T(8,128)(2,1)} %bitcast.4), calls=%async_computation | async-start | bytes 720896 | tf_op jit(solution)/shard_map/all_to_all | solution.py:718
  45.9 1.3 %collective-permute-start.4 = (bf16[96,128]{1,0:T(8,128)(2,1)S(1)}, bf16[96,128]{1,0:T(8,128)(2,1)S(1)}, u32[]{:S(2)}, u32[]{:S(2)}) collective-permute-start(bf16[96,128]{1,0:T(8,128)(2,1)S(1)} %get-tuple-element.94), channel_id=1, source_target_pairs={{0,16},{16,0},{1,17},{17,1},{2,18},{18,2},{3,19},{19,3},{4,20},{20... | collective-permute-start | bytes 73736 | tf_op jit(solution)/shard_map/ppermute | solution.py:735
  47.1 17.3 %copy-start = (f32[1,1152,128]{2,1,0:T(8,128)S(1)}, f32[1,1152,128]{2,1,0:T(8,128)}, u32[]{:S(2)}) copy-start(f32[1,1152,128]{2,1,0:T(8,128)} %refs_12_.1) | copy-start | bytes 1769476
  47.1 17.2 %copy-start.1 = (f32[1,1152,128]{2,1,0:T(8,128)S(1)}, f32[1,1152,128]{2,1,0:T(8,128)}, u32[]{:S(2)}) copy-start(f32[1,1152,128]{2,1,0:T(8,128)} %refs_13_.1) | copy-start | bytes 1769476
  47.2 17.2 %copy-start.2 = (f32[1,1152,128]{2,1,0:T(8,128)S(1)}, f32[1,1152,128]{2,1,0:T(8,128)}, u32[]{:S(2)}) copy-start(f32[1,1152,128]{2,1,0:T(8,128)} %refs_14_.1) | copy-start | bytes 1769476
  47.2 17.2 %copy-start.3 = (f32[1,512,64]{1,2,0:T(8,128)S(1)}, f32[1,512,64]{1,2,0:T(8,128)}, u32[]{:S(2)}) copy-start(f32[1,512,64]{1,2,0:T(8,128)} %param.21) | copy-start | bytes 393220
  47.2 17.2 %copy-start.5 = (f32[1,128,64]{1,2,0:T(8,128)S(1)}, f32[1,128,64]{1,2,0:T(8,128)}, u32[]{:S(2)}) copy-start(f32[1,128,64]{1,2,0:T(8,128)} %param.25) | copy-start | bytes 98308
  47.2 17.2 %copy-start.6 = (f32[1,27,128]{2,0,1:T(1,128)S(1)}, f32[1,27,128]{2,0,1:T(1,128)}, u32[]{:S(2)}) copy-start(f32[1,27,128]{2,0,1:T(1,128)} %param.22) | copy-start | bytes 41476
  47.2 17.2 %copy-start.7 = (f32[1,128,64]{1,2,0:T(8,128)S(1)}, f32[1,128,64]{1,2,0:T(8,128)}, u32[]{:S(2)}) copy-start(f32[1,128,64]{1,2,0:T(8,128)} %param.26) | copy-start | bytes 98308
  47.2 17.2 %copy-start.8 = (f32[1,128,64]{1,2,0:T(8,128)S(1)}, f32[1,128,64]{1,2,0:T(8,128)}, u32[]{:S(2)}) copy-start(f32[1,128,64]{1,2,0:T(8,128)} %param.27) | copy-start | bytes 98308
  47.2 17.2 %copy-start.9 = (f32[1,27,128]{2,0,1:T(1,128)S(1)}, f32[1,27,128]{2,0,1:T(1,128)}, u32[]{:S(2)}) copy-start(f32[1,27,128]{2,0,1:T(1,128)} %param.23) | copy-start | bytes 41476
  47.2 17.2 %copy-start.10 = (f32[1,27,128]{2,0,1:T(1,128)S(1)}, f32[1,27,128]{2,0,1:T(1,128)}, u32[]{:S(2)}) copy-start(f32[1,27,128]{2,0,1:T(1,128)} %param.24) | copy-start | bytes 41476
  47.3 17.2 %copy-start.11 = (f32[1,512]{1,0:T(1,128)S(1)}, f32[1,512]{1,0:T(1,128)}, u32[]{:S(2)}) copy-start(f32[1,512]{1,0:T(1,128)} %refs_4_.1) | copy-start | bytes 6148
  47.3 17.2 %copy-start.12 = (f32[1,128,3]{1,0,2:T(1,128)S(1)}, f32[1,128,3]{1,0,2:T(1,128)}, u32[]{:S(2)}) copy-start(f32[1,128,3]{1,0,2:T(1,128)} %param.31) | copy-start | bytes 4612
  47.3 17.2 %copy-start.13 = (f32[1,128,3]{1,0,2:T(1,128)S(1)}, f32[1,128,3]{1,0,2:T(1,128)}, u32[]{:S(2)}) copy-start(f32[1,128,3]{1,0,2:T(1,128)} %param.32) | copy-start | bytes 4612
  47.3 17.2 %copy-start.14 = (f32[1,128,3]{1,0,2:T(1,128)S(1)}, f32[1,128,3]{1,0,2:T(1,128)}, u32[]{:S(2)}) copy-start(f32[1,128,3]{1,0,2:T(1,128)} %param.33) | copy-start | bytes 4612
  49.1 6.0 %collective-permute-start.5 = (bf16[216,128]{1,0:T(8,128)(2,1)S(1)}, bf16[216,128]{1,0:T(8,128)(2,1)S(1)}, u32[]{:S(2)}, u32[]{:S(2)}) collective-permute-start(bf16[216,128]{1,0:T(8,128)(2,1)S(1)} %pad_maximum_fusion), channel_id=1, source_target_pairs={{0,12},{1,13},{2,14},{3,15},{4,8},{5,9},{6,10},{7,11},{8,4},{9,5},... | collective-permute-start | bytes 165896 | tf_op jit(solution)/shard_map/ppermute | solution.py:755
  51.2 5.2 %collective-permute-start.6 = (bf16[216,128]{1,0:T(8,128)(2,1)S(1)}, bf16[216,128]{1,0:T(8,128)(2,1)S(1)}, u32[]{:S(2)}, u32[]{:S(2)}) collective-permute-start(bf16[216,128]{1,0:T(8,128)(2,1)S(1)} %pad_maximum_fusion), channel_id=1, source_target_pairs={{0,8},{1,9},{2,10},{3,11},{4,12},{5,13},{6,14},{7,15},{8,0},{9,1},... | collective-permute-start | bytes 165896 | tf_op jit(solution)/shard_map/ppermute | solution.py:755
  51.6 4.7 %collective-permute-start.7 = (bf16[216,128]{1,0:T(8,128)(2,1)S(1)}, bf16[216,128]{1,0:T(8,128)(2,1)S(1)}, u32[]{:S(2)}, u32[]{:S(2)}) collective-permute-start(bf16[216,128]{1,0:T(8,128)(2,1)S(1)} %pad_maximum_fusion), channel_id=1, source_target_pairs={{0,4},{1,5},{2,6},{3,7},{4,0},{5,1},{6,2},{7,3},{8,12},{9,13},{10,... | collective-permute-start | bytes 165896 | tf_op jit(solution)/shard_map/ppermute | solution.py:755
  56.7 5.8 %collective-permute-start.10 = (bf16[480,128]{1,0:T(8,128)(2,1)S(1)}, bf16[480,128]{1,0:T(8,128)(2,1)S(1)}, u32[]{:S(2)}, u32[]{:S(2)}) collective-permute-start(bf16[480,128]{1,0:T(8,128)(2,1)S(1)} %concatenate.15.refs_0_), channel_id=1, source_target_pairs={{0,3},{1,2},{2,1},{3,0},{4,7},{5,6},{6,5},{7,4},{8,11},{9,10},{10,... | collective-permute-start | bytes 368648 | tf_op jit(solution)/shard_map/ppermute | solution.py:755
  59.0 4.9 %collective-permute-start.8 = (bf16[480,128]{1,0:T(8,128)(2,1)S(1)}, bf16[480,128]{1,0:T(8,128)(2,1)S(1)}, u32[]{:S(2)}, u32[]{:S(2)}) collective-permute-start(bf16[480,128]{1,0:T(8,128)(2,1)S(1)} %concatenate.15.refs_0_), channel_id=1, source_target_pairs={{0,1},{1,0},{2,3},{3,2},{4,5},{5,4},{6,7},{7,6},{8,9},{9,8},{10,11... | collective-permute-start | bytes 368648 | tf_op jit(solution)/shard_map/ppermute | solution.py:755
  59.5 4.9 %collective-permute-start.9 = (bf16[480,128]{1,0:T(8,128)(2,1)S(1)}, bf16[480,128]{1,0:T(8,128)(2,1)S(1)}, u32[]{:S(2)}, u32[]{:S(2)}) collective-permute-start(bf16[480,128]{1,0:T(8,128)(2,1)S(1)} %concatenate.15.refs_0_), channel_id=1, source_target_pairs={{0,2},{1,3},{2,0},{3,1},{4,6},{5,7},{6,4},{7,5},{8,10},{9,11},{10,... | collective-permute-start | bytes 368648 | tf_op jit(solution)/shard_map/ppermute | solution.py:755
